TPU v7x, 128 devices: a whole 4x4x4 slice. The times are simulated.
128 devices in a mesh: dp: 32 (over x, y, core), chan: 4 (over z).
Axes of the slice: x: 4, y: 4, z: 4, core: 2. Of those that a mesh axis runs over, the one named last changes fastest.
Arguments:
- features: float32 [294912, 112], P(('dp', 'chan')), may hold values from -32 to 32
- seg_units: int32 [128, 3], P('dp'), may hold values from 1 to 3, 6 in all within a row
- w_expand: float32 [112, 672], P(None, 'chan'), may hold values from -0.5 to 0.5
- gain_one: float32 [672], P('chan'), may hold values from 0.5 to 1.5
- bias_one: float32 [672], P('chan'), may hold values from -0.5 to 0.5
- w_depth: float32 [5, 5, 672], P(None, None, 'chan'), may hold values from -1.25 to 1.25
- gain_two: float32 [672], P('chan'), may hold values from 0.5 to 1.5
- bias_two: float32 [672], P('chan'), may hold values from -0.5 to 0.5
- w_reduce: float32 [672, 28], P('chan'), may hold values from -0.25 to 0.25
- b_reduce: float32 [28], replicated, may hold values from -4 to 4
- w_excite: float32 [28, 672], P(None, 'chan'), may hold values from -1 to 1
- b_excite: float32 [672], P('chan'), may hold values from -4 to 4
- w_project: float32 [672, 112], P('chan'), may hold values from -0.25 to 0.25
- gain_three: float32 [112], replicated, may hold values from 0.5 to 1.5
- bias_three: float32 [112], replicated, may hold values from -0.5 to 0.5
- cotangent: float32 [294912, 112], P(('dp', 'chan')), may hold values from -6 to 6
Outputs:
- output: float32 [294912, 112], P(('dp', 'chan'))
- input_grad: float32 [294912, 112], P(('dp', 'chan'))
- grad_expand: float32 [112, 672], P(None, 'chan')
- grad_gain_one: float32 [672], P('chan')
- grad_bias_one: float32 [672], P('chan')
- grad_depth: float32 [5, 5, 672], P(None, None, 'chan')
- grad_gain_two: float32 [672], P('chan')
- grad_bias_two: float32 [672], P('chan')
- grad_reduce: float32 [672, 28], P('chan')
- grad_reduce_bias: float32 [28], replicated
- grad_excite: float32 [28, 672], P(None, 'chan')
- grad_excite_bias: float32 [672], P('chan')
- grad_project: float32 [672, 112], P('chan')
- grad_gain_three: float32 [112], replicated
- grad_bias_three: float32 [112], replicated
Inputs may be any that keep to these rules, and one draw needn't show every extreme that they name: `seg_units`: in each slot the 3 lengths sum to 6 and the largest is exactly 3.
All inputs are finite; a program needn't handle non-finite values.
Results may differ from a plain program's by a relative error of at most 0.0003.
Values sent between devices are 32-bit elements; how exact they have to be, the bound alone decides.
A program may use at most 576 MiB of HBM per device.

v0:
```python
import jax
import jax.numpy as jnp
from jax import lax
from jax.sharding import PartitionSpec as P

H = 6
W = 4
FRAMES = 96
BLOCK = 16


EPSILON = 0.001
PRECISE = lax.Precision.HIGHEST


def segment_table(seg_units, frames):
    slot_count = seg_units.shape[0]
    widths = seg_units * BLOCK
    upper_end = (
        jnp.cumsum(widths, axis=1) + (jnp.arange(slot_count, dtype=jnp.int32) * FRAMES)[:, None]
    )
    upper_end = upper_end.reshape(-1)
    lower_end = upper_end - widths.reshape(-1)
    frame_index = jnp.arange(frames, dtype=jnp.int32)
    inside = (frame_index[:, None] >= lower_end[None, :]) & (
        frame_index[:, None] < upper_end[None, :]
    )
    counts = (widths * (H * W)).reshape(-1).astype(jnp.float32)
    return (inside.astype(jnp.float32), counts)


def depthwise(frames_in, kernel):
    radius_cells = kernel.shape[0] // 2
    padded = jnp.pad(
        frames_in, ((0, 0), (radius_cells, radius_cells), (radius_cells, radius_cells), (0, 0))
    )
    tall_cells = frames_in.shape[1]
    wide_cells = frames_in.shape[2]
    result = jnp.zeros(frames_in.shape, jnp.float32)
    for shift_down in range(kernel.shape[0]):
        for shift_right in range(kernel.shape[1]):
            window = padded[
                :, shift_down : shift_down + tall_cells, shift_right : shift_right + wide_cells, :
            ]
            result = result + window * kernel[shift_down, shift_right]
    return result


def silu_slope(values):
    sigmoid_value = jax.nn.sigmoid(values)
    return sigmoid_value * (1.0 + values * (1.0 - sigmoid_value))


def moments(values):
    return (jnp.sum(values, axis=0), jnp.sum(values * values, axis=0))


def slopes(upstream, centred):
    return (jnp.sum(upstream, axis=0), jnp.sum(upstream * centred, axis=0))


def normalize(values, gain, bias, sums, row_total):
    mean_value = sums[0] / row_total
    spread = sums[1] / row_total - mean_value * mean_value
    inv_std = lax.rsqrt(spread + EPSILON)
    centred = (values - mean_value) * inv_std
    return (centred, inv_std, centred * gain + bias)


def normalize_back(upstream, centred, inv_std, gain, sums, row_total):
    return gain * inv_std * (upstream - sums[0] / row_total - centred * (sums[1] / row_total))


def rows_gather(values):
    return lax.all_gather(values, "chan", axis=0, tiled=True)


def norm_sums(values):
    sum_plain, sum_square = moments(values)
    return lax.psum((sum_plain, sum_square), "dp")


def norm_grads(upstream, centred):
    sum_plain, sum_product = slopes(upstream, centred)
    return lax.psum((sum_plain, sum_product), "dp")


def squeeze(activated, seg_table, counts, w_reduce, b_reduce, w_excite, b_excite):
    frames = seg_table.shape[0]
    channels = activated.shape[1]
    framed = activated.reshape(frames, -1, channels)
    pooled = (
        jnp.einsum("fs,fe->se", seg_table, jnp.sum(framed, axis=1), precision=PRECISE)
        / counts[:, None]
    )
    reduced = lax.psum(jnp.dot(pooled, w_reduce, precision=PRECISE), "chan") + b_reduce
    squeezed = jax.nn.silu(reduced)
    gate_values = jax.nn.sigmoid(jnp.dot(squeezed, w_excite, precision=PRECISE) + b_excite)
    row_gate = jnp.dot(seg_table, gate_values, precision=PRECISE)
    scaled = (framed * row_gate[:, None, :]).reshape(activated.shape)
    return (pooled, reduced, squeezed, gate_values, row_gate, scaled)


def squeeze_back(
    upstream,
    activated,
    seg_table,
    counts,
    pooled,
    reduced,
    squeezed,
    gate_values,
    row_gate,
    w_reduce,
    w_excite,
):
    frames = seg_table.shape[0]
    channels = activated.shape[1]
    framed_up = upstream.reshape(frames, -1, channels)
    framed_act = activated.reshape(frames, -1, channels)
    gate_grad = jnp.einsum(
        "fs,fe->se", seg_table, jnp.sum(framed_up * framed_act, axis=1), precision=PRECISE
    )
    excite_in = gate_grad * gate_values * (1.0 - gate_values)
    excite_bias = jnp.sum(excite_in, axis=0)
    excite_weight = jnp.einsum("sq,se->qe", squeezed, excite_in, precision=PRECISE)
    squeezed_grad = lax.psum(
        jnp.einsum("se,qe->sq", excite_in, w_excite, precision=PRECISE), "chan"
    )
    reduced_grad = squeezed_grad * silu_slope(reduced)
    reduce_bias = jnp.sum(reduced_grad, axis=0)
    reduce_weight = jnp.einsum("se,sq->eq", pooled, reduced_grad, precision=PRECISE)
    pooled_grad = (
        jnp.einsum("sq,eq->se", reduced_grad, w_reduce, precision=PRECISE) / counts[:, None]
    )
    spread_back = jnp.dot(seg_table, pooled_grad, precision=PRECISE)
    active_grad = framed_up * row_gate[:, None, :] + spread_back[:, None, :]
    return (
        active_grad.reshape(activated.shape),
        reduce_weight,
        reduce_bias,
        excite_weight,
        excite_bias,
    )


def body(
    features,
    seg_units,
    w_expand,
    gain_one,
    bias_one,
    w_depth,
    gain_two,
    bias_two,
    w_reduce,
    b_reduce,
    w_excite,
    b_excite,
    w_project,
    gain_three,
    bias_three,
    cotangent,
):
    quarter = features.shape[0]
    row_total = float(quarter * lax.axis_size("chan") * lax.axis_size("dp"))
    gathered = rows_gather(features)
    frames = gathered.shape[0] // (H * W)
    seg_table, counts = segment_table(seg_units, frames)
    expanded = jnp.dot(gathered, w_expand, precision=PRECISE)
    centred_one, scale_one, normed_one = normalize(
        expanded, gain_one, bias_one, norm_sums(expanded), row_total
    )
    active_one = jax.nn.silu(normed_one)
    framed_one = active_one.reshape(frames, H, W, -1)
    depth_out = depthwise(framed_one, w_depth).reshape(expanded.shape)
    centred_two, scale_two, normed_two = normalize(
        depth_out, gain_two, bias_two, norm_sums(depth_out), row_total
    )
    active_two = jax.nn.silu(normed_two)
    pooled, reduced, squeezed, gate_values, row_gate, scaled = squeeze(
        active_two, seg_table, counts, w_reduce, b_reduce, w_excite, b_excite
    )
    projected = lax.psum_scatter(
        jnp.dot(scaled, w_project, precision=PRECISE), "chan", scatter_dimension=0, tiled=True
    )
    proj_plain, proj_square = moments(projected)
    sums_out = lax.psum((proj_plain, proj_square), ("dp", "chan"))
    centred_three, scale_three, normed_three = normalize(
        projected, gain_three, bias_three, sums_out, row_total
    )
    output = features + normed_three
    cot_plain, cot_product = slopes(cotangent, centred_three)
    sums_three = lax.psum((cot_plain, cot_product), ("dp", "chan"))
    project_grad = rows_gather(
        normalize_back(cotangent, centred_three, scale_three, gain_three, sums_three, row_total)
    )
    grad_project = jnp.einsum("re,rd->ed", scaled, project_grad, precision=PRECISE)
    scaled_grad = jnp.einsum("rd,ed->re", project_grad, w_project, precision=PRECISE)
    active_grad, grad_reduce, grad_reduce_bias, grad_excite, grad_excite_bias = squeeze_back(
        scaled_grad,
        active_two,
        seg_table,
        counts,
        pooled,
        reduced,
        squeezed,
        gate_values,
        row_gate,
        w_reduce,
        w_excite,
    )
    upstream_two = active_grad * silu_slope(normed_two)
    sums_two = norm_grads(upstream_two, centred_two)
    depth_grad = normalize_back(upstream_two, centred_two, scale_two, gain_two, sums_two, row_total)
    framed_grad, grad_depth = jax.vjp(depthwise, framed_one, w_depth)[1](
        depth_grad.reshape(framed_one.shape)
    )
    upstream_one = framed_grad.reshape(expanded.shape) * silu_slope(normed_one)
    sums_one = norm_grads(upstream_one, centred_one)
    expand_grad = normalize_back(
        upstream_one, centred_one, scale_one, gain_one, sums_one, row_total
    )
    grad_expand = jnp.einsum("rd,re->de", gathered, expand_grad, precision=PRECISE)
    input_grad = (
        lax.psum_scatter(
            jnp.einsum("re,de->rd", expand_grad, w_expand, precision=PRECISE),
            "chan",
            scatter_dimension=0,
            tiled=True,
        )
        + cotangent
    )
    summed = lax.psum(
        (
            grad_expand,
            grad_depth,
            grad_reduce,
            grad_reduce_bias,
            grad_excite,
            grad_excite_bias,
            grad_project,
        ),
        "dp",
    )
    return (
        output,
        input_grad,
        summed[0],
        sums_one[1],
        sums_one[0],
        summed[1],
        sums_two[1],
        sums_two[0],
        summed[2],
        summed[3],
        summed[4],
        summed[5],
        summed[6],
        sums_three[1],
        sums_three[0],
    )


def solution(mesh):
    placed = (
        P(("dp", "chan"), None),
        P("dp", None),
        P(None, "chan"),
        P("chan"),
        P("chan"),
        P(None, None, "chan"),
        P("chan"),
        P("chan"),
        P("chan", None),
        P(),
        P(None, "chan"),
        P("chan"),
        P("chan", None),
        P(),
        P(),
        P(("dp", "chan"), None),
    )
    return jax.shard_map(
        body,
        mesh=mesh,
        in_specs=placed,
        out_specs=(
            P(("dp", "chan"), None),
            P(("dp", "chan"), None),
            P(None, "chan"),
            P("chan"),
            P("chan"),
            P(None, None, "chan"),
            P("chan"),
            P("chan"),
            P("chan", None),
            P(),
            P(None, "chan"),
            P("chan"),
            P("chan", None),
            P(),
            P(),
        ),
        check_vma=False,
    )
```

profile of v0, /device:TPU:1, one launch (start us, length us, event | category | flops | bytes accessed | tf_op | source)
XLA Modules:
  0.0 1387.7 jit_solution(622191817344359247)
XLA Ops:
  7.2 0.7 all-gather.3.cloned.1.call-update
  8.0 0.7 multiply_convert_fusion
  9.2 0.9 fusion.35
  10.0 1.0 fusion.34
  11.1 49.8 %all-gather.3.cloned.1.call-done = f32[9216,112]{0,1:T(8,128)} async-done(((f32[2304,112]{0,1:T(8,128)}), f32[9216,112]{0,1:T(8,128)}) %all-gather.3.cloned.1.call-update) | async-done | bytes 4128784 | tf_op jit(solution)/shard_map/all_gather | solution.py:75
  60.8 10.3 fusion.29
  71.1 62.9 %all-reduce.56 = (f32[168]{0:T(256)S(1)}, f32[168]{0:T(256)S(1)}) all-reduce(f32[168]{0:T(256)S(1)} %get-tuple-element.46, f32[168]{0:T(256)S(1)} %get-tuple-element.45), channel_id=1, replica_groups=mesh['dp'=32,'chan'=4] {'dp'}, use_global_device_ids=true, to_apply=%region_3.4 | all-reduce | flops 336 | bytes 2688 | tf_op jit(solution)/shard_map/psum | solution.py:80
  134.0 0.6 fusion.20
  134.6 5.9 fusion.4
  140.6 8.5 copy.55
  149.1 11.8 reshape.282
  160.9 102.0 %fusion.26 = (f32[168]{0:T(256)S(1)}, f32[168]{0:T(256)S(1)}, f32[384,6,4,168]{3,2,1,0:T(4,128)}) fusion(f32[168]{0:T(256)S(1)} %bitcast.118, f32[168]{0:T(256)S(1)} %bitcast.120, f32[168]{0:T(256)S(1)} %bitcast.122, f32[168]{0:T(256)S(1)} %bitcast.124, f32[168]{0:T(256)S(1)} %bitcast.126, f32[168]{0:T(256)S(1)} %bitcast.128, f32[168]{0:T(256)S(1)} %bitcast.130, ...), kind=kLoop, calls=%fused_computation.151 | loop fusion | flops 80510640 | bytes 12404448 | tf_op jit(solution)/shard_map/reduce_sum | solution.py:55
  263.0 12.0 reshape.283
  274.9 67.5 %all-reduce.55 = (f32[168]{0:T(256)S(1)}, f32[168]{0:T(256)S(1)}) all-reduce(f32[168]{0:T(256)S(1)} %get-tuple-element.40, f32[168]{0:T(256)S(1)} %get-tuple-element.39), channel_id=1, replica_groups=mesh['dp'=32,'chan'=4] {'dp'}, use_global_device_ids=true, to_apply=%region_7.8 | all-reduce | flops 336 | bytes 2688 | tf_op jit(solution)/shard_map/psum | solution.py:80
  342.5 9.3 fusion
  352.2 6.7 psum.151
  359.5 8.6 copy.56
  368.1 4.3 mul.817
  372.5 8.6 copy.58
  381.0 5.9 multiply_multiply_fusion.2
  386.9 2.7 copy-done.1
  389.6 5.8 fusion.38
  395.5 43.0 %reduce-scatter.3.cloned.1.call-done = f32[2304,112]{0,1:T(8,128)} async-done(((f32[9216,112]{0,1:T(8,128)}), f32[2304,112]{0,1:T(8,128)}) %reduce-scatter.3.cloned.1.call-update) | async-done | bytes 1032208 | tf_op jit(solution)/shard_map/reduce_scatter | solution.py:184
  438.5 1.4 fusion.31
  439.9 64.5 %all-reduce.52 = (f32[112]{0:T(128)S(1)}, f32[112]{0:T(128)S(1)}) all-reduce(f32[112]{0:T(128)S(1)} %get-tuple-element.50, f32[112]{0:T(128)S(1)} %get-tuple-element.49), channel_id=1, replica_groups=mesh['dp'=32,'chan'=4] {'dp','chan'}, use_global_device_ids=true, to_apply=%region_15.16 | all-reduce | flops 224 | bytes 1792 | tf_op jit(solution)/shard_map/psum | solution.py:188
  504.5 1.6 fusion.30
  506.1 64.1 %all-reduce.51 = (f32[112]{0:T(128)S(1)}, f32[112]{0:T(128)S(1)}) all-reduce(f32[112]{0:T(128)S(1)} %get-tuple-element.48, f32[112]{0:T(128)S(1)} %get-tuple-element.47), channel_id=1, replica_groups=mesh['dp'=32,'chan'=4] {'dp','chan'}, use_global_device_ids=true, to_apply=%region_19.20 | all-reduce | flops 224 | bytes 1792 | tf_op jit(solution)/shard_map/psum | solution.py:194
  570.2 3.0 subtract_multiply_fusion.4
  573.4 11.2 copy.61
  584.6 33.0 %all-gather.5.cloned.1.call-done = f32[9216,112]{0,1:T(8,128)} async-done(((f32[2304,112]{0,1:T(8,128)}), f32[9216,112]{0,1:T(8,128)}) %all-gather.5.cloned.1.call-update) | async-done | bytes 4128784 | tf_op jit(solution)/shard_map/all_gather | solution.py:75
  617.6 9.8 fusion.39
  627.4 8.5 copy.60
  636.0 8.5 copy.62
  644.5 5.8 multiply_reduce_fusion.28
  650.3 0.9 fusion.36
  651.3 0.9 fusion.21
  652.2 6.6 psum.156
  659.5 0.8 fusion.42
  660.7 4.3 add.405
  664.9 8.6 copy.64
  673.5 12.8 fusion.28
  686.3 65.0 %all-reduce.54 = (f32[168]{0:T(256)S(1)}, f32[168]{0:T(256)S(1)}) all-reduce(f32[168]{0:T(256)S(1)} %get-tuple-element.44, f32[168]{0:T(256)S(1)} %get-tuple-element.43), channel_id=1, replica_groups=mesh['dp'=32,'chan'=4] {'dp'}, use_global_device_ids=true, to_apply=%region_25.26 | all-reduce | flops 336 | bytes 2688 | tf_op jit(solution)/shard_map/psum | solution.py:85
  751.3 10.4 multiply_reduce_fusion.25
  761.8 8.5 copy.65
  770.3 11.8 reshape.287
  782.1 82.7 %multiply_reduce_fusion.23 = (f32[168]{0:T(256)}, f32[168]{0:T(256)}, f32[168]{0:T(256)}, f32[168]{0:T(256)}, f32[168]{0:T(256)}, /*index=5*/f32[168]{0:T(256)},...) fusion(f32[384,6,4,168]{3,2,1,0:T(4,128)} %reshape.287, ...), kind=kLoop, calls=%fused_computation.55 | loop fusion | flops 55735344 | bytes 12398400 | tf_op jit(solution)/shard_map/transpose(jvp())/reduce_sum | solution.py:45
  864.9 54.7 %multiply_reduce_fusion.22 = (f32[168]{0:T(256)S(1)}, f32[168]{0:T(256)S(1)}, f32[168]{0:T(256)S(1)}, f32[168]{0:T(256)S(1)}, f32[168]{0:T(256)S(1)}, /*index=5*...) fusion(f32[384,6,4,168]{3,2,1,0:T(4,128)} %reshape.287, ...), kind=kLoop, calls=%fused_computation.54 | loop fusion | flops 37157904 | bytes 86716224 | tf_op jit(solution)/shard_map/transpose(jvp())/reduce_sum | solution.py:45
  919.6 45.7 %broadcast_multiply_fusion = (f32[384,6,4,168]{3,2,1,0:T(4,128)}, f32[384,6,4,168]{3,2,1,0:T(4,128)}, f32[384,6,4,168]{3,2,1,0:T(4,128)}, f32[384,6,4,168]{3,2,1...) fusion(f32[384,6,4,168]{3,2,1,0:T(4,128)} %reshape.287, ...), kind=kLoop, calls=%fused_computation.80 | loop fusion | flops 20127744 | bytes 86712864 | tf_op jit(solution)/shard_map/transpose(jvp())/mul | solution.py:45
  965.3 73.0 %pad_add_fusion = f32[384,10,8,168]{3,2,1,0:T(8,128)} fusion(f32[384,6,4,168]{3,2,1,0:T(4,128)} %get-tuple-element.85, f32[384,6,4,168]{3,2,1,0:T(4,128)} %get-tuple-element.86, f32[384,6,4,168]{3,2,1,0:T(4,128)} %get-tuple-element.87, f32[384,6,4,168]{3,2,1,0:T(4,128)} %get-tuple-element.88, f32[384,6,4,168]{3,2,1,0:T(4,128)} %get-tuple-element.89, ...), kind=kLoop, calls=%fused_computation.24 | loop fusion | flops 92897280 | bytes 138313728 | tf_op jit(solution)/shard_map/transpose(jvp())/add_any | solution.py:42
  1038.3 24.5 %pad_add_fusion.1 = f32[384,6,4,168]{3,2,1,0:T(4,128)} fusion(f32[384,6,4,168]{3,2,1,0:T(4,128)} %get-tuple-element.79, f32[384,6,4,168]{3,2,1,0:T(4,128)} %get-tuple-element.80, f32[384,6,4,168]{3,2,1,0:T(4,128)} %get-tuple-element.81, f32[384,6,4,168]{3,2,1,0:T(4,128)} %get-tuple-element.82, f32[384,6,4,168]{3,2,1,0:T(4,128)} %get-tuple-element.83, ...), kind=kLoop, calls=%fused_computation.26 | loop fusion | flops 9289728 | bytes 49545216 | tf_op jit(solution)/shard_map/transpose(jvp())/add_any | solution.py:42
  1062.8 12.0 reshape.288
  1074.8 8.8 copy.66
  1083.9 7.8 fusion.27
  1092.0 121.9 %all-reduce.53 = (f32[168]{0:T(256)S(1)}, f32[168]{0:T(256)S(1)}, f32[5,5,168]{2,1,0:T(8,128)}, f32[168,28]{0,1:T(8,128)}, f32[28]{0:T(128)}, /*index=5*/f32[28,168]{1,0:T(8,128)}, f32[168]{0:T(256)}) all-reduce(f32[168]{0:T(256)S(1)} %get-tuple-element.42, f32[168]{0:T(256)S(1)} %get-tuple-element.41, ...), channel_id=1, replica_groups=mesh['dp'=32,'chan'=4] {'dp'}, use_global_device_ids=true, to_apply=%region_29.30 | all-reduce | flops 14140 | bytes 113120 | tf_op jit(solution)/shard_map/psum | solution.py:85
  1214.0 6.6 subtract_multiply_fusion
  1220.6 2.6 copy-done.2
  1223.2 5.8 fusion.41
  1229.3 9.7 fusion.43
  1239.0 5.6 convolution_bitcast_fusion
  1244.7 30.4 %reduce-scatter.5.cloned.1.call-done = f32[2304,112]{0,1:T(8,128)} async-done(((f32[9216,112]{0,1:T(8,128)}), f32[2304,112]{0,1:T(8,128)}) %reduce-scatter.5.cloned.1.call-update) | async-done | bytes 1032208 | tf_op jit(solution)/shard_map/reduce_scatter | solution.py:226
  1275.1 2.4 add.410
  1277.4 100.5 %all-reduce.60.cloned.1.call-done = (f32[112,168]{0,1:T(8,128)}, f32[168,112]{1,0:T(8,128)}) async-done(((f32[112,168]{0,1:T(8,128)}, f32[168,112]{1,0:T(8,128)}), (f32[112,168]{0,1:T(8,128)}, f32[168,112]{1,0:T(8,128)})) %all-reduce.60.cloned.1.call-update) | async-done | bytes 150544 | tf_op jit(solution)/shard_map/psum | solution.py:234
  1377.9 1.5 copy.71
  1379.4 1.5 copy.72
  (140 shorter events, 3.5 us)
Async XLA Ops:
  7.2 53.7 %copy-start = (f32[112,168]{0,1:T(8,128)S(1)}, f32[112,168]{0,1:T(8,128)}, u32[]{:S(2)}) copy-start(f32[112,168]{0,1:T(8,128)} %param.18) | copy-start | bytes 225796
  7.2 53.6 %all-gather.3.cloned.1.call-start = ((), (), s32[]{:S(2)}) async-start(), calls=%async_computation.2 | async-start | bytes 5160960 | tf_op jit(solution)/shard_map/all_gather | solution.py:75
  7.9 430.5 %reduce-scatter.3.cloned.1.call-start = ((), (), s32[]{:S(2)}) async-start(), calls=%async_computation.3 | async-start | bytes 5160960 | tf_op jit(solution)/shard_map/reduce_scatter | solution.py:184
  11.0 123.0 %copy-start.19 = (f32[168]{0:T(256)S(1)}, f32[168]{0:T(256)}, u32[]{:S(2)}) copy-start(f32[168]{0:T(256)} %param.19) | copy-start | bytes 2020
  11.1 123.6 %copy-start.21 = (f32[168]{0:T(256)S(1)}, f32[168]{0:T(256)}, u32[]{:S(2)}) copy-start(f32[168]{0:T(256)} %param.20) | copy-start | bytes 2020
  134.6 616.7 %copy-start.14 = (f32[168]{0:T(256)}, f32[168]{0:T(256)S(1)}, u32[]{:S(2)}) copy-start(f32[168]{0:T(256)S(1)} %get-tuple-element.132) | copy-start | bytes 2020
  134.6 616.7 %copy-start.16 = (f32[168]{0:T(256)}, f32[168]{0:T(256)S(1)}, u32[]{:S(2)}) copy-start(f32[168]{0:T(256)S(1)} %get-tuple-element.137) | copy-start | bytes 2020
  262.9 79.5 %copy-start.13 = (f32[168]{0:T(256)S(1)}, f32[168]{0:T(256)}, u32[]{:S(2)}) copy-start(f32[168]{0:T(256)} %param.22) | copy-start | bytes 2020
  262.9 79.5 %copy-start.18 = (f32[168]{0:T(256)S(1)}, f32[168]{0:T(256)}, u32[]{:S(2)}) copy-start(f32[168]{0:T(256)} %param.23) | copy-start | bytes 2020
  274.9 77.2 %copy-start.12 = (f32[168,28]{0,1:T(8,128)S(1)}, f32[168,28]{0,1:T(8,128)}, u32[]{:S(2)}) copy-start(f32[168,28]{0,1:T(8,128)} %param.24) | copy-start | bytes 56452
  274.9 84.1 %copy-start.11 = (f32[28,168]{1,0:T(8,128)S(1)}, f32[28,168]{1,0:T(8,128)}, u32[]{:S(2)}) copy-start(f32[28,168]{1,0:T(8,128)} %param.26) | copy-start | bytes 56452
  274.9 84.1 %copy-start.45 = (f32[28]{0:T(128)S(1)}, f32[28]{0:T(128)}, u32[]{:S(2)}) copy-start(f32[28]{0:T(128)} %param.25) | copy-start | bytes 340
  274.9 84.1 %copy-start.54 = (f32[168]{0:T(256)S(1)}, f32[168]{0:T(256)}, u32[]{:S(2)}) copy-start(f32[168]{0:T(256)} %param.27) | copy-start | bytes 2020
  381.0 8.6 copy-start.8
  386.9 2.7 copy-start.1
  389.6 114.8 %copy-start.46 = (f32[112]{0:T(128)S(1)}, f32[112]{0:T(128)}, u32[]{:S(2)}) copy-start(f32[112]{0:T(128)} %param.29) | copy-start | bytes 1348
  389.6 114.8 %copy-start.5 = (f32[2304,112]{0,1:T(8,128)S(1)}, f32[2304,112]{0,1:T(8,128)}, u32[]{:S(2)}) copy-start(f32[2304,112]{0,1:T(8,128)} %param.31) | copy-start | bytes 3096580
  389.6 180.6 %copy-start.7 = (f32[2304,112]{0,1:T(8,128)S(1)}, f32[2304,112]{0,1:T(8,128)}, u32[]{:S(2)}) copy-start(f32[2304,112]{0,1:T(8,128)} %param.16) | copy-start | bytes 3096580
  389.6 180.6 %copy-start.51 = (f32[112]{0:T(128)S(1)}, f32[112]{0:T(128)}, u32[]{:S(2)}) copy-start(f32[112]{0:T(128)} %param.30) | copy-start | bytes 1348
  395.4 222.2 %all-gather.5.cloned.1.call-start = ((), (), s32[]{:S(2)}) async-start(), calls=%async_computation.4 | async-start | bytes 5160960 | tf_op jit(solution)/shard_map/all_gather | solution.py:75
  570.1 14.4 %copy-start.52 = (f32[112]{0:T(128)}, f32[112]{0:T(128)S(1)}, u32[]{:S(2)}) copy-start(f32[112]{0:T(128)S(1)} %get-tuple-element.158) | copy-start | bytes 1348
  570.1 14.4 %copy-start.53 = (f32[112]{0:T(128)}, f32[112]{0:T(128)S(1)}, u32[]{:S(2)}) copy-start(f32[112]{0:T(128)S(1)} %get-tuple-element.159) | copy-start | bytes 1348
  573.2 701.9 %reduce-scatter.5.cloned.1.call-start = ((), (), s32[]{:S(2)}) async-start(), calls=%async_computation.5 | async-start | bytes 5160960 | tf_op jit(solution)/shard_map/reduce_scatter | solution.py:226
  751.3 10.5 copy-start.47
  751.3 10.5 copy-start.48
  1074.8 8.8 copy-start.15
  1074.8 8.8 copy-start.17
  1074.8 8.8 copy-start.20
  1074.8 8.8 copy-start.22
  1083.6 8.1 copy-start.24
  1083.7 8.1 copy-start.25
  1083.7 8.1 copy-start.26
  1083.7 8.1 copy-start.27
  1083.7 8.1 copy-start.28
  1083.7 8.1 copy-start.29
  1083.7 8.1 copy-start.30
  1083.7 8.1 copy-start.31
  1083.7 8.1 copy-start.32
  1083.7 8.1 copy-start.33
  1083.8 8.1 copy-start.34
  1083.8 8.1 copy-start.35
  1083.8 8.1 copy-start.36
  1083.8 8.1 copy-start.37
  1083.8 8.1 copy-start.38
  1083.8 8.1 copy-start.39
  1083.8 8.1 copy-start.40
  1083.8 8.1 copy-start.41
  1083.8 8.1 copy-start.42
  1083.8 8.1 copy-start.9
  1083.9 8.1 copy-start.10
  1083.9 8.1 copy-start.23
  1083.9 8.1 copy-start.44
  1083.9 130.1 %copy-start.43 = (f32[168]{0:T(256)S(1)}, f32[168]{0:T(256)}, u32[]{:S(2)}) copy-start(f32[168]{0:T(256)} %get-tuple-element.131) | copy-start | bytes 2020
  1214.0 15.1 %copy-start.49 = (f32[168]{0:T(256)}, f32[168]{0:T(256)S(1)}, u32[]{:S(2)}) copy-start(f32[168]{0:T(256)S(1)} %get-tuple-element.148) | copy-start | bytes 2020
  1214.0 15.1 %copy-start.50 = (f32[168]{0:T(256)}, f32[168]{0:T(256)S(1)}, u32[]{:S(2)}) copy-start(f32[168]{0:T(256)S(1)} %get-tuple-element.149) | copy-start | bytes 2020
  1220.6 2.6 copy-start.2
  1229.0 148.8 %all-reduce.60.cloned.1.call-start = ((), (), s32[]{:S(2)}) async-start(), calls=%async_computation.6 | async-start | bytes 344064 | tf_op jit(solution)/shard_map/psum | solution.py:234
  1229.3 9.7 copy-start.3
  1229.3 9.7 copy-start.4
  1229.3 45.7 %copy-start.6 = (f32[2304,112]{0,1:T(8,128)S(1)}, f32[2304,112]{0,1:T(8,128)}, u32[]{:S(2)}) copy-start(f32[2304,112]{0,1:T(8,128)} %param.31) | copy-start | bytes 3096580
Sparse Core Ops, SparseCore 0:
  9.7 51.1 all-gather.2
  395.5 42.8 reduce-scatter.2
  573.3 44.2 all-gather.4
  1229.2 45.8 reduce-scatter.4
  1279.4 98.4 all-reduce.59
where the time goes:
time: 1400 us; the launch traced here: 1390 us
  blocking collectives  459 us (33%)
  other arithmetic  458 us (33%)
  waiting for transfers between devices  257 us (18%)
  local copies, waits for them, and re-layouts  147 us (10%)
  matrix products  51.1 us (4%)
  between operations  14.7 us (1%)
    psum x2, blocking collectives, norm_grads(): return lax.psum((sum_plain, sum_product), 'dp')  187 us
    reduce_sum x3, other arithmetic, depthwise(): result = result + window * kernel[shift_down, shift_right]  148 us
    psum x2, blocking collectives, norm_sums(): return lax.psum((sum_plain, sum_square), 'dp')  130 us
    reduce_sum x2, other arithmetic, moments(): return (jnp.sum(values, axis=0), jnp.sum(values * values, axis=0))  103 us
    psum x1, waiting for transfers between devices, body(): lax.psum((grad_expand, grad_depth, grad_reduce, grad_reduce_bias, grad_ex...  100 us
    add_any x2, other arithmetic, depthwise(): padded[:, shift_down:shift_down + tall_cells, shift_right:shift_right + w...  97.5 us
    all_gather x2, waiting for transfers between devices, rows_gather(): return lax.all_gather(values, 'chan', axis=0, tiled=True)  82.8 us
    psum x1, blocking collectives, body(): sums_out = lax.psum((proj_plain, proj_square), ('dp', 'chan'))  64.5 us
  transfers between devices with their start and end apart: 5, of which 5 were waited for; matrix products, arithmetic and copies ran while one was open for 2% of the time, Pallas kernels for 0%

commit v1 on v0

v1 whole, which is shorter than its diff:
```python
import jax
import jax.numpy as jnp
from jax import lax
from jax.experimental import pallas as pl
from jax.experimental.pallas import tpu as pltpu
from jax.sharding import PartitionSpec as P

MESH = pl.DeviceIdType.MESH
F32 = jnp.float32
BF16 = jnp.bfloat16
EPSILON = 0.001
PRECISE = lax.Precision.HIGHEST
D = 112
SQZ = 28
EXP = 672
H, W, CELLS = 6, 4, 24
TAPS = 25
BLOCK, BLOCKS = 16, 6
ROWS = 2304
CHUNK = BLOCK * CELLS
LANE = 128
WIDE = 768
GROUPS = WIDE // LANE
TOTAL = 294912.0
OWN = 168
REST = OWN - LANE

AT_EXPAND, AT_DEPTH, AT_VECS, AT_PROJECT, AT_REDUCE, AT_EXCITE, PANEL = 0, 112, 137, 144, 256, 288, 320
AT_R, AT_X, AT_B = 32, 64, 96


def split(values):
    high = values.astype(BF16)
    return high, (values - high.astype(F32)).astype(BF16)


def mm(a, b):
    return lax.dot_general(a, b, (((1,), (0,)), ((), ())), preferred_element_type=F32)


def mm_nt(a, b):
    return lax.dot_general(a, b, (((1,), (1,)), ((), ())), preferred_element_type=F32)


def exact(a, b, dims):
    return lax.dot_general(a, b, ((dims[:1], dims[1:]), ((), ())), precision=PRECISE, preferred_element_type=F32)


def place():
    dp = lax.axis_index("dp")
    z = lax.axis_index("chan")
    return dp // 8, lax.rem(dp // 2, 4), lax.rem(dp, 2), z


def column_peers():
    x, y, c, z = place()
    mine = z * 2 + c
    peers = []
    for k in range(1, 8):
        r = lax.rem(mine + k, 8)
        peers.append((r, (x * 8 + y * 2 + lax.rem(r, 2), r // 2)))
    return mine, peers


def plane_peers():
    x, y, c, z = place()
    mine = x * 4 + y
    peers = []
    for k in range(1, 16):
        r = lax.rem(mine + k, 16)
        peers.append((r, ((r // 4) * 8 + lax.rem(r, 4) * 2 + c, z)))
    return mine, peers


def push(sources, slots, mine, peers, send, recv):
    for rank, device in peers:
        pltpu.make_async_remote_copy(
            src_ref=sources(rank),
            dst_ref=slots.at[mine],
            send_sem=send,
            recv_sem=recv,
            device_id=device,
            device_id_type=MESH,
        ).start()


def drain(view, sem):
    pltpu.make_async_copy(view, view, sem).wait()


def add_slots(slots, count):
    total = slots[0]
    for k in range(1, count):
        total = total + slots[k]
    return total


class Vector:
    def __init__(self, near, far, sems):
        self.near, self.far, self.sems = near, far, sems

    def start(self, value):
        self.mine, peers = column_peers()
        self.near[self.mine] = value
        push(lambda rank: self.near.at[self.mine], self.near, self.mine, peers, self.sems.at[0], self.sems.at[1])

    def middle(self):
        drain(self.near.at[pl.ds(0, 7)], self.sems.at[1])
        mine, peers = plane_peers()
        self.far[mine] = add_slots(self.near, 8)
        push(lambda rank: self.far.at[mine], self.far, mine, peers, self.sems.at[2], self.sems.at[3])

    def finish(self):
        drain(self.far.at[pl.ds(0, 15)], self.sems.at[3])
        return add_slots(self.far, 16)

    def close(self):
        drain(self.near.at[pl.ds(0, 7)], self.sems.at[0])
        drain(self.far.at[pl.ds(0, 15)], self.sems.at[2])


class Panel:
    def __init__(self, source, first, parts, second, third, sems, cut):
        self.source, self.first, self.parts, self.second, self.third = source, first, parts, second, third
        self.sems, self.cut = sems, cut

    def start(self):
        mine, peers = plane_peers()
        self.first[mine] = self.source[mine]
        push(lambda rank: self.source.at[rank], self.first, mine, peers, self.sems.at[0], self.sems.at[1])

    def middle(self):
        drain(self.first.at[pl.ds(0, 15)], self.sems.at[1])
        total = add_slots(self.first, 16)
        mine, peers = column_peers()
        if self.cut:
            for z in range(4):
                self.parts[z, :, 0:LANE] = total[:, z * LANE : (z + 1) * LANE]
                rest = 4 + z // 2
                self.parts[z, :, LANE : 2 * LANE] = total[:, rest * LANE : (rest + 1) * LANE]
            self.second[mine] = self.parts[mine // 2]
            push(lambda rank: self.parts.at[rank // 2], self.second, mine, peers, self.sems.at[2], self.sems.at[3])
        else:
            self.second[mine] = total
            push(lambda rank: self.second.at[mine], self.second, mine, peers, self.sems.at[2], self.sems.at[3])

    def last(self):
        drain(self.second.at[pl.ds(0, 7)], self.sems.at[3])
        mine, peers = plane_peers()
        self.third[mine] = add_slots(self.second, 8)
        push(lambda rank: self.third.at[mine], self.third, mine, peers, self.sems.at[4], self.sems.at[5])

    def finish(self):
        drain(self.third.at[pl.ds(0, 15)], self.sems.at[5])
        return self.third[...].reshape(128, self.third.shape[-1])

    def close(self):
        drain(self.first.at[pl.ds(0, 15)], self.sems.at[0])
        drain(self.second.at[pl.ds(0, 7)], self.sems.at[2])
        drain(self.third.at[pl.ds(0, 15)], self.sems.at[4])


def half_gate(values, scale, shift):
    h = values * scale + shift
    return h, jnp.tanh(h)


def slope_of(h, th):
    return (0.5 + 0.5 * th) * (1.0 + (h - h * th))


def sigmoid(v):
    return 1.0 / (1.0 + jnp.exp(-v))


def kernel(
    f_in, q_in, panel_in, vecs, units,
    out, igrad, o_expand, o_project, o_depth, o_reduce, o_excite, o_vecs, o_small,
    f_rows, q_rows, p_rows, f3, ft, pg3, pgt,
    e_ref, a1, dv, q2, act_hi, act_lo,
    gathered, we, wp, wr, wx, we_b, wp_b, wd, par, gw, cov_we,
    pool, gates, spread, gg, sums, vec, gp_panel, misc, ge_panel, g_panel,
    near1, far1, near2, far2, near3, far3,
    g_first, g_second, g_third,
    p_first, p_parts, p_second, p_third,
    m_first, m_parts, m_second, m_third,
    e_first, e_parts, e_second, e_third,
    w_sems, v_sems, s_sems,
):
    x, y, c, z = place()
    barrier = pltpu.get_barrier_semaphore()
    col_mine, col_peers = column_peers()
    plane_mine, pl_peers = plane_peers()
    for _, device in col_peers + pl_peers:
        pl.semaphore_signal(barrier, inc=1, device_id=device, device_id_type=MESH)
    pl.semaphore_wait(barrier, 22)

    gathered[z] = panel_in[...]
    sections = ((0, AT_DEPTH), (AT_DEPTH, AT_PROJECT), (AT_PROJECT, PANEL))
    for s, (lo, hi) in enumerate(sections):
        for k in range(1, 4):
            pltpu.make_async_remote_copy(
                src_ref=gathered.at[z, pl.ds(lo, hi - lo)],
                dst_ref=gathered.at[z, pl.ds(lo, hi - lo)],
                send_sem=w_sems.at[0, s],
                recv_sem=w_sems.at[1, s],
                device_id={"chan": lax.rem(z + k, 4)},
                device_id_type=MESH,
            ).start()

    def section(s, way):
        lo, hi = sections[s]
        drain(gathered.at[pl.ds(0, 3), pl.ds(lo, hi - lo)], w_sems.at[way, s])

    def assembled(lo, rows):
        parts = [gathered[k, lo : lo + rows, 0:LANE] for k in range(4)]
        for k in (0, 2):
            parts.append(gathered[k, lo : lo + rows, LANE : 2 * LANE] + gathered[k + 1, lo : lo + rows, LANE : 2 * LANE])
        return jnp.concatenate(parts, axis=1)

    lane = lax.broadcasted_iota(jnp.int32, (2, 8, LANE), 2)
    f_rows[...] = jnp.where(lax.broadcasted_iota(jnp.int32, (288, 8, LANE), 2) == D, 1.0, 0.0)
    q_rows[...] = jnp.zeros_like(q_rows)

    @pl.loop(0, BLOCKS)
    def _(b):
        for cell in range(CELLS):
            t = (b * CELLS + cell) * 2
            rows = pl.ds(b * CHUNK + cell, BLOCK, stride=CELLS)
            f_rows[pl.ds(t, 2), :, 0:D] = f_in[rows, :].reshape(2, 8, D)
            q_rows[pl.ds(t, 2), :, 0:D] = q_in[rows, :].reshape(2, 8, D)

    @pl.loop(0, 18)
    def _(i):
        v = f_rows[pl.ds(i * 16, 16)].reshape(128, LANE)
        rows = pl.ds(i * 128, 128)
        hi, lo = split(v)
        f3[rows, 0:128] = hi
        f3[rows, 128:256] = hi
        f3[rows, 256:384] = lo
        hi, lo = split(v.T)
        ft[0:128, rows] = hi
        ft[128:256, rows] = lo

    gram = mm(ft[...], f3[:, 128:384])
    gram = gram[0:128, 0:128] + (gram[0:128, 128:256] + gram[128:256, 0:128]) + gram[128:256, 128:256]
    g_panel[...] = gram.reshape(16, 8, LANE)
    reduce_g = Panel(g_panel, g_first, None, g_second, g_third, s_sems.at[0], False)
    reduce_g.start()

    section(0, 1)
    we[0:D, :] = assembled(0, D)
    we[D:128, :] = jnp.zeros((128 - D, WIDE), F32)
    hi, lo = split(we[...])
    we_b[0:128, :] = hi
    we_b[128:256, :] = lo

    @pl.loop(0, BLOCKS)
    def _(b):
        rows = pl.ds(b * CHUNK, CHUNK)
        for n in range(3):
            cols = slice(n * 256, (n + 1) * 256)
            r = mm(f3[rows, 0:256], we_b[:, cols]) + mm(f3[rows, 256:384], we_b[0:128, cols])
            e_ref[pl.ds(b * 48, 48), :, cols] = r.reshape(48, 8, 256)

    reduce_g.middle()
    section(1, 1)
    taps = assembled(AT_DEPTH, 32)
    for t in range(TAPS):
        wd[t] = jnp.broadcast_to(taps[t : t + 1], (8, WIDE))
    gain1, bias1, gain2, bias2, bx = [taps[TAPS + i : TAPS + i + 1] for i in range(5)]
    section(2, 1)
    wp[0:D, :] = assembled(AT_PROJECT, D)
    wp[D:128, :] = jnp.zeros((128 - D, WIDE), F32)
    wr[...] = assembled(AT_REDUCE, 32)
    wx[...] = assembled(AT_EXCITE, 32)
    reduce_g.last()
    gram = reduce_g.finish() * (1.0 / TOTAL)
    f_mean_row = gram[D : D + 1, :]
    f_mean = gram[:, D : D + 1]
    cov = gram - f_mean * f_mean_row
    cov_we[...] = exact(cov, we[...], (1, 0))
    mean1 = jnp.sum(we[...] * f_mean, axis=0, keepdims=True)
    inv1 = lax.rsqrt(jnp.sum(we[...] * cov_we[...], axis=0, keepdims=True) + EPSILON)
    s1 = gain1 * inv1
    t1 = bias1 - mean1 * s1

    def put(i, row):
        par[i] = jnp.broadcast_to(row, (8, WIDE))

    put(0, 0.5 * s1)
    put(1, 0.5 * t1)

    @pl.loop(0, GROUPS)
    def _(g):
        cols = pl.ds(pl.multiple_of(g * LANE, LANE), LANE)

        def block(b, carry):
            total, square = carry
            base = b * 48
            scale, shift = par[0, :, cols], par[1, :, cols]
            for cell in range(CELLS):
                at = pl.ds(base + 2 * cell, 2)
                h, th = half_gate(e_ref[at, :, cols], scale, shift)
                a1[at, :, cols] = h + h * th
            for i in range(H):
                acc = [None] * W
                for a in range(5):
                    ii = i + a - 2
                    if not 0 <= ii < H:
                        continue
                    w = [wd[a * 5 + k, :, cols] for k in range(5)]
                    for jj in range(W):
                        v = a1[pl.ds(base + 2 * (ii * W + jj), 2), :, cols]
                        for j in range(W):
                            k = jj - j + 2
                            if 0 <= k < 5:
                                term = v * w[k]
                                acc[j] = term if acc[j] is None else acc[j] + term
                for j in range(W):
                    dv[pl.ds(base + 2 * (i * W + j), 2), :, cols] = acc[j]
                    total = total + (acc[j][0] + acc[j][1])
                    sq = acc[j] * acc[j]
                    square = square + (sq[0] + sq[1])
            return total, square

        zero = jnp.zeros((8, LANE), F32)
        total, square = lax.fori_loop(0, BLOCKS, block, (zero, zero))
        sums[pl.ds(g, 1), :] = jnp.sum(total, axis=0, keepdims=True)
        sums[pl.ds(g + 8, 1), :] = jnp.sum(square, axis=0, keepdims=True)

    def wide(rows, first):
        return jnp.concatenate([rows[first + g : first + g + 1, :] for g in range(GROUPS)], axis=1)

    def reduce_vector(near, far, index, value):
        v = Vector(near, far, v_sems.at[index])
        v.start(value)
        v.middle()
        return v, v.finish()

    sum2, got = reduce_vector(near1, far1, 0, sums[...])
    mean2 = wide(got, 0) * (1.0 / TOTAL)
    inv2 = lax.rsqrt(wide(got, 8) * (1.0 / TOTAL) - mean2 * mean2 + EPSILON)
    s2 = gain2 * inv2
    t2 = bias2 - mean2 * s2
    put(2, 0.5 * s2)
    put(3, 0.5 * t2)

    @pl.loop(0, GROUPS)
    def _(g):
        cols = pl.ds(pl.multiple_of(g * LANE, LANE), LANE)

        @pl.loop(0, BLOCKS)
        def _(b):
            scale, shift = par[2, :, cols], par[3, :, cols]
            pooled = jnp.zeros((8, LANE), F32)
            for cell in range(CELLS):
                at = pl.ds(b * 48 + 2 * cell, 2)
                h, th = half_gate(dv[at, :, cols], scale, shift)
                act = h + h * th
                q2[at, :, cols] = slope_of(h, th)
                pooled = pooled + (act[0] + act[1])
                hi, lo = split(act.reshape(16, LANE))
                rows = pl.ds(b * CHUNK + 16 * cell, 16)
                act_hi[rows, cols] = hi
                act_lo[rows, cols] = lo
            pool[b, :, cols] = pooled

    seg = lax.broadcasted_iota(jnp.int32, (8, LANE), 0)
    blk = lax.broadcasted_iota(jnp.int32, (8, LANE), 1)
    u0, u1, u2 = units[z, 0], units[z, 1], units[z, 2]
    lower = jnp.where(seg == 0, 0, jnp.where(seg == 1, u0, u0 + u1))
    length = jnp.where(seg == 0, u0, jnp.where(seg == 1, u1, u2))
    member = jnp.where((seg < 3) & (blk >= lower) & (blk < lower + length), 1.0, 0.0)
    per_count = jnp.where(seg < 3, 1.0 / (length * (BLOCK * CELLS)).astype(F32), 0.0)[:, 0:1]
    live = jnp.where(seg < 3, 1.0, 0.0)[:, 0:1]

    pooled = jnp.zeros((8, WIDE), F32)
    for b in range(BLOCKS):
        pooled = pooled + member[:, b : b + 1] * jnp.sum(pool[b], axis=0, keepdims=True)
    pooled = pooled * per_count
    reduced = exact(pooled, wr[...], (1, 1)) + vecs[0:1, 0:32]
    sig_r = sigmoid(reduced)
    squeezed = reduced * sig_r * live
    gate = sigmoid(exact(squeezed, wx[...], (1, 0)) + bx)

    def of_blocks(rows, b):
        return jnp.sum(member[:, b : b + 1] * rows, axis=0, keepdims=True)

    for b in range(BLOCKS):
        gates[b : b + 1, :] = of_blocks(gate, b)

    def project(b, carry):
        rows = pl.ds(b * CHUNK, CHUNK)
        hi, lo = split(wp[...] * gates[pl.ds(b, 1), :])
        wp_b[b, 0:128, :] = hi
        wp_b[b, 128:256, :] = lo
        r = mm_nt(act_hi[rows, :], wp_b[b])
        r = r[:, 0:128] + r[:, 128:256] + mm_nt(act_lo[rows, :], wp_b[b, 0:128, :])
        r = r.reshape(48, 8, LANE)
        q = q_rows[pl.ds(b * 48, 48)]
        p_rows[pl.ds(b * 48, 48)] = r
        return tuple(old + jnp.sum(new, axis=0) for old, new in zip(carry, (r, r * r, q, q * r)))

    zero = jnp.zeros((8, LANE), F32)
    four = lax.fori_loop(0, BLOCKS, project, (zero,) * 4)
    for i in range(4):
        vec[i : i + 1, :] = jnp.sum(four[i], axis=0, keepdims=True)
    sum3, got = reduce_vector(near2, far2, 1, vec[...])
    got = got * (1.0 / TOTAL)
    gain3, bias3 = vecs[1:2, :], vecs[2:3, :]
    mean3 = got[0:1]
    inv3 = lax.rsqrt(got[1:2] - mean3 * mean3 + EPSILON)
    b3 = got[2:3]
    g3 = (got[3:4] - mean3 * got[2:3]) * inv3
    o_small[0:1, :] = g3[:, 0:D] * TOTAL
    o_small[1:2, :] = b3[:, 0:D] * TOTAL
    s3 = gain3 * inv3
    t3 = bias3 - mean3 * s3
    pg_p = -s3 * inv3 * g3
    pg_0 = -s3 * b3 - pg_p * mean3

    @pl.loop(0, BLOCKS)
    def _(b):
        for cell in range(CELLS):
            at = pl.ds(b * 48 + 2 * cell, 2)
            r = f_rows[at] + (p_rows[at] * s3 + t3)
            out[pl.ds(b * CHUNK + cell, BLOCK, stride=CELLS), :] = r.reshape(16, LANE)[:, 0:D]

    @pl.loop(0, 18)
    def _(i):
        at = pl.ds(i * 16, 16)
        v = (q_rows[at] * s3 + (p_rows[at] * pg_p + pg_0)).reshape(128, LANE)
        rows = pl.ds(i * 128, 128)
        hi, lo = split(v)
        pg3[rows, 0:128] = hi
        pg3[rows, 128:256] = hi
        pg3[rows, 256:384] = lo
        hi, lo = split(v.T)
        pgt[0:128, rows] = hi
        pgt[128:256, rows] = lo

    gp_panel[...] = jnp.zeros_like(gp_panel)
    for b in range(BLOCKS):
        rows = slice(b * CHUNK, (b + 1) * CHUNK)
        for n in range(3):
            cols = slice(n * 256, (n + 1) * 256)
            m = mm(pgt[:, rows], act_hi[rows, cols])
            m = m[0:128] + m[128:256] + mm(pgt[0:128, rows], act_lo[rows, cols])
            gg[b : b + 1, cols] = jnp.sum(m * wp[:, cols], axis=0, keepdims=True)
            gp_panel[:, :, cols] += (m * gates[b : b + 1, cols]).reshape(16, 8, 256)
    reduce_p = Panel(gp_panel, p_first, p_parts, p_second, p_third, s_sems.at[1], True)
    reduce_p.start()

    gate_grad = jnp.zeros((8, WIDE), F32)
    for b in range(BLOCKS):
        gate_grad = gate_grad + member[:, b : b + 1] * gg[b : b + 1, :]
    excite_in = gate_grad * gate * (1.0 - gate)
    misc[...] = jnp.zeros_like(misc)
    misc[AT_X // 8 : AT_X // 8 + 4] = exact(squeezed, excite_in, (0, 0)).reshape(4, 8, WIDE)
    reduced_grad = exact(excite_in, wx[...], (1, 1)) * (sig_r * (1.0 + reduced * (1.0 - sig_r))) * live
    misc[AT_R // 8 : AT_R // 8 + 4] = exact(reduced_grad, pooled, (0, 0)).reshape(4, 8, WIDE)
    misc[AT_B // 8, 0:1, :] = jnp.sum(excite_in, axis=0, keepdims=True)
    for k in range(4):
        misc[AT_B // 8, 1:2, k * LANE : k * LANE + 32] = jnp.sum(reduced_grad, axis=0, keepdims=True)
    pooled_grad = exact(reduced_grad, wr[...], (1, 0)) * per_count
    for b in range(BLOCKS):
        spread[b : b + 1, :] = of_blocks(pooled_grad, b)

    par[8] = jnp.zeros((8, WIDE), F32)
    par[9] = jnp.zeros((8, WIDE), F32)

    @pl.loop(0, BLOCKS)
    def _(b):
        rows = pl.ds(b * CHUNK, CHUNK)
        at = pl.ds(b * 48, 48)
        for n in range(3):
            cols = slice(n * 256, (n + 1) * 256)
            r = mm(pg3[rows, 0:256], wp_b[b, :, cols]) + mm(pg3[rows, 256:384], wp_b[b, 0:128, cols])
            r = (r.reshape(48, 8, 256) + spread[pl.ds(b, 1), cols]) * q2[at, :, cols]
            q2[at, :, cols] = r
            par[8, :, cols] += jnp.sum(r, axis=0)
            par[9, :, cols] += jnp.sum(r * dv[at, :, cols], axis=0)

    for g in range(GROUPS):
        cols = slice(g * LANE, (g + 1) * LANE)
        sums[g : g + 1, :] = jnp.sum(par[8, :, cols], axis=0, keepdims=True)
        sums[g + 8 : g + 9, :] = jnp.sum(par[9, :, cols], axis=0, keepdims=True)
    sum4, got = reduce_vector(near3.at[0], far3.at[0], 2, sums[...])
    b2 = wide(got, 0)
    g2 = (wide(got, 8) - mean2 * b2) * inv2
    c1 = s2
    c3 = -s2 * inv2 * g2 * (1.0 / TOTAL)
    c2 = -s2 * b2 * (1.0 / TOTAL) - c3 * mean2
    put(4, c1)
    put(5, c2)
    put(6, c3)

    def own_lanes(rows):
        first = rows[:, 0:LANE]
        rest = rows[:, LANE : 2 * LANE]
        rest = jnp.where(lax.rem(z, 2) == 1, pltpu.roll(rest, 64, 1), rest)
        return first, rest

    def own_vector(row):
        first = jnp.zeros((1, LANE), F32)
        rest = jnp.zeros((1, LANE), F32)
        for k in range(4):
            first = jnp.where(z == k, row[:, k * LANE : (k + 1) * LANE], first)
        for k in range(2):
            rest = jnp.where(z // 2 == k, row[:, (4 + k) * LANE : (5 + k) * LANE], rest)
        rest = jnp.where(lax.rem(z, 2) == 1, pltpu.roll(rest, 64, 1), rest)
        return first, rest

    def emit_vector(i, row):
        first, rest = own_vector(row)
        o_vecs[i : i + 1, 0:LANE] = first
        o_vecs[i : i + 1, LANE:OWN] = rest[:, 0:REST]

    emit_vector(2, g2)
    emit_vector(3, b2)

    gw[...] = jnp.zeros_like(gw)

    @pl.loop(0, GROUPS)
    def _(g):
        cols = pl.ds(pl.multiple_of(g * LANE, LANE), LANE)

        def block(b, carry):
            total, product = carry
            base = b * 48
            k1, k2, k3 = par[4, :, cols], par[5, :, cols], par[6, :, cols]
            for cell in range(CELLS):
                at = pl.ds(base + 2 * cell, 2)
                q2[at, :, cols] = q2[at, :, cols] * k1 + (dv[at, :, cols] * k3 + k2)
            scale, shift = par[0, :, cols], par[1, :, cols]
            for ip in range(H):
                act = [a1[pl.ds(base + 2 * (ip * W + jp), 2), :, cols] for jp in range(W)]
                acc = [None] * W
                for a in range(5):
                    i = ip - a + 2
                    if not 0 <= i < H:
                        continue
                    w = [wd[a * 5 + k, :, cols] for k in range(5)]
                    part = [None] * 5
                    for j in range(W):
                        v = q2[pl.ds(base + 2 * (i * W + j), 2), :, cols]
                        for jp in range(W):
                            k = jp - j + 2
                            if 0 <= k < 5:
                                term = v * w[k]
                                acc[jp] = term if acc[jp] is None else acc[jp] + term
                                prod = v * act[jp]
                                part[k] = prod if part[k] is None else part[k] + prod
                    for k in range(5):
                        gw[a * 5 + k, :, cols] += part[k][0] + part[k][1]
                for jp in range(W):
                    at = pl.ds(base + 2 * (ip * W + jp), 2)
                    e = e_ref[at, :, cols]
                    h, th = half_gate(e, scale, shift)
                    q = acc[jp] * slope_of(h, th)
                    hi, lo = split(q.reshape(16, LANE))
                    rows = pl.ds(b * CHUNK + 16 * (ip * W + jp), 16)
                    act_hi[rows, cols] = hi
                    act_lo[rows, cols] = lo
                    total = total + (q[0] + q[1])
                    qe = q * e
                    product = product + (qe[0] + qe[1])
            return total, product

        zero = jnp.zeros((8, LANE), F32)
        total, product = lax.fori_loop(0, BLOCKS, block, (zero, zero))
        sums[pl.ds(g, 1), :] = jnp.sum(total, axis=0, keepdims=True)
        sums[pl.ds(g + 8, 1), :] = jnp.sum(product, axis=0, keepdims=True)

    sum5 = Vector(near3.at[1], far3.at[1], v_sems.at[3])
    sum5.start(sums[...])
    for t in range(TAPS):
        misc[t // 8, t % 8 : t % 8 + 1, :] = jnp.sum(gw[t], axis=0, keepdims=True)
    reduce_m = Panel(misc, m_first, m_parts, m_second, m_third, s_sems.at[2], True)
    reduce_m.start()
    for n in range(3):
        cols = slice(n * 256, (n + 1) * 256)
        m = mm(ft[...], act_hi[:, cols])
        m = m[0:128] + m[128:256] + mm(ft[0:128, :], act_lo[:, cols])
        ge_panel[:, :, cols] = m.reshape(16, 8, 256)
    reduce_e = Panel(ge_panel, e_first, e_parts, e_second, e_third, s_sems.at[3], True)
    reduce_e.start()
    sum5.middle()
    reduce_p.middle()
    reduce_m.middle()
    reduce_e.middle()
    reduce_p.last()
    got = sum5.finish()
    reduce_m.last()
    reduce_e.last()
    b1 = wide(got, 0)
    g1 = (wide(got, 8) - mean1 * b1) * inv1
    emit_vector(0, g1)
    emit_vector(1, b1)
    k3 = -s1 * inv1 * g1 * (1.0 / TOTAL)
    k2 = -s1 * b1 * (1.0 / TOTAL) - k3 * mean1
    hi, lo = split(we[...] * s1)
    we_b[0:128, :] = hi
    we_b[128:256, :] = lo
    mix = exact(we[...] * k3, we[...], (1, 1))
    const = exact(jnp.broadcast_to(k2, (8, WIDE)), we[...], (1, 1))[0:1, :]
    mix = jnp.where(lax.broadcasted_iota(jnp.int32, (128, LANE), 0) == D, const, mix)
    mix_hi, mix_lo = split(mix)
    mix_all = jnp.concatenate([mix_hi, mix_lo], axis=0)

    @pl.loop(0, BLOCKS)
    def _(b):
        rows = pl.ds(b * CHUNK, CHUNK)
        r = mm_nt(act_hi[rows, :], we_b[...])
        r = r[:, 0:128] + r[:, 128:256] + mm_nt(act_lo[rows, :], we_b[0:128, :])
        r = r + mm(f3[rows, 0:256], mix_all) + mm(f3[rows, 256:384], mix_hi)
        r = q_rows[pl.ds(b * 48, 48)] + r.reshape(48, 8, LANE)
        p_rows[pl.ds(b * 48, 48)] = r
        for cell in range(CELLS):
            at = pl.ds(b * 48 + 2 * cell, 2)
            igrad[pl.ds(b * CHUNK + cell, BLOCK, stride=CELLS), :] = p_rows[at].reshape(16, LANE)[:, 0:D]

    def own_wide(rows):
        first = jnp.zeros((rows.shape[0], LANE), F32)
        rest = jnp.zeros((rows.shape[0], LANE), F32)
        for k in range(4):
            first = jnp.where(z == k, rows[:, k * LANE : (k + 1) * LANE], first)
        for k in range(2):
            rest = jnp.where(z // 2 == k, rows[:, (4 + k) * LANE : (5 + k) * LANE], rest)
        return jnp.concatenate([first, rest], axis=1)

    total_p = reduce_p.finish()
    first, rest = own_lanes(total_p)
    o_project[0:LANE, :] = first.T[:, 0:D]
    o_project[LANE:OWN, :] = rest.T[0:REST, 0:D]
    total_m = reduce_m.finish()
    first, rest = own_lanes(total_m)
    o_depth[:, 0:LANE] = first[0:TAPS]
    o_depth[:, LANE:OWN] = rest[0:TAPS, 0:REST]
    o_excite[:, 0:LANE] = first[AT_X : AT_X + SQZ]
    o_excite[:, LANE:OWN] = rest[AT_X : AT_X + SQZ, 0:REST]
    o_reduce[0:LANE, :] = first.T[:, AT_R : AT_R + SQZ]
    o_reduce[LANE:OWN, :] = rest.T[0:REST, AT_R : AT_R + SQZ]
    o_vecs[4:5, 0:LANE] = first[AT_B : AT_B + 1]
    o_vecs[4:5, LANE:OWN] = rest[AT_B : AT_B + 1, 0:REST]
    o_small[2:3, :] = first[AT_B + 1 : AT_B + 2, 0:D]
    total_e = reduce_e.finish()
    fix = own_wide(s1) * (total_e - f_mean * own_wide(b1) - own_wide(cov_we[...]) * own_wide(inv1 * g1))
    first, rest = own_lanes(fix)
    o_expand[:, 0:LANE] = first[0:D]
    o_expand[:, LANE:OWN] = rest[0:D, 0:REST]

    for s in range(3):
        section(s, 0)
    for item in (reduce_g, sum2, sum3, sum4, sum5, reduce_p, reduce_m, reduce_e):
        item.close()


def body(
    features, seg_units, w_expand, gain_one, bias_one, w_depth, gain_two, bias_two,
    w_reduce, b_reduce, w_excite, b_excite, w_project, gain_three, bias_three, cotangent,
):
    z = lax.axis_index("chan")
    rows = jnp.concatenate(
        [
            w_expand,
            w_depth.reshape(TAPS, OWN),
            jnp.stack([gain_one, bias_one, gain_two, bias_two, b_excite]),
            jnp.zeros((2, OWN), F32),
            w_project.T,
            w_reduce.T,
            jnp.zeros((4, OWN), F32),
            w_excite,
            jnp.zeros((4, OWN), F32),
        ],
        axis=0,
    )
    rest = jnp.pad(rows[:, LANE:], ((0, 0), (0, 64 - REST)))
    blank = jnp.zeros_like(rest)
    odd = lax.rem(z, 2) == 1
    panel = jnp.concatenate([rows[:, :LANE], jnp.where(odd, blank, rest), jnp.where(odd, rest, blank)], axis=1)
    small = jnp.stack(
        [
            jnp.pad(b_reduce, (0, LANE - SQZ)),
            jnp.pad(gain_three, (0, LANE - D)),
            jnp.pad(bias_three, (0, LANE - D)),
        ]
    )
    small = jnp.pad(small, ((0, 5), (0, 0)))
    vm = pl.BlockSpec(memory_space=pltpu.VMEM)
    big = pltpu.VMEM((288, 8, WIDE), F32)
    rows128 = pltpu.VMEM((288, 8, LANE), F32)
    half = pltpu.VMEM((ROWS, WIDE), BF16)

    def f32(*shape):
        return pltpu.VMEM(shape, F32)

    def b16(*shape):
        return pltpu.VMEM(shape, BF16)

    panel_scratch = [f32(16, 8, WIDE), f32(4, 8, 256), f32(8, 8, 256), f32(16, 8, 256)]
    result = pl.pallas_call(
        kernel,
        out_shape=(
            jax.ShapeDtypeStruct((ROWS, D), F32),
            jax.ShapeDtypeStruct((ROWS, D), F32),
            jax.ShapeDtypeStruct((D, OWN), F32),
            jax.ShapeDtypeStruct((OWN, D), F32),
            jax.ShapeDtypeStruct((TAPS, OWN), F32),
            jax.ShapeDtypeStruct((OWN, SQZ), F32),
            jax.ShapeDtypeStruct((SQZ, OWN), F32),
            jax.ShapeDtypeStruct((8, OWN), F32),
            jax.ShapeDtypeStruct((8, D), F32),
        ),
        in_specs=[vm, vm, vm, vm, pl.BlockSpec(memory_space=pltpu.SMEM)],
        out_specs=(vm,) * 9,
        scratch_shapes=[
            rows128, rows128, rows128, b16(ROWS, 384), b16(256, ROWS), b16(ROWS, 384), b16(256, ROWS),
            big, big, big, big, half, half,
            f32(4, PANEL, 256), f32(128, WIDE), f32(128, WIDE), f32(32, WIDE), f32(32, WIDE),
            b16(256, WIDE), b16(BLOCKS, 256, WIDE), f32(TAPS, 8, WIDE), f32(10, 8, WIDE), f32(TAPS, 8, WIDE), f32(128, WIDE),
            f32(8, 8, WIDE), f32(8, WIDE), f32(8, WIDE), f32(8, WIDE), f32(16, LANE), f32(8, LANE),
            f32(16, 8, WIDE), f32(16, 8, WIDE), f32(16, 8, WIDE), f32(16, 8, LANE),
            f32(8, 16, LANE), f32(16, 16, LANE), f32(8, 8, LANE), f32(16, 8, LANE), f32(2, 8, 16, LANE), f32(2, 16, 16, LANE),
            f32(16, 8, LANE), f32(8, 8, LANE), f32(16, 8, LANE),
        ]
        + panel_scratch * 3
        + [
            pltpu.SemaphoreType.DMA((2, 3)),
            pltpu.SemaphoreType.DMA((4, 4)),
            pltpu.SemaphoreType.DMA((4, 6)),
        ],
        compiler_params=pltpu.CompilerParams(
            collective_id=0, has_side_effects=True, vmem_limit_bytes=64 * 1024 * 1024 - 65536
        ),
    )(features, cotangent, panel, small, seg_units)
    out, igrad, expand, project, depth, reduce, excite, vecs, little = result
    return (
        out,
        igrad,
        expand,
        vecs[0],
        vecs[1],
        depth.reshape(5, 5, OWN),
        vecs[2],
        vecs[3],
        reduce,
        little[2, :SQZ],
        excite,
        vecs[4],
        project,
        little[0],
        little[1],
    )


def solution(mesh):
    placed = (
        P(("dp", "chan"), None),
        P("dp", None),
        P(None, "chan"),
        P("chan"),
        P("chan"),
        P(None, None, "chan"),
        P("chan"),
        P("chan"),
        P("chan", None),
        P(),
        P(None, "chan"),
        P("chan"),
        P("chan", None),
        P(),
        P(),
        P(("dp", "chan"), None),
    )
    return jax.shard_map(
        body,
        mesh=mesh,
        in_specs=placed,
        out_specs=(
            P(("dp", "chan"), None),
            P(("dp", "chan"), None),
            P(None, "chan"),
            P("chan"),
            P("chan"),
            P(None, None, "chan"),
            P("chan"),
            P("chan"),
            P("chan", None),
            P(),
            P(None, "chan"),
            P("chan"),
            P("chan", None),
            P(),
            P(),
        ),
        check_vma=False,
    )
```

time: 1400 us -> 147 us (0.10)
  blocking collectives: 459 us -> 0 us
  other arithmetic: 458 us -> 1.47 us
  waiting for transfers between devices: 257 us -> 0 us
  local copies, waits for them, and re-layouts: 147 us -> 19.7 us
  Pallas kernels: 0 us -> 125 us
  matrix products: 51.1 us -> 0 us
    psum x8 -> x0, blocking collectives: 459 us -> none  [the longest x2 187 us: norm_grads(): return lax.psum((sum_plain, sum_product), 'dp')]
    reduce_sum x11 -> x0, other arithmetic: 289 us -> none  [the longest x3 148 us: depthwise(): result = result + window * kernel[shift_down, shift_right]]
    pallas_call x0 -> x1, Pallas kernels: none -> 125 us  [body(): pl.pallas_call(kernel, out_shape=(jax.ShapeDtypeStruct((ROWS, D), F32), j...]
    psum x1 -> x0, waiting for transfers between devices: 100 us -> none  [body(): lax.psum((grad_expand, grad_depth, grad_reduce, grad_reduce_bias, grad_ex...]
    add_any x3 -> x0, other arithmetic: 97.5 us -> none  [the longest x2 97.5 us: depthwise(): padded[:, shift_down:shift_down + tall_cells, shift_right:shift_right + w...]
    all_gather x2 -> x0, waiting for transfers between devices: 82.8 us -> none  [rows_gather(): return lax.all_gather(values, 'chan', axis=0, tiled=True)]
    reduce_scatter x2 -> x0, waiting for transfers between devices: 73.4 us -> none  [the longest x1 43 us: body(): lax.psum_scatter(jnp.dot(scaled, w_project, precision=PRECISE), 'chan', s...]
    reshape x8 -> x2, local copies, waits for them, and re-layouts: 73.7 us -> 1.41 us  [the longest x1 0.78 us: body(): w_depth.reshape(TAPS, OWN)]
  transfers between devices with their start and end apart: 5 -> 0, of which waited for: 5 -> 0; matrix products, arithmetic and copies ran while one was open for 2% -> 0% of each run, Pallas kernels for 0% -> 0%
where the time goes in v1:
time: 147 us
  Pallas kernels  125 us (85%)
  local copies, waits for them, and re-layouts  19.7 us (13%)
  other arithmetic  1.47 us (1%)
    pallas_call x1, Pallas kernels, body(): pl.pallas_call(kernel, out_shape=(jax.ShapeDtypeStruct((ROWS, D), F32), j...  125 us
    unnamed x28, local copies, waits for them, and re-layouts  11.5 us

profile of v1, /device:TPU:1, one launch (start us, length us, event | category | flops | bytes accessed | tf_op | source)
XLA Modules:
  0.0 146.8 jit_solution(2418130154110223167)
XLA Ops:
  0.6 0.7 pad_bitcast_fusion.2
  1.3 0.7 pad_bitcast_fusion
  2.0 0.6 select_maximum_fusion.vecs
  2.6 0.8 reshape.36
  3.4 1.0 copy.32
  4.4 1.0 copy.31
  5.4 0.0 copy-start.1
  5.4 2.4 %concatenate.6 = f32[320,168]{1,0:T(8,128)S(1)} concatenate(f32[112,168]{1,0:T(8,128)S(1)} %copy.32, f32[25,168]{1,0:T(8,128)S(1)} %reshape.36, f32[1,168]{1,0:T(1,128)} %bitcast.26, f32[1,168]{1,0:T(1,128)} %bitcast.27, f32[1,168]{1,0:T(1,128)} %bitcast.28, f32[1,168]{1,0:T(1,128)} %bitcast.29, f32[1,168]{1,0:T(1,128)} %bitcast.30, f32[2,168]{1,0:T(2,128)S(1)} %broadcast_in_dim.6, ...), dimensions={0} | concatenate | bytes 430080 | tf_op jit(solution)/shard_map/concatenate | solution.py:665
  7.9 0.8 pad_maximum_fusion.panel_in
  8.7 0.0 copy-done.1
  8.7 0.0 copy-start.2
  8.7 1.4 copy.33.f_in
  10.1 0.0 copy-done.2
  10.1 1.4 copy.34.q_in
  11.5 124.8 %shard_map.271 = (f32[2304,112]{1,0:T(8,128)}, f32[2304,112]{1,0:T(8,128)}, f32[112,168]{1,0:T(8,128)}, f32[168,112]{1,0:T(8,128)}, f32[25,168]{1,0:T(8,128)}, /...) custom-call(f32[2304,112]{1,0:T(8,128)} %copy.33.f_in, f32[2304,112]{1,0:T(8,128)} %copy.34.q_in, ...), custom_call_target="tpu_custom_call" | custom-call | tf_op jit(solution)/shard_map/pallas_call | solution.py:703
  136.3 0.0 copy-start.8
  136.3 0.0 copy-start.5
  136.4 0.0 copy-start.7
  136.4 0.0 copy-start.3
  136.4 0.0 copy-start
  136.4 2.7 %copy.35 = f32[2304,112]{0,1:T(8,128)} copy(f32[2304,112]{1,0:T(8,128)} %get-tuple-element.33) | data formatting | bytes 2064384
  139.1 1.2 slice_bitcast_fusion.2
  140.3 1.3 slice_bitcast_fusion
  141.5 0.0 copy-done.8
  141.5 0.6 fusion
  142.1 0.0 copy-done.5
  142.1 0.7 copy.38
  142.8 0.0 copy-done.7
  142.8 0.6 reshape.37
  143.4 0.0 copy-done.3
  143.5 0.0 copy-start.6
  143.5 0.7 copy.37
  144.2 0.0 copy-done
  144.2 0.0 copy-start.4
  144.2 1.3 copy.36
  145.5 0.0 copy-done.6
  145.5 0.6 copy.41
  146.1 0.0 copy-done.4
  146.1 0.6 copy.42
  (5 shorter events, 0.1 us)
Async XLA Ops:
  5.4 3.4 %copy-start.1 = (f32[2304,112]{0,1:T(8,128)S(1)}, f32[2304,112]{0,1:T(8,128)}, u32[]{:S(2)}) copy-start(f32[2304,112]{0,1:T(8,128)} %param.16) | copy-start | bytes 3096580
  8.7 1.4 copy-start.2
  136.3 5.2 %copy-start.8 = (f32[8,168]{1,0:T(8,128)S(1)}, f32[8,168]{1,0:T(8,128)}, u32[]{:S(2)}) copy-start(f32[8,168]{1,0:T(8,128)} %get-tuple-element.27) | copy-start | bytes 16132
  136.3 5.8 %copy-start.5 = (f32[168,28]{1,0:T(8,128)S(1)}, f32[168,28]{1,0:T(8,128)}, u32[]{:S(2)}) copy-start(f32[168,28]{1,0:T(8,128)} %get-tuple-element.41) | copy-start | bytes 56452
  136.4 6.5 %copy-start.7 = (f32[25,168]{1,0:T(8,128)S(1)}, f32[25,168]{1,0:T(8,128)}, u32[]{:S(2)}) copy-start(f32[25,168]{1,0:T(8,128)} %get-tuple-element.28) | copy-start | bytes 50404
  136.4 7.1 %copy-start.3 = (f32[112,168]{1,0:T(8,128)S(1)}, f32[112,168]{1,0:T(8,128)}, u32[]{:S(2)}) copy-start(f32[112,168]{1,0:T(8,128)} %get-tuple-element.35) | copy-start | bytes 225796
  136.4 7.8 %copy-start = (f32[2304,112]{1,0:T(8,128)S(1)}, f32[2304,112]{1,0:T(8,128)}, u32[]{:S(2)}) copy-start(f32[2304,112]{1,0:T(8,128)} %get-tuple-element.34) | copy-start | bytes 3096580
  143.5 2.1 %copy-start.6 = (f32[28,168]{1,0:T(8,128)S(1)}, f32[28,168]{1,0:T(8,128)}, u32[]{:S(2)}) copy-start(f32[28,168]{1,0:T(8,128)} %get-tuple-element.84) | copy-start | bytes 56452
  144.2 1.9 %copy-start.4 = (f32[168,112]{1,0:T(8,128)S(1)}, f32[168,112]{1,0:T(8,128)}, u32[]{:S(2)}) copy-start(f32[168,112]{1,0:T(8,128)} %get-tuple-element.86) | copy-start | bytes 225796

commit v2 on v1

v2 whole, which is shorter than its diff:
```python
import jax
import jax.numpy as jnp
from jax import lax
from jax.experimental import pallas as pl
from jax.experimental.pallas import tpu as pltpu
from jax.sharding import PartitionSpec as P

MESH = pl.DeviceIdType.MESH
F32 = jnp.float32
BF16 = jnp.bfloat16
EPSILON = 0.001
PRECISE = lax.Precision.HIGHEST
D = 112
SQZ = 28
EXP = 672
H, W, CELLS = 6, 4, 24
TAPS = 25
BLOCK, BLOCKS = 16, 6
ROWS = 2304
CHUNK = BLOCK * CELLS
LANE = 128
WIDE = 768
GROUPS = WIDE // LANE
TOTAL = 294912.0
OWN = 168
REST = OWN - LANE

AT_EXPAND, AT_DEPTH, AT_VECS, AT_PROJECT, AT_REDUCE, AT_EXCITE, PANEL = 0, 112, 137, 144, 256, 288, 320
AT_R, AT_X, AT_B = 32, 64, 96
OUT_PROJECT, OUT_MISC, OUT_VECS, OUT_SMALL, RESULTS = 128, 256, 384, 392, 400
GROUP = 2 * LANE


REPS = {}


def rep(name):
    count = REPS.get(name, 1)

    def run(fn):
        if count == 1:
            fn()
        else:
            lax.fori_loop(0, count, lambda i, carry: (fn(), carry)[1], 0)

    return run


def rloop(name, size):
    count = REPS.get(name, 1)

    def run(fn):
        if count == 1:
            pl.loop(0, size)(fn)
        else:
            pl.loop(0, size * count)(lambda i: fn(lax.rem(i, size)))

    return run


def split(values):
    high = values.astype(BF16)
    return high, (values - high.astype(F32)).astype(BF16)


def mm(a, b):
    return lax.dot_general(a, b, (((1,), (0,)), ((), ())), preferred_element_type=F32)


def mm_nt(a, b):
    return lax.dot_general(a, b, (((1,), (1,)), ((), ())), preferred_element_type=F32)


def exact(a, b, dims):
    return lax.dot_general(a, b, ((dims[:1], dims[1:]), ((), ())), precision=PRECISE, preferred_element_type=F32)


def place():
    dp = lax.axis_index("dp")
    z = lax.axis_index("chan")
    return dp // 8, lax.rem(dp // 2, 4), lax.rem(dp, 2), z


def ring(step):
    return min(step, 4 - step)


def column_peers():
    x, y, c, z = place()
    moves = [(dz, dc) for dz in range(4) for dc in range(2) if dz or dc]
    moves.sort(key=lambda m: -10 * ring(m[0]) - m[1])
    peers = []
    for dz, dc in moves:
        pz, pc = lax.rem(z + dz, 4), lax.rem(c + dc, 2)
        peers.append((pz * 2 + pc, (x * 8 + y * 2 + pc, pz)))
    return z * 2 + c, peers


def plane_peers():
    x, y, c, z = place()
    moves = [(dx, dy) for dx in range(4) for dy in range(4) if dx or dy]
    moves.sort(key=lambda m: -ring(m[0]) - ring(m[1]))
    peers = []
    for dx, dy in moves:
        px, py = lax.rem(x + dx, 4), lax.rem(y + dy, 4)
        peers.append((px * 4 + py, (px * 8 + py * 2 + c, z)))
    return x * 4 + y, peers


def push(sources, slots, mine, peers, send, recv):
    for rank, device in peers:
        pltpu.make_async_remote_copy(
            src_ref=sources(rank),
            dst_ref=slots.at[mine],
            send_sem=send,
            recv_sem=recv,
            device_id=device,
            device_id_type=MESH,
        ).start()


def drain(view, sem):
    pltpu.make_async_copy(view, view, sem).wait()


def add_slots(slots, count):
    total = slots[0]
    for k in range(1, count):
        total = total + slots[k]
    return total


class Vector:
    def __init__(self, near, far, sems):
        self.near, self.far, self.sems = near, far, sems

    def start(self, value):
        mine, peers = column_peers()
        self.near[mine] = value
        push(lambda rank: self.near.at[mine], self.near, mine, peers, self.sems.at[0], self.sems.at[1])

    def middle(self):
        drain(self.near.at[pl.ds(0, 7)], self.sems.at[1])
        mine, peers = plane_peers()
        self.far[mine] = add_slots(self.near, 8)
        push(lambda rank: self.far.at[mine], self.far, mine, peers, self.sems.at[2], self.sems.at[3])

    def finish(self):
        drain(self.far.at[pl.ds(0, 15)], self.sems.at[3])
        return add_slots(self.far, 16)

    def close(self):
        drain(self.near.at[pl.ds(0, 7)], self.sems.at[0])
        drain(self.far.at[pl.ds(0, 15)], self.sems.at[2])


class Square:
    def __init__(self, source, first, second, third, sems):
        self.source, self.first, self.second, self.third, self.sems = source, first, second, third, sems

    def start(self):
        mine, peers = column_peers()
        self.first[mine] = self.source[mine]
        push(lambda rank: self.source.at[rank], self.first, mine, peers, self.sems.at[0], self.sems.at[1])

    def middle(self):
        drain(self.first.at[pl.ds(0, 7)], self.sems.at[1])
        mine, peers = plane_peers()
        self.second[mine] = add_slots(self.first, 8)
        push(lambda rank: self.second.at[mine], self.second, mine, peers, self.sems.at[2], self.sems.at[3])

    def last(self):
        drain(self.second.at[pl.ds(0, 15)], self.sems.at[3])
        mine, peers = column_peers()
        self.third[mine] = add_slots(self.second, 16)
        push(lambda rank: self.third.at[mine], self.third, mine, peers, self.sems.at[4], self.sems.at[5])

    def finish(self):
        drain(self.third.at[pl.ds(0, 7)], self.sems.at[5])
        return self.third[...].reshape(128, LANE)

    def close(self):
        drain(self.first.at[pl.ds(0, 7)], self.sems.at[0])
        drain(self.second.at[pl.ds(0, 15)], self.sems.at[2])
        drain(self.third.at[pl.ds(0, 7)], self.sems.at[4])


class Panel:
    def __init__(self, source, first, parts, second, third, sems):
        self.source, self.first, self.parts, self.second, self.third, self.sems = source, first, parts, second, third, sems

    def start(self, group):
        mine, peers = plane_peers()
        self.first[group, mine] = self.source[group, mine]
        push(
            lambda rank: self.source.at[group, rank], self.first.at[group], mine, peers,
            self.sems.at[0], self.sems.at[1 + group],
        )

    def middle(self):
        totals = []
        for group in range(3):
            drain(self.first.at[group, pl.ds(0, 15)], self.sems.at[1 + group])
            totals.append(add_slots(self.first.at[group], 16))
        mine, peers = column_peers()
        for z in range(4):
            half = (z % 2) * LANE
            self.parts[z, :, 0:LANE] = totals[z // 2][:, half : half + LANE]
            half = (z // 2) * LANE
            self.parts[z, :, LANE:GROUP] = totals[2][:, half : half + LANE]
        self.second[mine] = self.parts[mine // 2]
        push(lambda rank: self.parts.at[rank // 2], self.second, mine, peers, self.sems.at[4], self.sems.at[5])

    def last(self):
        drain(self.second.at[pl.ds(0, 7)], self.sems.at[5])
        mine, peers = plane_peers()
        self.third[mine] = add_slots(self.second, 8)
        push(lambda rank: self.third.at[mine], self.third, mine, peers, self.sems.at[6], self.sems.at[7])

    def finish(self):
        drain(self.third.at[pl.ds(0, 15)], self.sems.at[7])
        return self.third[...].reshape(128, GROUP)

    def close(self):
        for group in range(3):
            drain(self.first.at[group, pl.ds(0, 15)], self.sems.at[0])
        drain(self.second.at[pl.ds(0, 7)], self.sems.at[4])
        drain(self.third.at[pl.ds(0, 15)], self.sems.at[6])


def half_gate(values, scale, shift):
    h = values * scale + shift
    return h, jnp.tanh(h)


def slope_of(h, th):
    return (0.5 + 0.5 * th) * (1.0 + (h - h * th))


def sigmoid(v):
    return 1.0 / (1.0 + jnp.exp(-v))


def lanes_of(g):
    return pl.ds(pl.multiple_of(g * LANE, LANE), LANE)


def fold(v):
    return v[0] + v[1]


def row_sum(v):
    return jnp.sum(v, axis=0, keepdims=True)


def products(target, left, right, base, cols):
    for a in range(5):
        acc = [None] * 5
        for i in range(H):
            ii = i + a - 2
            if not 0 <= ii < H:
                continue
            other = [right[pl.ds(base + 2 * (ii * W + jj), 2), :, cols] for jj in range(W)]
            for j in range(W):
                v = left[pl.ds(base + 2 * (i * W + j), 2), :, cols]
                for jj in range(W):
                    k = jj - j + 2
                    if 0 <= k < 5:
                        term = v * other[jj]
                        acc[k] = term if acc[k] is None else acc[k] + term
        for k in range(5):
            target[a * 5 + k, :, cols] += fold(acc[k])


def kernel(
    f_in, q_in, we_in, wp_in, wr_in, wx_in, wd_in, ga1_in, bi1_in, ga2_in, bi2_in, bx_in, br_in, ga3_in, bi3_in, units,
    out, igrad, o_panel,
    stage, wide_stage,
    f_rows, q_rows, p_rows, f3, ft, pg3, pgt,
    e_ref, a1, dv, q2, act_hi, act_lo,
    gathered, we, wp, wr, wx, we_b, wp_b, wd, par, tq, td, cells, cov_we,
    pool, gates, spread, gg, vec, sums, gp_panel, misc, ge_panel, g_panel,
    near, far,
    g_first, g_second, g_third,
    p_first, p_parts, p_second, p_third,
    m_first, m_parts, m_second, m_third,
    e_first, e_parts, e_second, e_third,
    w_sems, v_sems, g_sems, s_sems,
):
    x, y, c, z = place()
    barrier = pltpu.get_barrier_semaphore()
    for _, device in column_peers()[1] + plane_peers()[1]:
        pl.semaphore_signal(barrier, inc=1, device_id=device, device_id_type=MESH)

    vectors = [Vector(near.at[i], far.at[i], v_sems.at[i]) for i in range(7)]
    sum2a, sum2b, sum3, sum4a, sum4b, sum5a, sum5b = vectors
    reduce_g = Square(g_panel, g_first, g_second, g_third, g_sems)
    reduce_p = Panel(gp_panel, p_first, p_parts, p_second, p_third, s_sems.at[0])
    reduce_m = Panel(misc, m_first, m_parts, m_second, m_third, s_sems.at[1])
    reduce_e = Panel(ge_panel, e_first, e_parts, e_second, e_third, s_sems.at[2])

    ones = jnp.where(lax.broadcasted_iota(jnp.int32, (16, ROWS), 0) == 0, 1.0, 0.0)
    hi, lo = split(jnp.concatenate([f_in[...], ones], axis=0))
    ft[0:128, :] = hi
    ft[128:256, :] = lo
    gram = mm_nt(ft[...], ft[...])
    gram = gram[0:128, 0:128] + (gram[0:128, 128:256] + gram[128:256, 0:128]) + gram[128:256, 128:256]
    g_panel[...] = gram.reshape(8, 16, LANE)
    pl.semaphore_wait(barrier, 22)
    reduce_g.start()

    sections = ((0, AT_DEPTH), (AT_DEPTH, AT_PROJECT), (AT_PROJECT, PANEL))
    odd = lax.rem(z, 2) == 1

    def send_section(s):
        lo, hi = sections[s]
        rest = gathered[z, lo:hi, LANE:GROUP]
        gathered[z, lo:hi, LANE:GROUP] = jnp.where(odd, pltpu.roll(rest, 64, 1), rest)
        for k in (2, 1, 3):
            pltpu.make_async_remote_copy(
                src_ref=gathered.at[z, pl.ds(lo, hi - lo)],
                dst_ref=gathered.at[z, pl.ds(lo, hi - lo)],
                send_sem=w_sems.at[0, s],
                recv_sem=w_sems.at[1, s],
                device_id={"chan": lax.rem(z + k, 4)},
                device_id_type=MESH,
            ).start()

    def section(s, way):
        lo, hi = sections[s]
        drain(gathered.at[pl.ds(0, 3), pl.ds(lo, hi - lo)], w_sems.at[way, s])

    def assembled(lo, rows):
        parts = [gathered[k, lo : lo + rows, 0:LANE] for k in range(4)]
        for k in (0, 2):
            parts.append(gathered[k, lo : lo + rows, LANE:GROUP] + gathered[k + 1, lo : lo + rows, LANE:GROUP])
        return jnp.concatenate(parts, axis=1)

    gathered[z] = jnp.zeros((PANEL, GROUP), F32)
    wide_stage[...] = jnp.zeros_like(wide_stage)
    wide_stage[0:OWN, 0:D] = we_in[...]
    gathered[z, 0:D, :] = wide_stage[...].T[0:D]
    send_section(0)
    for a in range(5):
        gathered[z, AT_DEPTH + 5 * a : AT_DEPTH + 5 * a + 5, 0:OWN] = wd_in[a]
    for i, row in enumerate((ga1_in, bi1_in, ga2_in, bi2_in, bx_in)):
        gathered[z, AT_VECS + i : AT_VECS + i + 1, 0:OWN] = row[...]
    send_section(1)

    tail = jnp.where(lax.broadcasted_iota(jnp.int32, (16, LANE), 0) == 0, 1.0, 0.0)

    def rows_of(source, tail, target):
        @pl.loop(0, BLOCKS)
        def _(b):
            for i in range(3):
                v = source[:, pl.ds(pl.multiple_of(b * CHUNK + i * LANE, LANE), LANE)]
                stage[i * LANE : (i + 1) * LANE, :] = jnp.concatenate([v, tail], axis=0).T
            for cell in range(CELLS):
                v = stage[pl.ds(cell, BLOCK, stride=CELLS), :]
                target[pl.ds((b * CELLS + cell) * 2, 2)] = v.reshape(2, 8, LANE)

    rows_of(f_in, tail, f_rows)

    @rloop("ft", 18)
    def _(i):
        v = f_rows[pl.ds(i * 16, 16)].reshape(128, LANE)
        rows = pl.ds(pl.multiple_of(i * 128, 128), 128)
        hi, lo = split(v)
        f3[rows, 0:128] = hi
        f3[rows, 128:256] = hi
        f3[rows, 256:384] = lo
        hi, lo = split(v.T)
        ft[0:128, rows] = hi
        ft[128:256, rows] = lo

    reduce_g.middle()

    section(0, 1)
    we[0:D, :] = assembled(0, D)
    we[D:128, :] = jnp.zeros((128 - D, WIDE), F32)
    hi, lo = split(we[...])
    we_b[0:128, :] = hi
    we_b[128:256, :] = lo

    @rloop("E", BLOCKS)
    def _(b):
        rows = pl.ds(pl.multiple_of(b * CHUNK, CHUNK), CHUNK)
        for n in range(3):
            cols = slice(n * GROUP, (n + 1) * GROUP)
            r = mm(f3[rows, 0:256], we_b[:, cols]) + mm(f3[rows, 256:384], we_b[0:128, cols])
            e_ref[pl.ds(b * 48, 48), :, cols] = r.reshape(48, 8, GROUP)

    reduce_g.last()
    section(1, 1)
    taps = assembled(AT_DEPTH, 32)
    for t in range(TAPS):
        wd[t] = jnp.broadcast_to(taps[t : t + 1], (8, WIDE))
    gain1, bias1, gain2, bias2, bx = [taps[TAPS + i : TAPS + i + 1] for i in range(5)]
    rows_of(q_in, jnp.zeros((16, LANE), F32), q_rows)
    sums[...] = jnp.zeros_like(sums)
    tq[...] = jnp.zeros_like(tq)
    td[...] = jnp.zeros_like(td)
    cells[...] = jnp.zeros_like(cells)

    gram = reduce_g.finish() * (1.0 / TOTAL)
    wide_stage[0:OWN, 0:D] = wp_in[...]
    gathered[z, AT_PROJECT : AT_PROJECT + D, :] = wide_stage[...].T[0:D]
    gathered[z, AT_REDUCE : AT_REDUCE + SQZ, 0:OWN] = wr_in[...]
    gathered[z, AT_EXCITE : AT_EXCITE + SQZ, 0:OWN] = wx_in[...]
    send_section(2)
    f_mean_row = gram[D : D + 1, :]
    f_mean = gram[:, D : D + 1]
    cov = gram - f_mean * f_mean_row
    cov_we[...] = exact(cov, we[...], (1, 0))
    mean1 = row_sum(we[...] * f_mean)
    inv1 = lax.rsqrt(row_sum(we[...] * cov_we[...]) + EPSILON)
    s1 = gain1 * inv1
    t1 = bias1 - mean1 * s1

    def put(i, row, lo=0, hi=WIDE):
        par[i, :, lo:hi] = jnp.broadcast_to(row, (8, hi - lo))

    put(0, 0.5 * s1)
    put(1, 0.5 * t1)

    def put_sums(first, second, g, low, size):
        sums[pl.ds(g - low, 1), :] = row_sum(first)
        sums[pl.ds(g - low + size, 1), :] = row_sum(second)

    @rloop("conv1", GROUPS)
    def _(g):
        cols = lanes_of(g)

        def block(b, carry):
            total, square = carry
            base = b * 48
            scale, shift = par[0, :, cols], par[1, :, cols]
            for cell in range(CELLS):
                at = pl.ds(base + 2 * cell, 2)
                h, th = half_gate(e_ref[at, :, cols], scale, shift)
                a1[at, :, cols] = h + h * th
            for i in range(H):
                acc = [None] * W
                for a in range(5):
                    ii = i + a - 2
                    if not 0 <= ii < H:
                        continue
                    w = [wd[a * 5 + k, :, cols] for k in range(5)]
                    for jj in range(W):
                        v = a1[pl.ds(base + 2 * (ii * W + jj), 2), :, cols]
                        for j in range(W):
                            k = jj - j + 2
                            if 0 <= k < 5:
                                term = v * w[k]
                                acc[j] = term if acc[j] is None else acc[j] + term
                for j in range(W):
                    dv[pl.ds(base + 2 * (i * W + j), 2), :, cols] = acc[j]
                    total = total + fold(acc[j])
                    square = square + fold(acc[j] * acc[j])
            return total, square

        zero = jnp.zeros((8, LANE), F32)
        total, square = lax.fori_loop(0, BLOCKS, block, (zero, zero))
        put_sums(total, square, g, jnp.where(g < 3, 0, 3), 3)

        @pl.when(g == 2)
        def _():
            sum2a.start(sums[...])

        @pl.when(g == 5)
        def _():
            sum2a.middle()
            sum2b.start(sums[...])

    def wide(rows, first, count):
        return jnp.concatenate([rows[first + g : first + g + 1, :] for g in range(count)], axis=1)

    mean2, inv2 = [None] * 2, [None] * 2

    def second_norm(got, lo, hi):
        count = (hi - lo) // LANE
        mean = wide(got, 0, count) * (1.0 / TOTAL)
        inv = lax.rsqrt(wide(got, count, count) * (1.0 / TOTAL) - mean * mean + EPSILON)
        scale = par[7, 0:1, lo:hi] * inv
        put(2, 0.5 * scale, lo, hi)
        put(3, 0.5 * (par[8, 0:1, lo:hi] - mean * scale), lo, hi)
        put(9, mean, lo, hi)
        put(10, inv, lo, hi)
        put(11, scale, lo, hi)

    put(7, gain2)
    put(8, bias2)

    def one_products(g):
        cols = lanes_of(g)

        @pl.loop(0, BLOCKS)
        def _(b):
            products(td, dv, a1, b * 48, cols)
            for cell in range(CELLS):
                cells[cell, :, cols] += fold(a1[pl.ds(b * 48 + 2 * cell, 2), :, cols])

    def one_activation(g):
        cols = lanes_of(g)

        @pl.loop(0, BLOCKS)
        def _(b):
            scale, shift = par[2, :, cols], par[3, :, cols]
            pooled = jnp.zeros((8, LANE), F32)
            for cell in range(CELLS):
                at = pl.ds(b * 48 + 2 * cell, 2)
                h, th = half_gate(dv[at, :, cols], scale, shift)
                q2[at, :, cols] = th
                act = h + h * th
                pooled = pooled + fold(act)
                hi, lo = split(act.reshape(16, LANE))
                rows = pl.ds(b * CHUNK + 16 * cell, 16)
                act_hi[rows, cols] = hi
                act_lo[rows, cols] = lo
            pool[b, :, cols] = pooled

    @pl.loop(0, 12)
    def _(step):
        @pl.when(step == 3)
        def _():
            sum2b.middle()

        @pl.when(step == 5)
        def _():
            second_norm(sum2a.finish(), 0, 3 * LANE)

        @pl.when(step == 9)
        def _():
            second_norm(sum2b.finish(), 3 * LANE, WIDE)

        early = (step < 5) | (step == 8)

        @pl.when(early)
        def _():
            one_products(jnp.where(step == 8, 5, step))

        @pl.when(jnp.logical_not(early))
        def _():
            one_activation(jnp.where(step < 8, step - 5, step - 6))

    section(2, 1)
    wp[0:D, :] = assembled(AT_PROJECT, D)
    wp[D:128, :] = jnp.zeros((128 - D, WIDE), F32)
    wr[...] = assembled(AT_REDUCE, 32)
    wx[...] = assembled(AT_EXCITE, 32)
    seg = lax.broadcasted_iota(jnp.int32, (8, LANE), 0)
    blk = lax.broadcasted_iota(jnp.int32, (8, LANE), 1)
    u0, u1, u2 = units[z, 0], units[z, 1], units[z, 2]
    lower = jnp.where(seg == 0, 0, jnp.where(seg == 1, u0, u0 + u1))
    length = jnp.where(seg == 0, u0, jnp.where(seg == 1, u1, u2))
    member = jnp.where((seg < 3) & (blk >= lower) & (blk < lower + length), 1.0, 0.0)
    per_count = jnp.where(seg < 3, 1.0 / (length * (BLOCK * CELLS)).astype(F32), 0.0)[:, 0:1]
    live = jnp.where(seg < 3, 1.0, 0.0)[:, 0:1]

    vec[...] = jnp.zeros((8, LANE), F32)
    vec[0:1, 0:SQZ] = br_in[...]
    pooled = jnp.zeros((8, WIDE), F32)
    for b in range(BLOCKS):
        pooled = pooled + member[:, b : b + 1] * row_sum(pool[b])
    pooled = pooled * per_count
    reduced = exact(pooled, wr[...], (1, 1)) + vec[0:1, 0:32]
    sig_r = sigmoid(reduced)
    squeezed = reduced * sig_r * live
    gate = sigmoid(exact(squeezed, wx[...], (1, 0)) + bx)

    def of_blocks(rows, b):
        return row_sum(member[:, b : b + 1] * rows)

    for b in range(BLOCKS):
        gates[b : b + 1, :] = of_blocks(gate, b)

    def project(b, carry):
        rows = pl.ds(pl.multiple_of(b * CHUNK, CHUNK), CHUNK)
        hi, lo = split(wp[...] * gates[pl.ds(b, 1), :])
        wp_b[b, 0:128, :] = hi
        wp_b[b, 128:256, :] = lo
        r = mm_nt(act_hi[rows, :], wp_b[b])
        r = r[:, 0:128] + r[:, 128:256] + mm_nt(act_lo[rows, :], wp_b[b, 0:128, :])
        r = r.reshape(48, 8, LANE)
        q = q_rows[pl.ds(b * 48, 48)]
        p_rows[pl.ds(b * 48, 48)] = r
        return tuple(old + jnp.sum(new, axis=0) for old, new in zip(carry, (r, r * r, q, q * r)))

    zero = jnp.zeros((8, LANE), F32)
    four = lax.fori_loop(0, BLOCKS * REPS.get("proj", 1), lambda i, v: project(lax.rem(i, BLOCKS), v), (zero,) * 4)
    for i in range(4):
        vec[i : i + 1, :] = row_sum(four[i])
    sum3.start(vec[...])

    @rloop("slopes", GROUPS)
    def _(g):
        cols = lanes_of(g)

        @pl.loop(0, BLOCKS)
        def _(b):
            scale, shift = par[0, :, cols], par[1, :, cols]
            scale2, shift2 = par[2, :, cols], par[3, :, cols]
            for cell in range(CELLS):
                at = pl.ds(b * 48 + 2 * cell, 2)
                h, th = half_gate(e_ref[at, :, cols], scale, shift)
                e_ref[at, :, cols] = slope_of(h, th)
                q2[at, :, cols] = slope_of(dv[at, :, cols] * scale2 + shift2, q2[at, :, cols])

        @pl.when(g == 4)
        def _():
            sum3.middle()

    got = sum3.finish() * (1.0 / TOTAL)
    vec[...] = jnp.zeros((8, LANE), F32)
    vec[0:1, 0:D] = ga3_in[...]
    vec[1:2, 0:D] = bi3_in[...]
    gain3, bias3 = vec[0:1, :], vec[1:2, :]
    mean3 = got[0:1]
    inv3 = lax.rsqrt(got[1:2] - mean3 * mean3 + EPSILON)
    b3 = got[2:3]
    g3 = (got[3:4] - mean3 * got[2:3]) * inv3
    o_panel[OUT_SMALL : OUT_SMALL + 1, 0:LANE] = g3 * TOTAL
    o_panel[OUT_SMALL + 1 : OUT_SMALL + 2, 0:LANE] = b3 * TOTAL
    s3 = gain3 * inv3
    t3 = bias3 - mean3 * s3
    pg_p = -s3 * inv3 * g3
    pg_0 = -s3 * b3 - pg_p * mean3

    @rloop("pgs", 18)
    def _(i):
        at = pl.ds(i * 16, 16)
        v = (q_rows[at] * s3 + (p_rows[at] * pg_p + pg_0)).reshape(128, LANE)
        rows = pl.ds(pl.multiple_of(i * 128, 128), 128)
        hi, lo = split(v)
        pg3[rows, 0:128] = hi
        pg3[rows, 128:256] = hi
        pg3[rows, 256:384] = lo
        hi, lo = split(v.T)
        pgt[0:128, rows] = hi
        pgt[128:256, rows] = lo

    @rep("mm")
    def _():
        gp_panel[...] = jnp.zeros_like(gp_panel)
        for b in range(BLOCKS):
            rows = slice(b * CHUNK, (b + 1) * CHUNK)
            for n in range(3):
                cols = slice(n * GROUP, (n + 1) * GROUP)
                m = mm(pgt[:, rows], act_hi[rows, cols])
                m = m[0:128] + m[128:256] + mm(pgt[0:128, rows], act_lo[rows, cols])
                gg[b : b + 1, cols] = row_sum(m * wp[:, cols])
                gp_panel[n] += (m * gates[b : b + 1, cols]).reshape(16, 8, GROUP)

    for n in range(3):
        reduce_p.start(n)

    gate_grad = jnp.zeros((8, WIDE), F32)
    for b in range(BLOCKS):
        gate_grad = gate_grad + member[:, b : b + 1] * gg[b : b + 1, :]
    excite_in = gate_grad * gate * (1.0 - gate)
    misc[...] = jnp.zeros_like(misc)

    def put_misc(row, values):
        for n in range(3):
            part = values[:, n * GROUP : (n + 1) * GROUP]
            misc[n, row // 8 : (row + values.shape[0]) // 8] = part.reshape(values.shape[0] // 8, 8, GROUP)

    put_misc(AT_X, exact(squeezed, excite_in, (0, 0)))
    reduced_grad = exact(excite_in, wx[...], (1, 1)) * (sig_r * (1.0 + reduced * (1.0 - sig_r))) * live
    put_misc(AT_R, exact(reduced_grad, pooled, (0, 0)))
    for n in range(3):
        misc[n, AT_B // 8, 0:1, :] = row_sum(excite_in)[:, n * GROUP : (n + 1) * GROUP]
    for k in range(4):
        half = (k % 2) * LANE
        misc[k // 2, AT_B // 8, 1:2, half : half + 32] = row_sum(reduced_grad)
    pooled_grad = exact(reduced_grad, wr[...], (1, 0)) * per_count
    for b in range(BLOCKS):
        spread[b : b + 1, :] = of_blocks(pooled_grad, b)

    @rloop("a2g", 3)
    def _(n):
        cols = pl.ds(pl.multiple_of(n * GROUP, GROUP), GROUP)

        def block(b, carry):
            rows = pl.ds(pl.multiple_of(b * CHUNK, CHUNK), CHUNK)
            at = pl.ds(b * 48, 48)
            r = mm(pg3[rows, 0:256], wp_b[b, :, cols]) + mm(pg3[rows, 256:384], wp_b[b, 0:128, cols])
            r = (r.reshape(48, 8, GROUP) + spread[pl.ds(b, 1), cols]) * q2[at, :, cols]
            q2[at, :, cols] = r
            return carry[0] + jnp.sum(r, axis=0), carry[1] + jnp.sum(r * dv[at, :, cols], axis=0)

        zero = jnp.zeros((8, GROUP), F32)
        total, product = lax.fori_loop(0, BLOCKS, block, (zero, zero))
        size = jnp.where(n == 0, 2, 4)
        low = jnp.where(n == 0, 0, 2)
        for half in range(2):
            put_sums(
                total[:, half * LANE : (half + 1) * LANE], product[:, half * LANE : (half + 1) * LANE],
                n * 2 + half, low, size,
            )

        @pl.when(n == 0)
        def _():
            sum4a.start(sums[...])

        @pl.when(n == 2)
        def _():
            sum4b.start(sums[...])

    @rloop("tq", GROUPS)
    def _(g):
        cols = lanes_of(g)

        @pl.loop(0, BLOCKS)
        def _(b):
            products(tq, q2, a1, b * 48, cols)

        @pl.when(g == 1)
        def _():
            sum4a.middle()

        @pl.when(g == 2)
        def _():
            sum4b.middle()

    def second_norm_grad(got, lo, hi):
        count = (hi - lo) // LANE
        mean, inv, scale = [par[i, 0:1, lo:hi] for i in (9, 10, 11)]
        bias = wide(got, 0, count)
        gain = (wide(got, count, count) - mean * bias) * inv
        c3 = -scale * inv * gain * (1.0 / TOTAL)
        put(4, scale, lo, hi)
        put(5, -scale * bias * (1.0 / TOTAL) - c3 * mean, lo, hi)
        put(6, c3, lo, hi)
        put(7, gain, lo, hi)
        put(8, bias, lo, hi)

    def own_lanes(rows):
        first = rows[:, 0:LANE]
        rest = rows[:, LANE:GROUP]
        return first, jnp.where(odd, pltpu.roll(rest, 64, 1), rest)

    def own_wide(rows):
        first = jnp.zeros((rows.shape[0], LANE), F32)
        rest = jnp.zeros((rows.shape[0], LANE), F32)
        for k in range(4):
            first = jnp.where(z == k, rows[:, k * LANE : (k + 1) * LANE], first)
        for k in range(2):
            rest = jnp.where(z // 2 == k, rows[:, (4 + k) * LANE : (5 + k) * LANE], rest)
        return jnp.concatenate([first, rest], axis=1)

    def emit(row, values):
        first, rest = own_lanes(values)
        o_panel[row : row + values.shape[0], 0:LANE] = first
        o_panel[row : row + values.shape[0], LANE:GROUP] = rest

    def emit_vector(i, row):
        emit(OUT_VECS + i, own_wide(row))

    @rloop("conv2", GROUPS)
    def _(g):
        @pl.when(g == 0)
        def _():
            second_norm_grad(sum4a.finish(), 0, GROUP)
            reduce_p.middle()

        @pl.when(g == 2)
        def _():
            second_norm_grad(sum4b.finish(), GROUP, WIDE)
            for t in range(TAPS):
                a, k = t // 5, t % 5
                plain = None
                for i in range(H):
                    for j in range(W):
                        ii, jj = i + a - 2, j + k - 2
                        if 0 <= ii < H and 0 <= jj < W:
                            v = cells[ii * W + jj]
                            plain = v if plain is None else plain + v
                row = row_sum(tq[t] * par[4] + td[t] * par[6] + plain * par[5])
                for n in range(3):
                    misc[n, t // 8, t % 8 : t % 8 + 1, :] = row[:, n * GROUP : (n + 1) * GROUP]
            for n in range(3):
                reduce_m.start(n)
            reduce_p.last()

        @pl.when(g == 5)
        def _():
            reduce_m.middle()

        cols = lanes_of(g)

        @pl.loop(0, BLOCKS)
        def _(b):
            base = b * 48
            k1, k2, k3 = par[4, :, cols], par[5, :, cols], par[6, :, cols]
            for cell in range(CELLS):
                at = pl.ds(base + 2 * cell, 2)
                q2[at, :, cols] = q2[at, :, cols] * k1 + (dv[at, :, cols] * k3 + k2)
            for ip in range(H):
                acc = [None] * W
                for a in range(5):
                    i = ip - a + 2
                    if not 0 <= i < H:
                        continue
                    w = [wd[a * 5 + k, :, cols] for k in range(5)]
                    for j in range(W):
                        v = q2[pl.ds(base + 2 * (i * W + j), 2), :, cols]
                        for jp in range(W):
                            k = jp - j + 2
                            if 0 <= k < 5:
                                term = v * w[k]
                                acc[jp] = term if acc[jp] is None else acc[jp] + term
                for jp in range(W):
                    at = pl.ds(base + 2 * (ip * W + jp), 2)
                    hi, lo = split((acc[jp] * e_ref[at, :, cols]).reshape(16, LANE))
                    rows = pl.ds(b * CHUNK + 16 * (ip * W + jp), 16)
                    act_hi[rows, cols] = hi
                    act_lo[rows, cols] = lo

        @pl.when(lax.rem(g, 2) == 1)
        def _():
            n = g // 2
            cols = pl.ds(pl.multiple_of(n * GROUP, GROUP), GROUP)
            m = mm(ft[...], act_hi[:, cols])
            m = m[0:128] + m[128:256] + mm(ft[0:128, :], act_lo[:, cols])
            ge_panel[n] = m.reshape(16, 8, GROUP)
            product = row_sum(m * we[:, cols])
            size = jnp.where(n < 2, 4, 2)
            low = jnp.where(n < 2, 0, 4)
            for half in range(2):
                sums[pl.ds(g - 1 + half - low, 1), :] = m[D : D + 1, half * LANE : (half + 1) * LANE]
                sums[pl.ds(g - 1 + half - low + size, 1), :] = product[:, half * LANE : (half + 1) * LANE]

            @pl.when(g == 3)
            def _():
                sum5a.start(sums[...])

            @pl.when(g == 5)
            def _():
                sum5a.middle()
                sum5b.start(sums[...])

            reduce_e.start(n)

    hi, lo = split(we[...] * s1)
    we_b[0:128, :] = hi
    we_b[128:256, :] = lo

    @rloop("ig", BLOCKS)
    def _(b):
        rows = pl.ds(pl.multiple_of(b * CHUNK, CHUNK), CHUNK)
        at = pl.ds(b * 48, 48)
        r = mm_nt(act_hi[rows, :], we_b[...])
        r = r[:, 0:128] + r[:, 128:256] + mm_nt(act_lo[rows, :], we_b[0:128, :])
        igrad[at] = q_rows[at] + r.reshape(48, 8, LANE)
        out[at] = f_rows[at] + (p_rows[at] * s3 + t3)

    sum5b.middle()
    reduce_m.last()
    emit(OUT_PROJECT, reduce_p.finish())
    reduce_e.middle()
    emit_vector(2, par[7, 0:1, :])
    emit_vector(3, par[8, 0:1, :])
    first = sum5a.finish()
    reduce_e.last()
    second = sum5b.finish()
    b1 = jnp.concatenate([wide(first, 0, 4), wide(second, 0, 2)], axis=1)
    g1 = (jnp.concatenate([wide(first, 4, 4), wide(second, 2, 2)], axis=1) - mean1 * b1) * inv1
    k3 = -s1 * inv1 * g1 * (1.0 / TOTAL)
    k2 = -s1 * b1 * (1.0 / TOTAL) - k3 * mean1
    mix = exact(we[...] * k3, we[...], (1, 1))
    const = exact(jnp.broadcast_to(k2, (8, WIDE)), we[...], (1, 1))[0:1, :]
    mix = jnp.where(lax.broadcasted_iota(jnp.int32, (128, LANE), 0) == D, const, mix)
    mix_hi, mix_lo = split(mix)
    mix_all = jnp.concatenate([mix_hi, mix_lo], axis=0)

    @rloop("ig2", BLOCKS)
    def _(b):
        rows = pl.ds(pl.multiple_of(b * CHUNK, CHUNK), CHUNK)
        r = mm(f3[rows, 0:256], mix_all) + mm(f3[rows, 256:384], mix_hi)
        igrad[pl.ds(b * 48, 48)] += r.reshape(48, 8, LANE)

    emit_vector(0, g1)
    emit_vector(1, b1)
    emit(OUT_MISC, reduce_m.finish())
    total_e = reduce_e.finish()
    emit(0, own_wide(s1) * (total_e - f_mean * own_wide(b1) - own_wide(cov_we[...]) * own_wide(inv1 * g1)))

    for s in range(3):
        section(s, 0)
    for item in vectors + [reduce_g, reduce_p, reduce_m, reduce_e]:
        item.close()


def finish_kernel(
    out_in, igrad_in, panel,
    out, igrad, expand, gain1, bias1, depth, gain2, bias2, reduce, b_reduce, excite, b_excite, project, gain3, bias3,
    stage,
):
    for source, target in ((out_in, out), (igrad_in, igrad)):
        for cell in range(CELLS):
            stage[pl.ds(cell, BLOCK, stride=CELLS), :] = source[2 * cell : 2 * cell + 2].reshape(16, LANE)
        for i in range(3):
            target[:, i * LANE : (i + 1) * LANE] = stage[i * LANE : (i + 1) * LANE, :].T[0:D]

    @pl.when(pl.program_id(0) == 0)
    def _():
        expand[...] = panel[0:LANE, :].T[0:OWN, 0:D]
        project[...] = panel[OUT_PROJECT : OUT_PROJECT + LANE, :].T[0:OWN, 0:D]
        for a in range(5):
            depth[a] = panel[OUT_MISC + 5 * a : OUT_MISC + 5 * a + 5, 0:OWN]
        reduce[...] = panel[OUT_MISC + AT_R : OUT_MISC + AT_R + SQZ, 0:OWN]
        excite[...] = panel[OUT_MISC + AT_X : OUT_MISC + AT_X + SQZ, 0:OWN]
        b_excite[...] = panel[OUT_MISC + AT_B : OUT_MISC + AT_B + 1, 0:OWN]
        b_reduce[...] = panel[OUT_MISC + AT_B + 1 : OUT_MISC + AT_B + 2, 0:SQZ]
        for i, ref in enumerate((gain1, bias1, gain2, bias2)):
            ref[...] = panel[OUT_VECS + i : OUT_VECS + i + 1, 0:OWN]
        gain3[...] = panel[OUT_SMALL : OUT_SMALL + 1, 0:D]
        bias3[...] = panel[OUT_SMALL + 1 : OUT_SMALL + 2, 0:D]


def body(
    features, seg_units, w_expand, gain_one, bias_one, w_depth, gain_two, bias_two,
    w_reduce, b_reduce, w_excite, b_excite, w_project, gain_three, bias_three, cotangent,
):
    vm = pl.BlockSpec(memory_space=pltpu.VMEM)
    big = pltpu.VMEM((288, 8, WIDE), F32)
    rows128 = pltpu.VMEM((288, 8, LANE), F32)
    half = pltpu.VMEM((ROWS, WIDE), BF16)

    def f32(*shape):
        return pltpu.VMEM(shape, F32)

    def b16(*shape):
        return pltpu.VMEM(shape, BF16)

    def shape(*dims):
        return jax.ShapeDtypeStruct(dims, F32)

    def row(vector):
        return vector.reshape(1, vector.shape[0])

    dma = pltpu.SemaphoreType.DMA
    slots = [f32(3, 16, 8, GROUP), f32(4, 8, GROUP), f32(8, 8, GROUP), f32(16, 8, GROUP)]
    out, igrad, panel = pl.pallas_call(
        kernel,
        out_shape=(shape(288, 8, LANE), shape(288, 8, LANE), shape(RESULTS, GROUP)),
        in_specs=[vm] * 15 + [pl.BlockSpec(memory_space=pltpu.SMEM)],
        out_specs=(vm,) * 3,
        scratch_shapes=[
            f32(CHUNK, LANE), f32(GROUP, LANE),
            rows128, rows128, rows128, b16(ROWS, 384), b16(256, ROWS), b16(ROWS, 384), b16(256, ROWS),
            big, big, big, big, half, half,
            f32(4, PANEL, GROUP), f32(128, WIDE), f32(128, WIDE), f32(32, WIDE), f32(32, WIDE),
            b16(256, WIDE), b16(BLOCKS, 256, WIDE), f32(TAPS, 8, WIDE), f32(12, 8, WIDE),
            f32(TAPS, 8, WIDE), f32(TAPS, 8, WIDE), f32(CELLS, 8, WIDE), f32(128, WIDE),
            f32(BLOCKS, 8, WIDE), f32(8, WIDE), f32(8, WIDE), f32(8, WIDE), f32(8, LANE), f32(8, LANE),
            f32(3, 16, 8, GROUP), f32(3, 16, 8, GROUP), f32(3, 16, 8, GROUP), f32(8, 16, LANE),
            f32(7, 8, 8, LANE), f32(7, 16, 8, LANE),
            f32(8, 16, LANE), f32(16, 16, LANE), f32(8, 16, LANE),
        ]
        + slots * 3
        + [dma((2, 3)), dma((7, 4)), dma((6,)), dma((3, 8))],
        compiler_params=pltpu.CompilerParams(
            collective_id=0, has_side_effects=True, vmem_limit_bytes=64 * 1024 * 1024 - 65536
        ),
    )(
        features.T, cotangent.T, w_expand.T, w_project, w_reduce.T, w_excite, w_depth,
        row(gain_one), row(bias_one), row(gain_two), row(bias_two), row(b_excite), row(b_reduce), row(gain_three), row(bias_three),
        seg_units,
    )

    def whole(*dims):
        return pl.BlockSpec(dims, lambda b: (0,) * len(dims))

    small = [
        (OWN, D), (1, OWN), (1, OWN), (5, 5, OWN), (1, OWN), (1, OWN),
        (SQZ, OWN), (1, SQZ), (SQZ, OWN), (1, OWN), (OWN, D), (1, D), (1, D),
    ]
    rows_in = pl.BlockSpec((48, 8, LANE), lambda b: (b, 0, 0))
    rows_out = pl.BlockSpec((D, CHUNK), lambda b: (0, b))
    results = pl.pallas_call(
        finish_kernel,
        grid=(BLOCKS,),
        out_shape=(shape(D, ROWS), shape(D, ROWS)) + tuple(shape(*dims) for dims in small),
        in_specs=[rows_in, rows_in, whole(RESULTS, GROUP)],
        out_specs=(rows_out, rows_out) + tuple(whole(*dims) for dims in small),
        scratch_shapes=[f32(CHUNK, LANE)],
    )(out, igrad, panel)
    (out, igrad, expand, gain1, bias1, depth, gain2, bias2, reduce, small_b, excite, b_x, project, gain3, bias3) = results
    return (
        out.T, igrad.T, expand.T, gain1[0], bias1[0], depth, gain2[0], bias2[0],
        reduce.T, small_b[0], excite, b_x[0], project, gain3[0], bias3[0],
    )


def solution(mesh):
    placed = (
        P(("dp", "chan"), None),
        P("dp", None),
        P(None, "chan"),
        P("chan"),
        P("chan"),
        P(None, None, "chan"),
        P("chan"),
        P("chan"),
        P("chan", None),
        P(),
        P(None, "chan"),
        P("chan"),
        P("chan", None),
        P(),
        P(),
        P(("dp", "chan"), None),
    )
    return jax.shard_map(
        body,
        mesh=mesh,
        in_specs=placed,
        out_specs=(
            P(("dp", "chan"), None),
            P(("dp", "chan"), None),
            P(None, "chan"),
            P("chan"),
            P("chan"),
            P(None, None, "chan"),
            P("chan"),
            P("chan"),
            P("chan", None),
            P(),
            P(None, "chan"),
            P("chan"),
            P("chan", None),
            P(),
            P(),
        ),
        check_vma=False,
    )
```

time: 147 us -> 114 us (0.78)
  local copies, waits for them, and re-layouts: 19.7 us -> 0 us
  Pallas kernels: 125 us -> 113 us
  other arithmetic: 1.47 us -> 0 us
    pallas_call x1 -> x2, Pallas kernels: 125 us -> 113 us  [the longest x1 107 us: body(): pl.pallas_call(kernel, out_shape=(shape(288, 8, LANE), shape(288, 8, LANE...]
    unnamed x28 -> x0, local copies, waits for them, and re-layouts: 11.5 us -> none
    squeeze x2 -> x0, local copies, waits for them, and re-layouts: 2.45 us -> none  [the longest x1 1.26 us: body(): little[1]]
    concatenate x1 -> x0, local copies, waits for them, and re-layouts: 2.43 us -> none  [body(): jnp.concatenate([w_expand, w_depth.reshape(TAPS, OWN), jnp.stack([gain_on...]
where the time goes in v2:
time: 114 us
  Pallas kernels  113 us (99%)
    pallas_call x1, Pallas kernels, body(): pl.pallas_call(kernel, out_shape=(shape(288, 8, LANE), shape(288, 8, LANE...  107 us
    pallas_call x1, Pallas kernels, body(): pl.pallas_call(finish_kernel, grid=(BLOCKS,), out_shape=(shape(D, ROWS),...  5.84 us

profile of v2, /device:TPU:1, one launch (start us, length us, event | category | flops | bytes accessed | tf_op | source)
XLA Modules:
  0.0 113.9 jit_solution(2071992568140183466)
XLA Ops:
  0.7 107.4 %shard_map.271 = (f32[288,8,128]{2,1,0:T(8,128)}, f32[288,8,128]{2,1,0:T(8,128)}, f32[400,256]{1,0:T(8,128)}) custom-call(f32[112,2304]{1,0:T(8,128)} %bitcast.24, f32[112,2304]{1,0:T(8,128)} %bitcast.25, f32[168,112]{1,0:T(8,128)} %bitcast.26, f32[168,112]{1,0:T(8,128)} %wp_in.1, f32[28,168]{1,0:T(8,128)} %bitcast.27, f32[28,168]{1,0:T(8,128)} %wx_in.1, ...), custom_call_target="tpu_custom_call" | custom-call | tf_op jit(solution)/shard_map/pallas_call | solution.py:945
  108.0 5.8 %shard_map.272 = (f32[112,2304]{1,0:T(8,128)}, f32[112,2304]{1,0:T(8,128)}, f32[168,112]{1,0:T(8,128)}, f32[1,168]{1,0:T(1,128)}, f32[1,168]{1,0:T(1,128)}, /*in...) custom-call(f32[288,8,128]{2,1,0:T(8,128)} %get-tuple-element.33.out, ...), custom_call_target="tpu_custom_call" | custom-call | tf_op jit(solution)/shard_map/pallas_call | solution.py:982

commit v3 on v2

v3 whole, which is shorter than its diff:
```python
import jax
import jax.numpy as jnp
from jax import lax
from jax.experimental import pallas as pl
from jax.experimental.pallas import tpu as pltpu
from jax.sharding import PartitionSpec as P

MESH = pl.DeviceIdType.MESH
F32 = jnp.float32
BF16 = jnp.bfloat16
EPSILON = 0.001
PRECISE = lax.Precision.HIGHEST
D = 112
SQZ = 28
EXP = 672
H, W, CELLS = 6, 4, 24
TAPS = 25
BLOCK, BLOCKS = 16, 6
ROWS = 2304
CHUNK = BLOCK * CELLS
LANE = 128
WIDE = 768
GROUPS = WIDE // LANE
TOTAL = 294912.0
OWN = 168
REST = OWN - LANE

AT_EXPAND, AT_DEPTH, AT_VECS, AT_PROJECT, AT_REDUCE, AT_EXCITE, PANEL = 0, 112, 137, 144, 256, 288, 320
AT_DD, AT_PLAIN, AT_R, AT_X = TAPS, 2 * TAPS, 3 * TAPS, 3 * TAPS + SQZ
IN_THIRD = 128 - AT_X
OUT_PROJECT, OUT_MISC, OUT_VECS, OUT_SMALL, RESULTS = 128, 256, 384, 392, 400
GROUP = 2 * LANE


REPS = {}


def rep(name):
    count = REPS.get(name, 1)

    def run(fn):
        if count == 1:
            fn()
        else:
            lax.fori_loop(0, count, lambda i, carry: (fn(), carry)[1], 0)

    return run


def rloop(name, size):
    count = REPS.get(name, 1)

    def run(fn):
        if count == 1:
            pl.loop(0, size)(fn)
        else:
            pl.loop(0, size * count)(lambda i: fn(lax.rem(i, size)))

    return run


def split(values):
    high = values.astype(BF16)
    return high, (values - high.astype(F32)).astype(BF16)


def mm(a, b):
    return lax.dot_general(a, b, (((1,), (0,)), ((), ())), preferred_element_type=F32)


def mm_nt(a, b):
    return lax.dot_general(a, b, (((1,), (1,)), ((), ())), preferred_element_type=F32)


def exact(a, b, dims):
    return lax.dot_general(a, b, ((dims[:1], dims[1:]), ((), ())), precision=PRECISE, preferred_element_type=F32)


def pair(values):
    return jnp.concatenate(split(values), axis=0)


def pair_nt(a, b, rows, cols):
    r = mm_nt(a, b)
    return (r[0:rows, 0:cols] + r[rows:, cols:]) + (r[0:rows, cols:] + r[rows:, 0:cols])


def place():
    dp = lax.axis_index("dp")
    z = lax.axis_index("chan")
    return dp // 8, lax.rem(dp // 2, 4), lax.rem(dp, 2), z


def ring(step):
    return min(step, 4 - step)


def column_peers():
    x, y, c, z = place()
    moves = [(dz, dc) for dz in range(4) for dc in range(2) if dz or dc]
    moves.sort(key=lambda m: -10 * ring(m[0]) - m[1])
    base = x * 8 + y * 2
    zs = [lax.rem(z + dz, 4) for dz in range(4)]
    cs = [c, 1 - c]
    return z * 2 + c, [(zs[dz] * 2 + cs[dc], (base + cs[dc], zs[dz])) for dz, dc in moves]


def plane_peers():
    x, y, c, z = place()
    moves = [(dx, dy) for dx in range(4) for dy in range(4) if dx or dy]
    moves.sort(key=lambda m: -ring(m[0]) - ring(m[1]))
    xs = [lax.rem(x + dx, 4) for dx in range(4)]
    ys = [lax.rem(y + dy, 4) for dy in range(4)]
    peers = []
    for dx, dy in moves:
        rank = xs[dx] * 4 + ys[dy]
        peers.append((rank, (rank * 2 + c, z)))
    return x * 4 + y, peers


def push(sources, slots, mine, peers, send, recv):
    for rank, device in peers:
        pltpu.make_async_remote_copy(
            src_ref=sources(rank),
            dst_ref=slots.at[mine],
            send_sem=send,
            recv_sem=recv,
            device_id=device,
            device_id_type=MESH,
        ).start()


def drain(view, sem):
    pltpu.make_async_copy(view, view, sem).wait()


def add_slots(slots, count):
    total = slots[0]
    for k in range(1, count):
        total = total + slots[k]
    return total


class Vector:
    def __init__(self, column, plane, near, far, sems):
        self.column, self.plane, self.near, self.far, self.sems = column, plane, near, far, sems

    def start(self, value):
        mine, peers = self.column
        self.near[mine] = value
        push(lambda rank: self.near.at[mine], self.near, mine, peers, self.sems.at[0], self.sems.at[1])

    def middle(self):
        drain(self.near.at[pl.ds(0, 7)], self.sems.at[1])
        mine, peers = self.plane
        self.far[mine] = add_slots(self.near, 8)
        push(lambda rank: self.far.at[mine], self.far, mine, peers, self.sems.at[2], self.sems.at[3])

    def finish(self):
        drain(self.far.at[pl.ds(0, 15)], self.sems.at[3])
        return add_slots(self.far, 16)

    def close(self):
        drain(self.near.at[pl.ds(0, 7)], self.sems.at[0])
        drain(self.far.at[pl.ds(0, 15)], self.sems.at[2])


class Square:
    def __init__(self, column, plane, source, first, second, third, sems):
        self.column, self.plane = column, plane
        self.source, self.first, self.second, self.third, self.sems = source, first, second, third, sems

    def start(self):
        mine, peers = self.column
        self.first[mine] = self.source[mine]
        push(lambda rank: self.source.at[rank], self.first, mine, peers, self.sems.at[0], self.sems.at[1])

    def middle(self):
        drain(self.first.at[pl.ds(0, 7)], self.sems.at[1])
        mine, peers = self.plane
        self.second[mine] = add_slots(self.first, 8)
        push(lambda rank: self.second.at[mine], self.second, mine, peers, self.sems.at[2], self.sems.at[3])

    def last(self):
        drain(self.second.at[pl.ds(0, 15)], self.sems.at[3])
        mine, peers = self.column
        self.third[mine] = add_slots(self.second, 16)
        push(lambda rank: self.third.at[mine], self.third, mine, peers, self.sems.at[4], self.sems.at[5])

    def finish(self):
        drain(self.third.at[pl.ds(0, 7)], self.sems.at[5])
        return self.third[...].reshape(128, LANE)

    def close(self):
        drain(self.first.at[pl.ds(0, 7)], self.sems.at[0])
        drain(self.second.at[pl.ds(0, 15)], self.sems.at[2])
        drain(self.third.at[pl.ds(0, 7)], self.sems.at[4])


class Panel:
    def __init__(self, column, plane, ranges, source, first, parts, second, third, sems):
        self.column, self.plane, self.ranges = column, plane, ranges
        self.source, self.first, self.parts, self.second, self.third, self.sems = source, first, parts, second, third, sems

    def start(self, index):
        mine, peers = self.plane
        lo, hi = self.ranges[index]
        lanes = pl.ds(lo, hi - lo)
        self.first[mine, :, lo:hi] = self.source[mine, :, lo:hi]
        for rank, device in peers:
            pltpu.make_async_remote_copy(
                src_ref=self.source.at[rank, :, lanes],
                dst_ref=self.first.at[mine, :, lanes],
                send_sem=self.sems.at[0],
                recv_sem=self.sems.at[1 + index],
                device_id=device,
                device_id_type=MESH,
            ).start()

    def scattered(self, index, sem):
        lo, hi = self.ranges[index]
        drain(self.first.at[pl.ds(0, 15), :, pl.ds(lo, hi - lo)], self.sems.at[sem])

    def middle(self):
        for index in range(len(self.ranges)):
            self.scattered(index, 1 + index)
        total = add_slots(self.first, 16)
        mine, peers = self.column
        for z in range(4):
            self.parts[z, :, 0:LANE] = total[:, z * LANE : (z + 1) * LANE]
            rest = 4 + z // 2
            self.parts[z, :, LANE:GROUP] = total[:, rest * LANE : (rest + 1) * LANE]
        self.second[mine] = self.parts[mine // 2]
        push(lambda rank: self.parts.at[rank // 2], self.second, mine, peers, self.sems.at[4], self.sems.at[5])

    def last(self):
        drain(self.second.at[pl.ds(0, 7)], self.sems.at[5])
        mine, peers = self.plane
        self.third[mine] = add_slots(self.second, 8)
        push(lambda rank: self.third.at[mine], self.third, mine, peers, self.sems.at[6], self.sems.at[7])

    def finish(self):
        drain(self.third.at[pl.ds(0, 15)], self.sems.at[7])
        return self.third[...].reshape(128, GROUP)

    def close(self):
        for index in range(len(self.ranges)):
            self.scattered(index, 0)
        drain(self.second.at[pl.ds(0, 7)], self.sems.at[4])
        drain(self.third.at[pl.ds(0, 15)], self.sems.at[6])


def half_gate(values, scale, shift):
    h = values * scale + shift
    return h, jnp.tanh(h)


def slope_of(h, th):
    return (0.5 + 0.5 * th) * (1.0 + (h - h * th))


def sigmoid(v):
    return 1.0 / (1.0 + jnp.exp(-v))


def lanes_of(g):
    return pl.ds(pl.multiple_of(g * LANE, LANE), LANE)


def fold(v):
    return v[0] + v[1]


def row_sum(v):
    return jnp.sum(v, axis=0, keepdims=True)


def row_pairs():
    return [(i, i + a - 2, a) for a in range(5) for i in range(H) if 0 <= i + a - 2 < H]


def nine_weights(w):
    m2, m1, w0, p1, p2 = w
    return [
        w0, p1 - w0, m1 - w0,
        p2 - w0, w0 - p1 - p2, (p1 - m1) + (w0 - p2),
        m2 - w0, (m1 - p1) + (w0 - m2), w0 - m1 - m2,
    ]


def five_taps(g):
    return [
        g[6] - g[7] - g[8],
        (g[2] - g[5]) + (g[7] - g[8]),
        (g[0] - g[1]) - (g[2] + g[3]) + (g[4] + g[5]) - (g[6] - g[7] - g[8]),
        (g[1] - g[4]) + (g[5] - g[7]),
        g[3] - g[4] - g[5],
    ]


def nine_inputs(x):
    x02, x13 = x[0] + x[2], x[1] + x[3]
    return [x02 + x13, x13, x02, x[2] + x[3], x[3], x[2], x[0] + x[1], x[1], x[0]]


def nine_outputs(y):
    y02, y13 = y[0] + y[2], y[1] + y[3]
    return [y02 + y13, y02, y13, y[0] + y[1], y[0], y[1], y[2] + y[3], y[2], y[3]]


def expand_rows(target, expand, cell):
    for i in range(H):
        for m, v in enumerate(expand([cell(i * W + j) for j in range(W)])):
            target[i * 9 + m] = v


def convolve(inputs, outputs, weights, cols):
    for m in range(9):
        x = [inputs[i * 9 + m] for i in range(H)]
        w = [jnp.broadcast_to(weights[a * 9 + m : a * 9 + m + 1, cols], (8, LANE)) for a in range(5)]
        acc = [None] * H
        for i, ii, a in row_pairs():
            term = x[ii] * w[a]
            acc[i] = term if acc[i] is None else acc[i] + term
        for i in range(H):
            outputs[i * 9 + m] = acc[i]


def four_cells(outputs, i):
    m = [outputs[i * 9 + k] for k in range(9)]
    a, b, c, d, e, f = m[0] + m[1], m[0] + m[2], m[3] + m[4], m[3] + m[5], m[6] + m[7], m[6] + m[8]
    return [a + c, b + d, a + e, b + f]


def correlate(target, left, right):
    for m in range(9):
        x = [right[i * 9 + m] for i in range(H)]
        y = [left[i * 9 + m] for i in range(H)]
        acc = [None] * 5
        for i, ii, a in row_pairs():
            term = y[i] * x[ii]
            acc[a] = term if acc[a] is None else acc[a] + term
        for a in range(5):
            target[a * 9 + m] += fold(acc[a])


def row_sums(target, source, cols):
    for t in range(45):
        target[t : t + 1, cols] = row_sum(source[t])


def kernel(
    f_hbm, q_hbm, we_in, wp_in, wr_in, wx_in, wd_in, ga1_in, bi1_in, ga2_in, bi2_in, bx_in, br_in, ga3_in, bi3_in, units,
    out, igrad, o_panel,
    f_in, q_in, copy_sems, stage, wide_stage,
    f_rows, q_rows, p_rows, f3, ft, pg3, qpt, qa,
    e_ref, a1, dv, q2, act_hi, act_lo,
    gathered, we, wp, wr, wx, we_b, ws_b, wp_b, wd, wt, par, tq, td, acc45, cells, cov_we, nine_a, nine_b,
    pool, gates, spread, vec, sums, gp_panel, misc, ge_panel, g_panel,
    near, far, near2, far2,
    g_first, g_second, g_third,
    p_first, p_parts, p_second, p_third,
    m_first, m_parts, m_second, m_third,
    e_first, e_parts, e_second, e_third,
    w_sems, v_sems, g_sems, s_sems,
):
    fetch_f = pltpu.make_async_copy(f_hbm, f_in, copy_sems.at[13])
    fetch_f.start()
    fetch_q = pltpu.make_async_copy(q_hbm, q_in, copy_sems.at[0])
    fetch_q.start()
    x, y, c, z = place()
    column, plane = column_peers(), plane_peers()
    barrier = pltpu.get_barrier_semaphore()
    for _, device in column[1] + plane[1]:
        pl.semaphore_signal(barrier, inc=1, device_id=device, device_id_type=MESH)

    sum2a = Vector(column, plane, near2.at[0], far2.at[0], v_sems.at[0])
    sum2b = Vector(column, plane, near2.at[1], far2.at[1], v_sems.at[1])
    sum3 = Vector(column, plane, near2.at[2], far2.at[2], v_sems.at[2])
    sum4 = Vector(column, plane, near.at[0], far.at[0], v_sems.at[3])
    sum5 = Vector(column, plane, near.at[1], far.at[1], v_sems.at[4])
    vectors = [sum2a, sum2b, sum3, sum4, sum5]
    reduce_g = Square(column, plane, g_panel, g_first, g_second, g_third, g_sems)
    whole = [(0, WIDE)]
    reduce_p = Panel(column, plane, whole, gp_panel, p_first, p_parts, p_second, p_third, s_sems.at[0])
    reduce_m = Panel(column, plane, whole, misc, m_first, m_parts, m_second, m_third, s_sems.at[1])
    early_late = [(0, 2 * GROUP), (2 * GROUP, WIDE)]
    reduce_e = Panel(column, plane, early_late, ge_panel, e_first, e_parts, e_second, e_third, s_sems.at[2])

    fetch_f.wait()

    ones = jnp.where(lax.broadcasted_iota(jnp.int32, (16, ROWS), 0) == 0, 1.0, 0.0)
    hi, lo = split(jnp.concatenate([f_in[...], ones], axis=0))
    ft[0:128, :] = hi
    ft[128:256, :] = lo
    gram = mm_nt(ft[...], ft[...])
    gram = gram[0:128, 0:128] + (gram[0:128, 128:256] + gram[128:256, 0:128]) + gram[128:256, 128:256]
    g_panel[...] = gram.reshape(8, 16, LANE)
    pl.semaphore_wait(barrier, 22)
    reduce_g.start()

    sections = ((0, AT_DEPTH), (AT_DEPTH, AT_PROJECT), (AT_PROJECT, PANEL))
    odd = lax.rem(z, 2) == 1

    across = [(lax.rem(z + k, 4), {"chan": lax.rem(z + k, 4)}) for k in (2, 1, 3)]

    def halves(s):
        lo, hi = sections[s]
        size = (hi - lo) // 2
        return size, pl.ds(pl.multiple_of(lo + c * size, 8), size), pl.ds(lo, size)

    def send_section(s):
        lo, hi = sections[s]
        rest = gathered[z, lo:hi, LANE:GROUP]
        gathered[z, lo:hi, LANE:GROUP] = jnp.where(odd, pltpu.roll(rest, 64, 1), rest)
        size, rows, _ = halves(s)
        for _, device in across:
            pltpu.make_async_remote_copy(
                src_ref=gathered.at[z, rows],
                dst_ref=gathered.at[z, rows],
                send_sem=w_sems.at[0, s],
                recv_sem=w_sems.at[1, s],
                device_id=device,
                device_id_type=MESH,
            ).start()

    def forward_section(s):
        size, rows, some = halves(s)
        drain(gathered.at[pl.ds(0, 3), some], w_sems.at[1, s])
        for other, _ in across:
            pltpu.make_async_remote_copy(
                src_ref=gathered.at[other, rows],
                dst_ref=gathered.at[other, rows],
                send_sem=w_sems.at[0, s],
                recv_sem=w_sems.at[2, s],
                device_id=(x * 8 + y * 2 + 1 - c, z),
                device_id_type=MESH,
            ).start()

    def section(s):
        size, rows, some = halves(s)
        drain(gathered.at[pl.ds(0, 3), some], w_sems.at[2, s])

    def close_section(s):
        size, rows, some = halves(s)
        for _ in range(2):
            drain(gathered.at[pl.ds(0, 3), some], w_sems.at[0, s])

    def assembled(lo, rows):
        parts = [gathered[k, lo : lo + rows, 0:LANE] for k in range(4)]
        for k in (0, 2):
            parts.append(gathered[k, lo : lo + rows, LANE:GROUP] + gathered[k + 1, lo : lo + rows, LANE:GROUP])
        return jnp.concatenate(parts, axis=1)

    gathered[z] = jnp.zeros((PANEL, GROUP), F32)
    wide_stage[...] = jnp.zeros_like(wide_stage)
    wide_stage[0:OWN, 0:D] = we_in[...]
    gathered[z, 0:D, :] = wide_stage[...].T[0:D]
    send_section(0)
    for a in range(5):
        gathered[z, AT_DEPTH + 5 * a : AT_DEPTH + 5 * a + 5, 0:OWN] = wd_in[a]
    for i, row in enumerate((ga1_in, bi1_in, ga2_in, bi2_in, bx_in)):
        gathered[z, AT_VECS + i : AT_VECS + i + 1, 0:OWN] = row[...]
    send_section(1)

    tail = jnp.where(lax.broadcasted_iota(jnp.int32, (16, LANE), 0) == 0, 1.0, 0.0)

    def rows_of(source, tail, target):
        @pl.loop(0, BLOCKS)
        def _(b):
            for i in range(3):
                v = source[:, pl.ds(pl.multiple_of(b * CHUNK + i * LANE, LANE), LANE)]
                stage[i * LANE : (i + 1) * LANE, :] = jnp.concatenate([v, tail], axis=0).T
            for cell in range(CELLS):
                v = stage[pl.ds(cell, BLOCK, stride=CELLS), :]
                target[pl.ds((b * CELLS + cell) * 2, 2)] = v.reshape(2, 8, LANE)

    rows_of(f_in, tail, f_rows)

    @rloop("ft", 18)
    def _(i):
        v = f_rows[pl.ds(i * 16, 16)].reshape(128, LANE)
        rows = pl.ds(pl.multiple_of(i * 128, 128), 128)
        hi, lo = split(v)
        f3[rows, 0:128] = hi
        f3[rows, 128:256] = hi
        f3[rows, 256:384] = lo
        hi, lo = split(v.T)
        ft[0:128, rows] = hi
        ft[128:256, rows] = lo

    def parts_of(source, row):
        @pl.loop(0, 18)
        def _(i):
            hi, lo = split(source[pl.ds(i * 16, 16)].reshape(128, LANE).T)
            rows = pl.ds(pl.multiple_of(i * 128, 128), 128)
            qpt[row : row + 128, rows] = hi
            qpt[256 + row : 384 + row, rows] = lo

    reduce_g.middle()
    fetch_q.wait()
    rows_of(q_in, jnp.zeros((16, LANE), F32), q_rows)
    parts_of(q_rows, 0)
    sums[...] = jnp.zeros_like(sums)
    cells[...] = jnp.zeros_like(cells)
    qa[...] = jnp.zeros_like(qa)

    forward_section(0)
    forward_section(1)
    section(0)
    we[0:D, :] = assembled(0, D)
    we[D:128, :] = jnp.zeros((128 - D, WIDE), F32)
    hi, lo = split(we[...])
    we_b[0:128, :] = hi
    we_b[128:256, :] = lo

    @rloop("E", BLOCKS)
    def _(b):
        @pl.when(b == 3)
        def _():
            reduce_g.last()

        rows = pl.ds(pl.multiple_of(b * CHUNK, CHUNK), CHUNK)
        for n in range(3):
            cols = slice(n * GROUP, (n + 1) * GROUP)
            r = mm(f3[rows, 0:256], we_b[:, cols]) + mm(f3[rows, 256:384], we_b[0:128, cols])
            e_ref[pl.ds(b * 48, 48), :, cols] = r.reshape(48, 8, GROUP)

    section(1)
    taps = assembled(AT_DEPTH, 32)
    for a in range(5):
        row = [taps[5 * a + k : 5 * a + k + 1] for k in range(5)]
        for m, v in enumerate(nine_weights(row)):
            wd[a * 9 + m : a * 9 + m + 1, :] = v
        for m, v in enumerate(nine_weights(row[::-1])):
            wt[(4 - a) * 9 + m : (4 - a) * 9 + m + 1, :] = v
    gain1, bias1, gain2, bias2, bx = [taps[TAPS + i : TAPS + i + 1] for i in range(5)]
    wide_stage[0:OWN, 0:D] = wp_in[...]
    gathered[z, AT_PROJECT : AT_PROJECT + D, :] = wide_stage[...].T[0:D]
    gathered[z, AT_REDUCE : AT_REDUCE + SQZ, 0:OWN] = wr_in[...]
    gathered[z, AT_EXCITE : AT_EXCITE + SQZ, 0:OWN] = wx_in[...]

    gram = reduce_g.finish() * (1.0 / TOTAL)
    send_section(2)
    f_mean_row = gram[D : D + 1, :]
    f_mean = gram[:, D : D + 1]
    cov = gram - f_mean * f_mean_row
    hi, lo = split(cov)
    cov_we[...] = mm(jnp.concatenate([hi, hi], axis=1), we_b[...]) + mm(jnp.concatenate([lo, lo], axis=1), we_b[...])
    mean1 = row_sum(we[...] * f_mean)
    inv1 = lax.rsqrt(row_sum(we[...] * cov_we[...]) + EPSILON)
    s1 = gain1 * inv1
    t1 = bias1 - mean1 * s1

    def put(i, row, lo=0, hi=WIDE):
        par[i, :, lo:hi] = jnp.broadcast_to(row, (8, hi - lo))

    put(0, 0.5 * s1)
    put(1, 0.5 * t1)

    def put_sums(first, second, g, low, size):
        sums[pl.ds(g - low, 1), :] = row_sum(first)
        sums[pl.ds(g - low + size, 1), :] = row_sum(second)

    @rloop("conv1", GROUPS)
    def _(g):
        cols = lanes_of(g)

        def block(b, carry):
            total, square = carry
            base = b * 48
            scale, shift = par[0, :, cols], par[1, :, cols]

            def activate(cell):
                at = pl.ds(base + 2 * cell, 2)
                h, th = half_gate(e_ref[at, :, cols], scale, shift)
                act = h + h * th
                a1[at, :, cols] = act
                return act

            expand_rows(nine_a, nine_inputs, activate)
            convolve(nine_a, nine_b, wd, cols)
            for i in range(H):
                for j, v in enumerate(four_cells(nine_b, i)):
                    dv[pl.ds(base + 2 * (i * W + j), 2), :, cols] = v
                    total = total + fold(v)
                    square = square + fold(v * v)
            return total, square

        zero = jnp.zeros((8, LANE), F32)
        total, square = lax.fori_loop(0, BLOCKS, block, (zero, zero))
        put_sums(total, square, g, jnp.where(g < 3, 0, 3), 3)

        @pl.when(g == 2)
        def _():
            sum2a.start(sums[0:8, :])

        @pl.when(g == 4)
        def _():
            forward_section(2)

        @pl.when(g == 5)
        def _():
            sum2a.middle()
            sum2b.start(sums[0:8, :])

    def wide(rows, first, count):
        return jnp.concatenate([rows[first + g : first + g + 1, :] for g in range(count)], axis=1)

    mean2, inv2 = [None] * 2, [None] * 2

    def second_norm(got, lo, hi):
        count = (hi - lo) // LANE
        mean = wide(got, 0, count) * (1.0 / TOTAL)
        inv = lax.rsqrt(wide(got, count, count) * (1.0 / TOTAL) - mean * mean + EPSILON)
        scale = par[7, 0:1, lo:hi] * inv
        put(2, 0.5 * scale, lo, hi)
        put(3, 0.5 * (par[8, 0:1, lo:hi] - mean * scale), lo, hi)
        put(9, mean, lo, hi)
        put(10, inv, lo, hi)
        put(11, scale, lo, hi)

    put(7, gain2)
    put(8, bias2)

    def one_products(g):
        cols = lanes_of(g)
        acc45[...] = jnp.zeros_like(acc45)

        @pl.loop(0, BLOCKS)
        def _(b):
            def act(cell):
                v = a1[pl.ds(b * 48 + 2 * cell, 2), :, cols]
                cells[cell, :, cols] += fold(v)
                return v

            expand_rows(nine_a, nine_inputs, act)
            expand_rows(nine_b, nine_outputs, lambda cell: dv[pl.ds(b * 48 + 2 * cell, 2), :, cols])
            correlate(acc45, nine_b, nine_a)

        row_sums(td, acc45, cols)

    def one_activation(g):
        cols = lanes_of(g)

        @pl.loop(0, BLOCKS)
        def _(b):
            scale, shift = par[2, :, cols], par[3, :, cols]
            pooled = jnp.zeros((8, LANE), F32)
            for cell in range(CELLS):
                at = pl.ds(b * 48 + 2 * cell, 2)
                h, th = half_gate(dv[at, :, cols], scale, shift)
                q2[at, :, cols] = th
                act = h + h * th
                pooled = pooled + fold(act)
                hi, lo = split(act.reshape(16, LANE))
                rows = pl.ds(b * CHUNK + 16 * cell, 16)
                act_hi[rows, cols] = hi
                act_lo[rows, cols] = lo
            pool[b, :, cols] = pooled

    @pl.loop(0, 12)
    def _(step):
        @pl.when(step == 3)
        def _():
            sum2b.middle()

        @pl.when(step == 5)
        def _():
            second_norm(sum2a.finish(), 0, 3 * LANE)

        @pl.when(step == 9)
        def _():
            second_norm(sum2b.finish(), 3 * LANE, WIDE)

        early = (step < 5) | (step == 8)

        @pl.when(early)
        def _():
            one_products(jnp.where(step == 8, 5, step))

        @pl.when(jnp.logical_not(early))
        def _():
            one_activation(jnp.where(step < 8, step - 5, step - 6))

    section(2)
    wp[0:D, :] = assembled(AT_PROJECT, D)
    wp[D:128, :] = jnp.zeros((128 - D, WIDE), F32)
    hi, lo = split(assembled(AT_REDUCE, 32))
    wr[...] = jnp.concatenate([hi, lo, hi, lo], axis=0)
    hi, lo = split(assembled(AT_EXCITE, 32))
    wx[...] = jnp.concatenate([hi, lo, hi, lo], axis=0)
    seg = lax.broadcasted_iota(jnp.int32, (8, LANE), 0)
    blk = lax.broadcasted_iota(jnp.int32, (8, LANE), 1)
    u0, u1, u2 = units[z, 0], units[z, 1], units[z, 2]
    lower = jnp.where(seg == 0, 0, jnp.where(seg == 1, u0, u0 + u1))
    length = jnp.where(seg == 0, u0, jnp.where(seg == 1, u1, u2))
    member = jnp.where((seg < 3) & (blk >= lower) & (blk < lower + length), 1.0, 0.0)
    per_count = jnp.where(seg < 3, 1.0 / (length * (BLOCK * CELLS)).astype(F32), 0.0)[:, 0:1]
    live = jnp.where(seg < 3, 1.0, 0.0)[:, 0:1]

    vec[...] = jnp.zeros((8, LANE), F32)
    vec[0:1, 0:SQZ] = br_in[...]
    pooled = jnp.zeros((8, WIDE), F32)
    for b in range(BLOCKS):
        pooled = pooled + member[:, b : b + 1] * row_sum(pool[b])
    plain_sums = pooled
    pooled = pooled * per_count
    pooled_pair = pair(pooled)
    reduced = pair_nt(pooled_pair, wr[0:64, :], 8, 32) + vec[0:1, 0:32]
    sig_r = sigmoid(reduced)
    squeezed = reduced * sig_r * live

    def quad(values):
        hi, lo = split(values)
        return jnp.concatenate([hi, hi, lo, lo], axis=1)

    gate = sigmoid(mm(quad(squeezed), wx[...]) + bx)

    def of_blocks(rows, b):
        return row_sum(member[:, b : b + 1] * rows)

    for b in range(BLOCKS):
        gates[b : b + 1, :] = of_blocks(gate, b)

    def project(b, carry):
        rows = pl.ds(pl.multiple_of(b * CHUNK, CHUNK), CHUNK)
        hi, lo = split(wp[...] * gates[pl.ds(b, 1), :])
        wp_b[b, 0:128, :] = hi
        wp_b[b, 128:256, :] = lo
        r = mm_nt(act_hi[rows, :], wp_b[b])
        r = r[:, 0:128] + r[:, 128:256] + mm_nt(act_lo[rows, :], wp_b[b, 0:128, :])
        r = r.reshape(48, 8, LANE)
        q = q_rows[pl.ds(b * 48, 48)]
        p_rows[pl.ds(b * 48, 48)] = r
        return tuple(old + jnp.sum(new, axis=0) for old, new in zip(carry, (r, r * r, q, q * r)))

    zero = jnp.zeros((8, LANE), F32)
    four = lax.fori_loop(0, BLOCKS * REPS.get("proj", 1), lambda i, v: project(lax.rem(i, BLOCKS), v), (zero,) * 4)
    for i in range(4):
        vec[i : i + 1, :] = row_sum(four[i])
    sum3.start(vec[...])

    parts_of(p_rows, 128)

    @rloop("qa", BLOCKS)
    def _(b):
        rows = pl.ds(pl.multiple_of(b * CHUNK, CHUNK), CHUNK)
        inside = [jnp.where((b >= low) & (b < high), 1.0, 0.0) for low, high in ((0, u0), (u0, u0 + u1), (u0 + u1, 6))]
        for n in range(3):
            cols = slice(n * GROUP, (n + 1) * GROUP)
            m = mm(qpt[:, rows], act_hi[rows, cols])
            m = m[0:256] + m[256:512] + mm(qpt[0:256, rows], act_lo[rows, cols])
            for k in range(3):
                qa[k, :, cols] += m * inside[k]

        @pl.when(b == 3)
        def _():
            sum3.middle()

    @rloop("slope2", GROUPS)
    def _(g):
        cols = lanes_of(g)

        @pl.loop(0, BLOCKS)
        def _(b):
            scale, shift = par[2, :, cols], par[3, :, cols]
            for cell in range(CELLS):
                at = pl.ds(b * 48 + 2 * cell, 2)
                q2[at, :, cols] = slope_of(dv[at, :, cols] * scale + shift, q2[at, :, cols])

    got = sum3.finish() * (1.0 / TOTAL)
    vec[...] = jnp.zeros((8, LANE), F32)
    vec[0:1, 0:D] = ga3_in[...]
    vec[1:2, 0:D] = bi3_in[...]
    gain3, bias3 = vec[0:1, :], vec[1:2, :]
    mean3 = got[0:1]
    inv3 = lax.rsqrt(got[1:2] - mean3 * mean3 + EPSILON)
    b3 = got[2:3]
    g3 = (got[3:4] - mean3 * got[2:3]) * inv3
    o_panel[OUT_SMALL : OUT_SMALL + 1, 0:LANE] = g3 * TOTAL
    o_panel[OUT_SMALL + 1 : OUT_SMALL + 2, 0:LANE] = b3 * TOTAL
    s3 = gain3 * inv3
    t3 = bias3 - mean3 * s3
    pg_p = -s3 * inv3 * g3
    pg_0 = -s3 * b3 - pg_p * mean3

    columns = jnp.concatenate([s3, pg_p, pg_0, jnp.zeros((5, LANE), F32)], axis=0).T
    by_q, by_p, by_1 = columns[:, 0:1], columns[:, 1:2], columns[:, 2:3]
    base = row_sum(wp[...] * by_1)
    w_q, w_p = wp[...] * by_q, wp[...] * by_p
    gate_grad = jnp.concatenate(
        [row_sum(w_q * qa[k, 0:128] + w_p * qa[k, 128:256]) + base * plain_sums[k : k + 1] for k in range(3)]
        + [jnp.zeros((5, WIDE), F32)],
        axis=0,
    )
    excite_in = gate_grad * gate * (1.0 - gate)
    reduced_grad = pair_nt(pair(excite_in), wx[0:64, :], 8, 32) * (sig_r * (1.0 + reduced * (1.0 - sig_r))) * live
    pooled_grad = mm(quad(reduced_grad), wr[...]) * per_count
    for b in range(BLOCKS):
        spread[b : b + 1, :] = of_blocks(pooled_grad, b)

    @rloop("pgs", BLOCKS)
    def _(b):
        at = pl.ds(b * 48, 48)
        hi, lo = split((q_rows[at] * s3 + (p_rows[at] * pg_p + pg_0)).reshape(CHUNK, LANE))
        rows = pl.ds(pl.multiple_of(b * CHUNK, CHUNK), CHUNK)
        pg3[rows, 0:128] = hi
        pg3[rows, 128:256] = hi
        pg3[rows, 256:384] = lo

    @rloop("a2g", 3)
    def _(n):
        cols = pl.ds(pl.multiple_of(n * GROUP, GROUP), GROUP)

        def block(b, carry):
            rows = pl.ds(pl.multiple_of(b * CHUNK, CHUNK), CHUNK)
            at = pl.ds(b * 48, 48)
            r = mm(pg3[rows, 0:256], wp_b[b, :, cols]) + mm(pg3[rows, 256:384], wp_b[b, 0:128, cols])
            r = (r.reshape(48, 8, GROUP) + spread[pl.ds(b, 1), cols]) * q2[at, :, cols]
            q2[at, :, cols] = r
            return carry[0] + jnp.sum(r, axis=0), carry[1] + jnp.sum(r * dv[at, :, cols], axis=0)

        zero = jnp.zeros((8, GROUP), F32)
        total, product = lax.fori_loop(0, BLOCKS, block, (zero, zero))
        for half in range(2):
            lanes = slice(half * LANE, (half + 1) * LANE)
            put_sums(total[:, lanes], product[:, lanes], n * 2 + half, 0, 8)

    sum4.start(sums[...])

    gp = jnp.zeros((128, WIDE), F32)
    for k in range(3):
        gp = gp + gate[k : k + 1] * (by_q * qa[k, 0:128] + by_p * qa[k, 128:256] + by_1 * plain_sums[k : k + 1])
    gp_panel[...] = gp.reshape(16, 8, WIDE)
    g_excite = exact(squeezed, excite_in, (0, 0))
    gp_panel[14, 0:1, :] = row_sum(excite_in)
    gp_panel[15, 0:1, :] = jnp.zeros((1, WIDE), F32)
    for k in range(4):
        gp_panel[15, 0:1, k * LANE : k * LANE + 32] = row_sum(reduced_grad)
    for i in range(IN_THIRD, SQZ):
        gp_panel[14, 1 + i - IN_THIRD : 2 + i - IN_THIRD, :] = g_excite[i : i + 1]
    reduce_p.start(0)

    def put_misc(row, values):
        for i in range(values.shape[0]):
            misc[(row + i) // 8, (row + i) % 8 : (row + i) % 8 + 1, :] = values[i : i + 1]

    put_misc(AT_R, exact(reduced_grad, pooled, (0, 0))[0:SQZ])
    put_misc(AT_X, g_excite[0:IN_THIRD])

    @rloop("tq", GROUPS)
    def _(g):
        cols = lanes_of(g)
        acc45[...] = jnp.zeros_like(acc45)

        @pl.loop(0, BLOCKS)
        def _(b):
            expand_rows(nine_a, nine_inputs, lambda cell: a1[pl.ds(b * 48 + 2 * cell, 2), :, cols])
            expand_rows(nine_b, nine_outputs, lambda cell: q2[pl.ds(b * 48 + 2 * cell, 2), :, cols])
            correlate(acc45, nine_b, nine_a)
            scale, shift = par[0, :, cols], par[1, :, cols]
            for cell in range(CELLS):
                at = pl.ds(b * 48 + 2 * cell, 2)
                e_ref[at, :, cols] = slope_of(*half_gate(e_ref[at, :, cols], scale, shift))

        row_sums(tq, acc45, cols)

        @pl.when(g == 2)
        def _():
            sum4.middle()

        @pl.when(g == 4)
        def _():
            reduce_p.middle()

    def own_lanes(rows):
        first = rows[:, 0:LANE]
        rest = rows[:, LANE:GROUP]
        return first, jnp.where(odd, pltpu.roll(rest, 64, 1), rest)

    def own_wide(rows):
        first = jnp.zeros((rows.shape[0], LANE), F32)
        rest = jnp.zeros((rows.shape[0], LANE), F32)
        for k in range(4):
            first = jnp.where(z == k, rows[:, k * LANE : (k + 1) * LANE], first)
        for k in range(2):
            rest = jnp.where(z // 2 == k, rows[:, (4 + k) * LANE : (5 + k) * LANE], rest)
        return jnp.concatenate([first, rest], axis=1)

    def emit(row, values):
        first, rest = own_lanes(values)
        o_panel[row : row + values.shape[0], 0:LANE] = first
        o_panel[row : row + values.shape[0], LANE:GROUP] = rest

    def emit_vector(i, row):
        emit(OUT_VECS + i, own_wide(row))

    for t in range(TAPS):
        a, k = t // 5, t % 5
        plain = None
        for i in range(H):
            for j in range(W):
                ii, jj = i + a - 2, j + k - 2
                if 0 <= ii < H and 0 <= jj < W:
                    v = cells[ii * W + jj]
                    plain = v if plain is None else plain + v
        put_misc(AT_PLAIN + t, row_sum(plain))
    for first, source in ((0, tq), (AT_DD, td)):
        for a in range(5):
            for k, v in enumerate(five_taps([source[a * 9 + m : a * 9 + m + 1, :] for m in range(9)])):
                put_misc(first + 5 * a + k, v)
    reduce_m.start(0)

    got = sum4.finish()
    mean2, inv2, s2 = [par[i, 0:1, :] for i in (9, 10, 11)]
    b2 = wide(got, 0, GROUPS)
    g2 = (wide(got, 8, GROUPS) - mean2 * b2) * inv2
    c3 = -s2 * inv2 * g2 * (1.0 / TOTAL)
    c2 = -s2 * b2 * (1.0 / TOTAL) - c3 * mean2
    put(4, s2)
    put(5, c2)
    put(6, c3)
    emit_vector(2, g2)
    emit_vector(3, b2)

    @rloop("conv2", GROUPS)
    def _(g):
        @pl.when(g == 1)
        def _():
            reduce_p.last()

        @pl.when(g == 4)
        def _():
            reduce_m.middle()

        cols = lanes_of(g)

        @pl.loop(0, BLOCKS)
        def _(b):
            base = b * 48
            k1, k2, k3 = par[4, :, cols], par[5, :, cols], par[6, :, cols]

            def grad(cell):
                at = pl.ds(base + 2 * cell, 2)
                return q2[at, :, cols] * k1 + (dv[at, :, cols] * k3 + k2)

            expand_rows(nine_a, nine_inputs, grad)
            convolve(nine_a, nine_b, wt, cols)
            for i in range(H):
                for j, v in enumerate(four_cells(nine_b, i)):
                    at = pl.ds(base + 2 * (i * W + j), 2)
                    hi, lo = split((v * e_ref[at, :, cols]).reshape(16, LANE))
                    rows = pl.ds(b * CHUNK + 16 * (i * W + j), 16)
                    act_hi[rows, cols] = hi
                    act_lo[rows, cols] = lo

        @pl.when(lax.rem(g, 2) == 1)
        def _():
            n = g // 2
            cols = pl.ds(pl.multiple_of(n * GROUP, GROUP), GROUP)
            m = mm(ft[...], act_hi[:, cols])
            m = m[0:128] + m[128:256] + mm(ft[0:128, :], act_lo[:, cols])
            ge_panel[:, :, cols] = m.reshape(16, 8, GROUP)
            product = row_sum(m * we[:, cols])
            for half in range(2):
                lanes = slice(half * LANE, (half + 1) * LANE)
                sums[pl.ds(g - 1 + half, 1), :] = m[D : D + 1, lanes]
                sums[pl.ds(g + 7 + half, 1), :] = product[:, lanes]

            @pl.when(g == 3)
            def _():
                reduce_e.start(0)

    reduce_e.start(1)
    sum5.start(sums[...])

    hi, lo = split(we[...] * s1)
    ws_b[0:128, :] = hi
    ws_b[128:256, :] = lo

    @rloop("ig", BLOCKS)
    def _(b):
        rows = pl.ds(pl.multiple_of(b * CHUNK, CHUNK), CHUNK)
        at = pl.ds(b * 48, 48)
        r = mm_nt(act_hi[rows, :], ws_b[...])
        r = r[:, 0:128] + r[:, 128:256] + mm_nt(act_lo[rows, :], ws_b[0:128, :])
        q_rows[at] += r.reshape(48, 8, LANE)

    sum5.middle()

    def write(target, b, rows_of_cell):
        for cell in range(CELLS):
            stage[pl.ds(cell, BLOCK, stride=CELLS), :] = rows_of_cell(pl.ds(b * 48 + 2 * cell, 2)).reshape(16, LANE)
        for i in range(3):
            at = pl.ds(pl.multiple_of(b * CHUNK + i * LANE, LANE), LANE)
            target[:, at] = stage[i * LANE : (i + 1) * LANE, :].T[0:D]

    def store(source, target, sem, b):
        at = pl.ds(pl.multiple_of(b * CHUNK, CHUNK), CHUNK)
        return pltpu.make_async_copy(source.at[:, at], target.at[:, at], sem)

    @rloop("out", BLOCKS)
    def _(b):
        write(f_in, b, lambda at: f_rows[at] + (p_rows[at] * s3 + t3))
        store(f_in, out, copy_sems.at[1 + b], b).start()

    reduce_e.middle()
    reduce_m.last()
    emit(OUT_PROJECT, reduce_p.finish())
    got = sum5.finish()
    b1 = wide(got, 0, GROUPS)
    g1 = (wide(got, 8, GROUPS) - mean1 * b1) * inv1
    k3 = -s1 * inv1 * g1 * (1.0 / TOTAL)
    k2 = -s1 * b1 * (1.0 / TOTAL) - k3 * mean1
    reduce_e.last()
    left = jnp.where(lax.broadcasted_iota(jnp.int32, (128, WIDE), 0) == D, k2, we[...] * k3)
    mix = pair_nt(pair(left), we_b[...], 128, 128)
    mix_hi, mix_lo = split(mix)
    mix_all = jnp.concatenate([mix_hi, mix_lo], axis=0)

    @rloop("ig2", BLOCKS)
    def _(b):
        rows = pl.ds(pl.multiple_of(b * CHUNK, CHUNK), CHUNK)
        r = mm(f3[rows, 0:256], mix_all) + mm(f3[rows, 256:384], mix_hi)
        q_rows[pl.ds(b * 48, 48)] += r.reshape(48, 8, LANE)
        write(q_in, b, lambda at: q_rows[at])
        store(q_in, igrad, copy_sems.at[7 + b], b).start()

    emit_vector(0, g1)
    emit_vector(1, b1)
    total_m = reduce_m.finish()
    emit(OUT_MISC, total_m)
    by = [own_wide(v) for v in (s2, c2, c3)]
    taps_grad = total_m[0:TAPS] * by[0] + total_m[AT_DD : AT_DD + TAPS] * by[2] + total_m[AT_PLAIN : AT_PLAIN + TAPS] * by[1]
    emit(OUT_MISC, taps_grad)
    total_e = reduce_e.finish()
    emit(0, own_wide(s1) * (total_e - f_mean * own_wide(b1) - own_wide(cov_we[...]) * own_wide(inv1 * g1)))

    for b in range(BLOCKS):
        store(f_in, out, copy_sems.at[1 + b], b).wait()
        store(q_in, igrad, copy_sems.at[7 + b], b).wait()
    for s in range(3):
        close_section(s)
    for item in vectors + [reduce_g, reduce_p, reduce_m, reduce_e]:
        item.close()


def finish_kernel(
    out_in, igrad_in, panel,
    out, igrad, expand, gain1, bias1, depth, gain2, bias2, reduce, b_reduce, excite, b_excite, project, gain3, bias3,
    held, sems,
):
    pieces = []
    for i in range(6):
        source, target = ((out_in, out), (igrad_in, igrad))[i // 3]
        at = pl.ds((i % 3) * (ROWS // 3), ROWS // 3)
        pieces.append((
            pltpu.make_async_copy(source.at[:, at], held.at[i], sems.at[0, i]),
            pltpu.make_async_copy(held.at[i], target.at[:, at], sems.at[1, i]),
        ))
    for arrive, _ in pieces:
        arrive.start()
    expand[...] = panel[0:LANE, :].T[0:OWN, 0:D]
    project[...] = panel[OUT_PROJECT : OUT_PROJECT + LANE, :].T[0:OWN, 0:D]
    for arrive, leave in pieces:
        arrive.wait()
        leave.start()
    for a in range(5):
        depth[a] = panel[OUT_MISC + 5 * a : OUT_MISC + 5 * a + 5, 0:OWN]
    reduce[...] = panel[OUT_MISC + AT_R : OUT_MISC + AT_R + SQZ, 0:OWN]
    excite[0:IN_THIRD, :] = panel[OUT_MISC + AT_X : OUT_MISC + 128, 0:OWN]
    excite[IN_THIRD:SQZ, :] = panel[OUT_PROJECT + D + 1 : OUT_PROJECT + D + 1 + SQZ - IN_THIRD, 0:OWN]
    b_excite[...] = panel[OUT_PROJECT + D : OUT_PROJECT + D + 1, 0:OWN]
    b_reduce[...] = panel[OUT_PROJECT + D + 8 : OUT_PROJECT + D + 9, 0:SQZ]
    for i, ref in enumerate((gain1, bias1, gain2, bias2)):
        ref[...] = panel[OUT_VECS + i : OUT_VECS + i + 1, 0:OWN]
    gain3[...] = panel[OUT_SMALL : OUT_SMALL + 1, 0:D]
    bias3[...] = panel[OUT_SMALL + 1 : OUT_SMALL + 2, 0:D]
    for _, leave in pieces:
        leave.wait()


def body(
    features, seg_units, w_expand, gain_one, bias_one, w_depth, gain_two, bias_two,
    w_reduce, b_reduce, w_excite, b_excite, w_project, gain_three, bias_three, cotangent,
):
    vm = pl.BlockSpec(memory_space=pltpu.VMEM)
    anywhere = pl.BlockSpec(memory_space=pl.ANY)
    big = pltpu.VMEM((288, 8, WIDE), F32)
    rows128 = pltpu.VMEM((288, 8, LANE), F32)
    half = pltpu.VMEM((ROWS, WIDE), BF16)

    def f32(*shape):
        return pltpu.VMEM(shape, F32)

    def b16(*shape):
        return pltpu.VMEM(shape, BF16)

    def shape(*dims):
        return jax.ShapeDtypeStruct(dims, F32)

    def row(vector):
        return vector.reshape(1, vector.shape[0])

    dma = pltpu.SemaphoreType.DMA
    slots = [f32(16, 8, WIDE), f32(4, 8, GROUP), f32(8, 8, GROUP), f32(16, 8, GROUP)]
    out, igrad, panel = pl.pallas_call(
        kernel,
        out_shape=(shape(D, ROWS), shape(D, ROWS), shape(RESULTS, GROUP)),
        in_specs=[anywhere, anywhere] + [vm] * 13 + [pl.BlockSpec(memory_space=pltpu.SMEM)],
        out_specs=(anywhere, anywhere, vm),
        scratch_shapes=[
            f32(D, ROWS), f32(D, ROWS), dma((14,)), f32(CHUNK, LANE), f32(GROUP, LANE),
            rows128, rows128, rows128, b16(ROWS, 384), b16(256, ROWS), b16(ROWS, 384), b16(512, ROWS), f32(3, 256, WIDE),
            big, big, big, big, half, half,
            f32(4, PANEL, GROUP), f32(128, WIDE), f32(128, WIDE), b16(128, WIDE), b16(128, WIDE),
            b16(256, WIDE), b16(256, WIDE), b16(BLOCKS, 256, WIDE), f32(48, WIDE), f32(48, WIDE), f32(12, 8, WIDE),
            f32(48, WIDE), f32(48, WIDE), f32(45, 8, LANE), f32(CELLS, 8, WIDE), f32(128, WIDE), f32(54, 2, 8, LANE), f32(54, 2, 8, LANE),
            f32(BLOCKS, 8, WIDE), f32(8, WIDE), f32(8, WIDE), f32(8, LANE), f32(16, LANE),
            f32(16, 8, WIDE), f32(16, 8, WIDE), f32(16, 8, WIDE), f32(8, 16, LANE),
            f32(2, 8, 16, LANE), f32(2, 16, 16, LANE), f32(3, 8, 8, LANE), f32(3, 16, 8, LANE),
            f32(8, 16, LANE), f32(16, 16, LANE), f32(8, 16, LANE),
        ]
        + slots * 3
        + [dma((3, 3)), dma((5, 4)), dma((6,)), dma((3, 8))],
        compiler_params=pltpu.CompilerParams(
            collective_id=0, has_side_effects=True, vmem_limit_bytes=64 * 1024 * 1024 - 65536
        ),
    )(
        features.T, cotangent.T, w_expand.T, w_project, w_reduce.T, w_excite, w_depth,
        row(gain_one), row(bias_one), row(gain_two), row(bias_two), row(b_excite), row(b_reduce), row(gain_three), row(bias_three),
        seg_units,
    )

    small = [
        (OWN, D), (1, OWN), (1, OWN), (5, 5, OWN), (1, OWN), (1, OWN),
        (SQZ, OWN), (1, SQZ), (SQZ, OWN), (1, OWN), (OWN, D), (1, D), (1, D),
    ]
    results = pl.pallas_call(
        finish_kernel,
        out_shape=(shape(D, ROWS), shape(D, ROWS)) + tuple(shape(*dims) for dims in small),
        in_specs=[anywhere, anywhere, vm],
        out_specs=(anywhere, anywhere) + (vm,) * 13,
        scratch_shapes=[f32(6, D, ROWS // 3), dma((2, 6))],
    )(out, igrad, panel)
    (out, igrad, expand, gain1, bias1, depth, gain2, bias2, reduce, small_b, excite, b_x, project, gain3, bias3) = results
    return (
        out.T, igrad.T, expand.T, gain1[0], bias1[0], depth, gain2[0], bias2[0],
        reduce.T, small_b[0], excite, b_x[0], project, gain3[0], bias3[0],
    )


def solution(mesh):
    placed = (
        P(("dp", "chan"), None),
        P("dp", None),
        P(None, "chan"),
        P("chan"),
        P("chan"),
        P(None, None, "chan"),
        P("chan"),
        P("chan"),
        P("chan", None),
        P(),
        P(None, "chan"),
        P("chan"),
        P("chan", None),
        P(),
        P(),
        P(("dp", "chan"), None),
    )
    return jax.shard_map(
        body,
        mesh=mesh,
        in_specs=placed,
        out_specs=(
            P(("dp", "chan"), None),
            P(("dp", "chan"), None),
            P(None, "chan"),
            P("chan"),
            P("chan"),
            P(None, None, "chan"),
            P("chan"),
            P("chan"),
            P("chan", None),
            P(),
            P(None, "chan"),
            P("chan"),
            P("chan", None),
            P(),
            P(),
        ),
        check_vma=False,
    )
```

time: 114 us -> 101 us (0.89)
  Pallas kernels: 113 us -> 100 us
    pallas_call x2, Pallas kernels: 113 us -> 100 us  [the longest x1 95.9 us: body(): pl.pallas_call(kernel, out_shape=(shape(D, ROWS), shape(D, ROWS), shape(R...]
where the time goes in v3:
time: 101 us
  Pallas kernels  100 us (99%)
    pallas_call x1, Pallas kernels, body(): pl.pallas_call(kernel, out_shape=(shape(D, ROWS), shape(D, ROWS), shape(R...  95.9 us
    pallas_call x1, Pallas kernels, body(): pl.pallas_call(finish_kernel, out_shape=(shape(D, ROWS), shape(D, ROWS))...  4.12 us

profile of v3, /device:TPU:1, one launch (start us, length us, event | category | flops | bytes accessed | tf_op | source)
XLA Modules:
  0.0 100.7 jit_solution(302303942779248466)
XLA Ops:
  0.7 95.9 %shard_map.271 = (f32[112,2304]{1,0:T(8,128)}, f32[112,2304]{1,0:T(8,128)}, f32[400,256]{1,0:T(8,128)}) custom-call(f32[112,2304]{1,0:T(8,128)} %bitcast.24, f32[112,2304]{1,0:T(8,128)} %bitcast.25, f32[168,112]{1,0:T(8,128)} %bitcast.26, f32[168,112]{1,0:T(8,128)} %wp_in.1, f32[28,168]{1,0:T(8,128)} %bitcast.27, f32[28,168]{1,0:T(8,128)} %wx_in.1, ...), custom_call_target="tpu_custom_call" | custom-call | tf_op jit(solution)/shard_map/pallas_call | solution.py:1108
  96.6 4.1 %shard_map.272 = (f32[112,2304]{1,0:T(8,128)}, f32[112,2304]{1,0:T(8,128)}, f32[168,112]{1,0:T(8,128)}, f32[1,168]{1,0:T(1,128)}, f32[1,168]{1,0:T(1,128)}, /*in...) custom-call(f32[112,2304]{1,0:T(8,128)} %get-tuple-element.33.out_in, ...), custom_call_target="tpu_custom_call" | custom-call | tf_op jit(solution)/shard_map/pallas_call | solution.py:1140

commit v4 on v3

--- a/solution.py
+++ b/solution.py
@@ -243,9 +243,11 @@
         drain(self.third.at[pl.ds(0, 15)], self.sems.at[7])
         return self.third[...].reshape(128, GROUP)
 
-    def close(self):
+    def sent(self):
         for index in range(len(self.ranges)):
             self.scattered(index, 0)
+
+    def close(self):
         drain(self.second.at[pl.ds(0, 7)], self.sems.at[4])
         drain(self.third.at[pl.ds(0, 15)], self.sems.at[6])
 
@@ -351,12 +353,12 @@
 
 def kernel(
     f_hbm, q_hbm, we_in, wp_in, wr_in, wx_in, wd_in, ga1_in, bi1_in, ga2_in, bi2_in, bx_in, br_in, ga3_in, bi3_in, units,
-    out, igrad, o_panel,
-    f_in, q_in, copy_sems, stage, wide_stage,
+    f_in, q_in, o_panel,
+    copy_sems, stage, wide_stage,
     f_rows, q_rows, p_rows, f3, ft, pg3, qpt, qa,
     e_ref, a1, dv, q2, act_hi, act_lo,
-    gathered, we, wp, wr, wx, we_b, ws_b, wp_b, wd, wt, par, tq, td, acc45, cells, cov_we, nine_a, nine_b,
-    pool, gates, spread, vec, sums, gp_panel, misc, ge_panel, g_panel,
+    gathered, we, wp, wr, wx, we_b, ws_b, wp_b, wd, wt, par, tq, td, acc45, acc24, cells, cov_we, nine_a, nine_b,
+    pool, gates, spread, vec, sums, gp_panel, misc, g_panel,
     near, far, near2, far2,
     g_first, g_second, g_third,
     p_first, p_parts, p_second, p_third,
@@ -364,7 +366,7 @@
     e_first, e_parts, e_second, e_third,
     w_sems, v_sems, g_sems, s_sems,
 ):
-    fetch_f = pltpu.make_async_copy(f_hbm, f_in, copy_sems.at[13])
+    fetch_f = pltpu.make_async_copy(f_hbm, f_in, copy_sems.at[1])
     fetch_f.start()
     fetch_q = pltpu.make_async_copy(q_hbm, q_in, copy_sems.at[0])
     fetch_q.start()
@@ -385,7 +387,7 @@
     reduce_p = Panel(column, plane, whole, gp_panel, p_first, p_parts, p_second, p_third, s_sems.at[0])
     reduce_m = Panel(column, plane, whole, misc, m_first, m_parts, m_second, m_third, s_sems.at[1])
     early_late = [(0, 2 * GROUP), (2 * GROUP, WIDE)]
-    reduce_e = Panel(column, plane, early_late, ge_panel, e_first, e_parts, e_second, e_third, s_sems.at[2])
+    reduce_e = Panel(column, plane, early_late, gp_panel, e_first, e_parts, e_second, e_third, s_sems.at[2])
 
     fetch_f.wait()
 
@@ -502,7 +504,6 @@
     rows_of(q_in, jnp.zeros((16, LANE), F32), q_rows)
     parts_of(q_rows, 0)
     sums[...] = jnp.zeros_like(sums)
-    cells[...] = jnp.zeros_like(cells)
     qa[...] = jnp.zeros_like(qa)
 
     forward_section(0)
@@ -626,12 +627,13 @@
     def one_products(g):
         cols = lanes_of(g)
         acc45[...] = jnp.zeros_like(acc45)
+        acc24[...] = jnp.zeros_like(acc24)
 
         @pl.loop(0, BLOCKS)
         def _(b):
             def act(cell):
                 v = a1[pl.ds(b * 48 + 2 * cell, 2), :, cols]
-                cells[cell, :, cols] += fold(v)
+                acc24[cell] += fold(v)
                 return v
 
             expand_rows(nine_a, nine_inputs, act)
@@ -639,6 +641,8 @@
             correlate(acc45, nine_b, nine_a)
 
         row_sums(td, acc45, cols)
+        for cell in range(CELLS):
+            cells[cell : cell + 1, cols] = row_sum(acc24[cell])
 
     def one_activation(g):
         cols = lanes_of(g)
@@ -724,8 +728,8 @@
         gates[b : b + 1, :] = of_blocks(gate, b)
 
     def project(b, carry):
-        rows = pl.ds(pl.multiple_of(b * CHUNK, CHUNK), CHUNK)
-        hi, lo = split(wp[...] * gates[pl.ds(b, 1), :])
+        rows = slice(b * CHUNK, (b + 1) * CHUNK)
+        hi, lo = split(wp[...] * gates[b : b + 1, :])
         wp_b[b, 0:128, :] = hi
         wp_b[b, 128:256, :] = lo
         r = mm_nt(act_hi[rows, :], wp_b[b])
@@ -736,25 +740,26 @@
         return tuple(old + jnp.sum(new, axis=0) for old, new in zip(carry, (r, r * r, q, q * r)))
 
     zero = jnp.zeros((8, LANE), F32)
-    four = lax.fori_loop(0, BLOCKS * REPS.get("proj", 1), lambda i, v: project(lax.rem(i, BLOCKS), v), (zero,) * 4)
+    four = (zero,) * 4
+    for b in range(BLOCKS):
+        four = project(b, four)
     for i in range(4):
         vec[i : i + 1, :] = row_sum(four[i])
     sum3.start(vec[...])
 
     parts_of(p_rows, 128)
 
-    @rloop("qa", BLOCKS)
-    def _(b):
-        rows = pl.ds(pl.multiple_of(b * CHUNK, CHUNK), CHUNK)
-        inside = [jnp.where((b >= low) & (b < high), 1.0, 0.0) for low, high in ((0, u0), (u0, u0 + u1), (u0 + u1, 6))]
-        for n in range(3):
-            cols = slice(n * GROUP, (n + 1) * GROUP)
-            m = mm(qpt[:, rows], act_hi[rows, cols])
-            m = m[0:256] + m[256:512] + mm(qpt[0:256, rows], act_lo[rows, cols])
+    @rloop("qa", 3)
+    def _(i):
+        for b in (2 * i, 2 * i + 1):
+            rows = pl.ds(pl.multiple_of(b * CHUNK, CHUNK), CHUNK)
+            inside = [jnp.where((b >= low) & (b < high), 1.0, 0.0) for low, high in ((0, u0), (u0, u0 + u1), (u0 + u1, 6))]
+            m = mm(qpt[:, rows], act_hi[rows, :])
+            m = m[0:256] + m[256:512] + mm(qpt[0:256, rows], act_lo[rows, :])
             for k in range(3):
-                qa[k, :, cols] += m * inside[k]
-
-        @pl.when(b == 3)
+                qa[k] += m * inside[k]
+
+        @pl.when(i == 1)
         def _():
             sum3.middle()
 
@@ -809,24 +814,24 @@
         pg3[rows, 128:256] = hi
         pg3[rows, 256:384] = lo
 
-    @rloop("a2g", 3)
-    def _(n):
-        cols = pl.ds(pl.multiple_of(n * GROUP, GROUP), GROUP)
-
-        def block(b, carry):
+    def backward(i, carry):
+        total, product = carry
+        for b in (2 * i, 2 * i + 1):
             rows = pl.ds(pl.multiple_of(b * CHUNK, CHUNK), CHUNK)
             at = pl.ds(b * 48, 48)
-            r = mm(pg3[rows, 0:256], wp_b[b, :, cols]) + mm(pg3[rows, 256:384], wp_b[b, 0:128, cols])
-            r = (r.reshape(48, 8, GROUP) + spread[pl.ds(b, 1), cols]) * q2[at, :, cols]
-            q2[at, :, cols] = r
-            return carry[0] + jnp.sum(r, axis=0), carry[1] + jnp.sum(r * dv[at, :, cols], axis=0)
-
-        zero = jnp.zeros((8, GROUP), F32)
-        total, product = lax.fori_loop(0, BLOCKS, block, (zero, zero))
-        for half in range(2):
-            lanes = slice(half * LANE, (half + 1) * LANE)
-            put_sums(total[:, lanes], product[:, lanes], n * 2 + half, 0, 8)
-
+            r = mm(pg3[rows, 0:256], wp_b[b]) + mm(pg3[rows, 256:384], wp_b[b, 0:128, :])
+            r = (r.reshape(48, 8, WIDE) + spread[pl.ds(b, 1), :]) * q2[at]
+            q2[at] = r
+            total, product = total + jnp.sum(r, axis=0), product + jnp.sum(r * dv[at], axis=0)
+        return total, product
+
+    zero = jnp.zeros((8, WIDE), F32)
+    total, product = lax.fori_loop(0, 3, backward, (zero, zero))
+    total, product = row_sum(total), row_sum(product)
+    for g in range(GROUPS):
+        lanes = slice(g * LANE, (g + 1) * LANE)
+        sums[g : g + 1, :] = total[:, lanes]
+        sums[8 + g : 9 + g, :] = product[:, lanes]
     sum4.start(sums[...])
 
     gp = jnp.zeros((128, WIDE), F32)
@@ -870,10 +875,6 @@
         def _():
             sum4.middle()
 
-        @pl.when(g == 4)
-        def _():
-            reduce_p.middle()
-
     def own_lanes(rows):
         first = rows[:, 0:LANE]
         rest = rows[:, LANE:GROUP]
@@ -903,9 +904,9 @@
             for j in range(W):
                 ii, jj = i + a - 2, j + k - 2
                 if 0 <= ii < H and 0 <= jj < W:
-                    v = cells[ii * W + jj]
+                    v = cells[ii * W + jj : ii * W + jj + 1, :]
                     plain = v if plain is None else plain + v
-        put_misc(AT_PLAIN + t, row_sum(plain))
+        put_misc(AT_PLAIN + t, plain)
     for first, source in ((0, tq), (AT_DD, td)):
         for a in range(5):
             for k, v in enumerate(five_taps([source[a * 9 + m : a * 9 + m + 1, :] for m in range(9)])):
@@ -928,11 +929,12 @@
     def _(g):
         @pl.when(g == 1)
         def _():
+            reduce_p.middle()
+            reduce_p.sent()
+
+        @pl.when(g == 4)
+        def _():
             reduce_p.last()
-
-        @pl.when(g == 4)
-        def _():
-            reduce_m.middle()
 
         cols = lanes_of(g)
 
@@ -961,7 +963,7 @@
             cols = pl.ds(pl.multiple_of(n * GROUP, GROUP), GROUP)
             m = mm(ft[...], act_hi[:, cols])
             m = m[0:128] + m[128:256] + mm(ft[0:128, :], act_lo[:, cols])
-            ge_panel[:, :, cols] = m.reshape(16, 8, GROUP)
+            gp_panel[:, :, cols] = m.reshape(16, 8, GROUP)
             product = row_sum(m * we[:, cols])
             for half in range(2):
                 lanes = slice(half * LANE, (half + 1) * LANE)
@@ -974,18 +976,18 @@
 
     reduce_e.start(1)
     sum5.start(sums[...])
+    reduce_m.middle()
 
     hi, lo = split(we[...] * s1)
     ws_b[0:128, :] = hi
     ws_b[128:256, :] = lo
 
-    @rloop("ig", BLOCKS)
-    def _(b):
-        rows = pl.ds(pl.multiple_of(b * CHUNK, CHUNK), CHUNK)
-        at = pl.ds(b * 48, 48)
+    @rloop("ig", 3)
+    def _(i):
+        rows = pl.ds(pl.multiple_of(i * 2 * CHUNK, 2 * CHUNK), 2 * CHUNK)
         r = mm_nt(act_hi[rows, :], ws_b[...])
         r = r[:, 0:128] + r[:, 128:256] + mm_nt(act_lo[rows, :], ws_b[0:128, :])
-        q_rows[at] += r.reshape(48, 8, LANE)
+        q_rows[pl.ds(i * 96, 96)] += r.reshape(96, 8, LANE)
 
     sum5.middle()
 
@@ -996,24 +998,19 @@
             at = pl.ds(pl.multiple_of(b * CHUNK + i * LANE, LANE), LANE)
             target[:, at] = stage[i * LANE : (i + 1) * LANE, :].T[0:D]
 
-    def store(source, target, sem, b):
-        at = pl.ds(pl.multiple_of(b * CHUNK, CHUNK), CHUNK)
-        return pltpu.make_async_copy(source.at[:, at], target.at[:, at], sem)
-
     @rloop("out", BLOCKS)
     def _(b):
         write(f_in, b, lambda at: f_rows[at] + (p_rows[at] * s3 + t3))
-        store(f_in, out, copy_sems.at[1 + b], b).start()
 
     reduce_e.middle()
     reduce_m.last()
     emit(OUT_PROJECT, reduce_p.finish())
+    reduce_e.last()
     got = sum5.finish()
     b1 = wide(got, 0, GROUPS)
     g1 = (wide(got, 8, GROUPS) - mean1 * b1) * inv1
     k3 = -s1 * inv1 * g1 * (1.0 / TOTAL)
     k2 = -s1 * b1 * (1.0 / TOTAL) - k3 * mean1
-    reduce_e.last()
     left = jnp.where(lax.broadcasted_iota(jnp.int32, (128, WIDE), 0) == D, k2, we[...] * k3)
     mix = pair_nt(pair(left), we_b[...], 128, 128)
     mix_hi, mix_lo = split(mix)
@@ -1025,7 +1022,6 @@
         r = mm(f3[rows, 0:256], mix_all) + mm(f3[rows, 256:384], mix_hi)
         q_rows[pl.ds(b * 48, 48)] += r.reshape(48, 8, LANE)
         write(q_in, b, lambda at: q_rows[at])
-        store(q_in, igrad, copy_sems.at[7 + b], b).start()
 
     emit_vector(0, g1)
     emit_vector(1, b1)
@@ -1037,11 +1033,10 @@
     total_e = reduce_e.finish()
     emit(0, own_wide(s1) * (total_e - f_mean * own_wide(b1) - own_wide(cov_we[...]) * own_wide(inv1 * g1)))
 
-    for b in range(BLOCKS):
-        store(f_in, out, copy_sems.at[1 + b], b).wait()
-        store(q_in, igrad, copy_sems.at[7 + b], b).wait()
     for s in range(3):
         close_section(s)
+    reduce_m.sent()
+    reduce_e.sent()
     for item in vectors + [reduce_g, reduce_p, reduce_m, reduce_e]:
         item.close()
 
@@ -1049,23 +1044,13 @@
 def finish_kernel(
     out_in, igrad_in, panel,
     out, igrad, expand, gain1, bias1, depth, gain2, bias2, reduce, b_reduce, excite, b_excite, project, gain3, bias3,
-    held, sems,
+    sems,
 ):
-    pieces = []
-    for i in range(6):
-        source, target = ((out_in, out), (igrad_in, igrad))[i // 3]
-        at = pl.ds((i % 3) * (ROWS // 3), ROWS // 3)
-        pieces.append((
-            pltpu.make_async_copy(source.at[:, at], held.at[i], sems.at[0, i]),
-            pltpu.make_async_copy(held.at[i], target.at[:, at], sems.at[1, i]),
-        ))
-    for arrive, _ in pieces:
-        arrive.start()
+    large = [pltpu.make_async_copy(out_in, out, sems.at[0]), pltpu.make_async_copy(igrad_in, igrad, sems.at[1])]
+    for copy in large:
+        copy.start()
     expand[...] = panel[0:LANE, :].T[0:OWN, 0:D]
     project[...] = panel[OUT_PROJECT : OUT_PROJECT + LANE, :].T[0:OWN, 0:D]
-    for arrive, leave in pieces:
-        arrive.wait()
-        leave.start()
     for a in range(5):
         depth[a] = panel[OUT_MISC + 5 * a : OUT_MISC + 5 * a + 5, 0:OWN]
     reduce[...] = panel[OUT_MISC + AT_R : OUT_MISC + AT_R + SQZ, 0:OWN]
@@ -1077,8 +1062,8 @@
         ref[...] = panel[OUT_VECS + i : OUT_VECS + i + 1, 0:OWN]
     gain3[...] = panel[OUT_SMALL : OUT_SMALL + 1, 0:D]
     bias3[...] = panel[OUT_SMALL + 1 : OUT_SMALL + 2, 0:D]
-    for _, leave in pieces:
-        leave.wait()
+    for copy in large:
+        copy.wait()
 
 
 def body(
@@ -1107,25 +1092,25 @@
     slots = [f32(16, 8, WIDE), f32(4, 8, GROUP), f32(8, 8, GROUP), f32(16, 8, GROUP)]
     out, igrad, panel = pl.pallas_call(
         kernel,
-        out_shape=(shape(D, ROWS), shape(D, ROWS), shape(RESULTS, GROUP)),
+        out_shape=(f32(D, ROWS), f32(D, ROWS), f32(RESULTS, GROUP)),
         in_specs=[anywhere, anywhere] + [vm] * 13 + [pl.BlockSpec(memory_space=pltpu.SMEM)],
-        out_specs=(anywhere, anywhere, vm),
+        out_specs=(vm,) * 3,
         scratch_shapes=[
-            f32(D, ROWS), f32(D, ROWS), dma((14,)), f32(CHUNK, LANE), f32(GROUP, LANE),
+            dma((2,)), f32(CHUNK, LANE), f32(GROUP, LANE),
             rows128, rows128, rows128, b16(ROWS, 384), b16(256, ROWS), b16(ROWS, 384), b16(512, ROWS), f32(3, 256, WIDE),
             big, big, big, big, half, half,
             f32(4, PANEL, GROUP), f32(128, WIDE), f32(128, WIDE), b16(128, WIDE), b16(128, WIDE),
             b16(256, WIDE), b16(256, WIDE), b16(BLOCKS, 256, WIDE), f32(48, WIDE), f32(48, WIDE), f32(12, 8, WIDE),
-            f32(48, WIDE), f32(48, WIDE), f32(45, 8, LANE), f32(CELLS, 8, WIDE), f32(128, WIDE), f32(54, 2, 8, LANE), f32(54, 2, 8, LANE),
+            f32(48, WIDE), f32(48, WIDE), f32(45, 8, LANE), f32(CELLS, 8, LANE), f32(CELLS, WIDE), f32(128, WIDE), f32(54, 2, 8, LANE), f32(54, 2, 8, LANE),
             f32(BLOCKS, 8, WIDE), f32(8, WIDE), f32(8, WIDE), f32(8, LANE), f32(16, LANE),
-            f32(16, 8, WIDE), f32(16, 8, WIDE), f32(16, 8, WIDE), f32(8, 16, LANE),
+            f32(16, 8, WIDE), f32(16, 8, WIDE), f32(8, 16, LANE),
             f32(2, 8, 16, LANE), f32(2, 16, 16, LANE), f32(3, 8, 8, LANE), f32(3, 16, 8, LANE),
             f32(8, 16, LANE), f32(16, 16, LANE), f32(8, 16, LANE),
         ]
         + slots * 3
         + [dma((3, 3)), dma((5, 4)), dma((6,)), dma((3, 8))],
         compiler_params=pltpu.CompilerParams(
-            collective_id=0, has_side_effects=True, vmem_limit_bytes=64 * 1024 * 1024 - 65536
+            collective_id=0, has_side_effects=True, vmem_limit_bytes=61 * 1024 * 1024 + 256 * 1024
         ),
     )(
         features.T, cotangent.T, w_expand.T, w_project, w_reduce.T, w_excite, w_depth,
@@ -1140,10 +1125,11 @@
     results = pl.pallas_call(
         finish_kernel,
         out_shape=(shape(D, ROWS), shape(D, ROWS)) + tuple(shape(*dims) for dims in small),
-        in_specs=[anywhere, anywhere, vm],
+        in_specs=[vm] * 3,
         out_specs=(anywhere, anywhere) + (vm,) * 13,
-        scratch_shapes=[f32(6, D, ROWS // 3), dma((2, 6))],
-    )(out, igrad, panel)
+        scratch_shapes=[dma((2,))],
+        compiler_params=pltpu.CompilerParams(vmem_limit_bytes=8 * 1024 * 1024),
+    )(*(pltpu.with_memory_space_constraint(v, pltpu.VMEM) for v in (out, igrad, panel)))
     (out, igrad, expand, gain1, bias1, depth, gain2, bias2, reduce, small_b, excite, b_x, project, gain3, bias3) = results
     return (
         out.T, igrad.T, expand.T, gain1[0], bias1[0], depth, gain2[0], bias2[0],

time: 101 us -> 93.1 us (0.922)
  Pallas kernels: 100 us -> 92.3 us
    pallas_call x1, Pallas kernels: 95.9 us -> 90.2 us  [body(): pl.pallas_call(kernel, out_shape=(f32(D, ROWS), f32(D, ROWS), f32(RESULTS...]
    pallas_call x1, Pallas kernels: 4.12 us -> 2.07 us  [body(): pl.pallas_call(finish_kernel, out_shape=(shape(D, ROWS), shape(D, ROWS))...]
where the time goes in v4:
time: 93.1 us; the launch traced here: 93 us
  Pallas kernels  92.3 us (99%)
    pallas_call x1, Pallas kernels, body(): pl.pallas_call(kernel, out_shape=(f32(D, ROWS), f32(D, ROWS), f32(RESULTS...  90.2 us
    pallas_call x1, Pallas kernels, body(): pl.pallas_call(finish_kernel, out_shape=(shape(D, ROWS), shape(D, ROWS))...  2.07 us

profile of v4, /device:TPU:1, one launch (start us, length us, event | category | flops | bytes accessed | tf_op | source)
XLA Modules:
  0.0 93.0 jit_solution(14734769070794342620)
XLA Ops:
  0.7 90.2 %shard_map.271 = (f32[112,2304]{1,0:T(8,128)S(1)}, f32[112,2304]{1,0:T(8,128)S(1)}, f32[400,256]{1,0:T(8,128)S(1)}) custom-call(f32[112,2304]{1,0:T(8,128)} %bitcast.24, f32[112,2304]{1,0:T(8,128)} %bitcast.25, f32[168,112]{1,0:T(8,128)} %bitcast.26, f32[168,112]{1,0:T(8,128)} %wp_in.1, f32[28,168]{1,0:T(8,128)} %bitcast.27, f32[28,168]{1,0:T(8,128)} %wx_in.1, ...), custom_call_target="tpu_custom_call" | custom-call | tf_op jit(solution)/shard_map/pallas_call | solution.py:1093
  90.9 2.1 %shard_map.272 = (f32[112,2304]{1,0:T(8,128)}, f32[112,2304]{1,0:T(8,128)}, f32[168,112]{1,0:T(8,128)}, f32[1,168]{1,0:T(1,128)}, f32[1,168]{1,0:T(1,128)}, /*in...) custom-call(f32[112,2304]{1,0:T(8,128)S(1)} %get-tuple-element.33.ou, ...), custom_call_target="tpu_custom_call" | custom-call | tf_op jit(solution)/shard_map/pallas_call | solution.py:1125

commit v5 on v4

--- a/solution.py
+++ b/solution.py
@@ -1,5 +1,6 @@
 import jax
 import jax.numpy as jnp
+import numpy as np
 from jax import lax
 from jax.experimental import pallas as pl
 from jax.experimental.pallas import tpu as pltpu
@@ -257,8 +258,8 @@
     return h, jnp.tanh(h)
 
 
-def slope_of(h, th):
-    return (0.5 + 0.5 * th) * (1.0 + (h - h * th))
+def twice_slope_of(h, th):
+    return (1.0 + th) * (1.0 + (h - h * th))
 
 
 def sigmoid(v):
@@ -290,54 +291,67 @@
     ]
 
 
-def five_taps(g):
-    return [
-        g[6] - g[7] - g[8],
-        (g[2] - g[5]) + (g[7] - g[8]),
-        (g[0] - g[1]) - (g[2] + g[3]) + (g[4] + g[5]) - (g[6] - g[7] - g[8]),
-        (g[1] - g[4]) + (g[5] - g[7]),
-        g[3] - g[4] - g[5],
-    ]
-
-
-def nine_inputs(x):
-    x02, x13 = x[0] + x[2], x[1] + x[3]
-    return [x02 + x13, x13, x02, x[2] + x[3], x[3], x[2], x[0] + x[1], x[1], x[0]]
-
-
-def nine_outputs(y):
-    y02, y13 = y[0] + y[2], y[1] + y[3]
-    return [y02 + y13, y02, y13, y[0] + y[1], y[0], y[1], y[2] + y[3], y[2], y[3]]
-
-
-def expand_rows(target, expand, cell):
-    for i in range(H):
-        for m, v in enumerate(expand([cell(i * W + j) for j in range(W)])):
-            target[i * 9 + m] = v
-
-
-def convolve(inputs, outputs, weights, cols):
-    for m in range(9):
-        x = [inputs[i * 9 + m] for i in range(H)]
-        w = [jnp.broadcast_to(weights[a * 9 + m : a * 9 + m + 1, cols], (8, LANE)) for a in range(5)]
-        acc = [None] * H
-        for i, ii, a in row_pairs():
-            term = x[ii] * w[a]
-            acc[i] = term if acc[i] is None else acc[i] + term
-        for i in range(H):
-            outputs[i * 9 + m] = acc[i]
-
-
-def four_cells(outputs, i):
-    m = [outputs[i * 9 + k] for k in range(9)]
-    a, b, c, d, e, f = m[0] + m[1], m[0] + m[2], m[3] + m[4], m[3] + m[5], m[6] + m[7], m[6] + m[8]
-    return [a + c, b + d, a + e, b + f]
+FIVE = (
+    (0, 0, 0, 0, 0, 0, 1, -1, -1),
+    (0, 0, 1, 0, 0, -1, 0, 1, -1),
+    (1, -1, -1, -1, 1, 1, -1, 1, 1),
+    (0, 1, 0, 0, -1, 1, 0, -1, 0),
+    (0, 0, 0, 1, -1, -1, 0, 0, 0),
+)
+IN_D, IN_CELLS, IN_R, IN_X, SUMS = 48, 96, 120, 152, 192
+
+
+def combination():
+    c = np.zeros((128, SUMS), np.float32)
+    for a in range(5):
+        for k in range(5):
+            t = 5 * a + k
+            for m in range(9):
+                c[t, 9 * a + m] = FIVE[k][m]
+                c[AT_DD + t, IN_D + 9 * a + m] = FIVE[k][m]
+            for i in range(H):
+                for j in range(W):
+                    ii, jj = i + a - 2, j + k - 2
+                    if 0 <= ii < H and 0 <= jj < W:
+                        c[AT_PLAIN + t, IN_CELLS + ii * W + jj] = 1.0
+    for i in range(SQZ):
+        c[AT_R + i, IN_R + i] = 1.0
+    for i in range(IN_THIRD):
+        c[AT_X + i, IN_X + i] = 1.0
+    return c
+
+
+def over_rows(x, weights, m, cols):
+    w = [jnp.broadcast_to(weights[a * 9 + m : a * 9 + m + 1, cols], (8, LANE)) for a in range(5)]
+    acc = [None] * H
+    for i, ii, a in row_pairs():
+        term = x[ii] * w[a]
+        acc[i] = term if acc[i] is None else acc[i] + term
+    return acc
+
+
+def plus(a, b):
+    return [u + v for u, v in zip(a, b)]
+
+
+def convolve(column, weights, cols, kept, put):
+    x13 = plus(column(1), column(3))
+    x02 = plus(column(0), column(2))
+    m1 = over_rows(x13, weights, 1, cols)
+    m2 = over_rows(x02, weights, 2, cols)
+    m0 = over_rows(plus(x02, x13), weights, 0, cols)
+    for i, v in enumerate(plus(m0, m1) + plus(m0, m2)):
+        kept[i] = v
+    for first, left, right in ((3, 2, 0), (6, 0, 2)):
+        both = over_rows(plus(column(left), column(left + 1)), weights, first, cols)
+        for k, j in ((0, left + 1), (1, left)):
+            own = over_rows(column(j), weights, first + 1 + k, cols)
+            for i in range(H):
+                put(i, right + k, kept[k * H + i] + (both[i] + own[i]))
 
 
 def correlate(target, left, right):
-    for m in range(9):
-        x = [right[i * 9 + m] for i in range(H)]
-        y = [left[i * 9 + m] for i in range(H)]
+    def add(m, y, x):
         acc = [None] * 5
         for i, ii, a in row_pairs():
             term = y[i] * x[ii]
@@ -345,19 +359,35 @@
         for a in range(5):
             target[a * 9 + m] += fold(acc[a])
 
-
-def row_sums(target, source, cols):
-    for t in range(45):
-        target[t : t + 1, cols] = row_sum(source[t])
+    y02, x13 = plus(left(0), left(2)), plus(right(1), right(3))
+    add(1, y02, x13)
+    y13, x02 = plus(left(1), left(3)), plus(right(0), right(2))
+    add(2, y13, x02)
+    add(0, plus(y02, y13), plus(x02, x13))
+    for first, j, k in ((3, 0, 2), (6, 2, 0)):
+        add(first, plus(left(j), left(j + 1)), plus(right(k), right(k + 1)))
+        add(first + 1, left(j), right(k + 1))
+        add(first + 2, left(j + 1), right(k))
+
+
+def column_of(ref, base, cols):
+    return lambda j: [ref[pl.ds(base + 2 * (i * W + j), 2), :, cols] for i in range(H)]
+
+
+def row_sums(target, first, source, cols):
+    for t in range(source.shape[0]):
+        target[first + t : first + t + 1, cols] = row_sum(source[t])
 
 
 def kernel(
-    f_hbm, q_hbm, we_in, wp_in, wr_in, wx_in, wd_in, ga1_in, bi1_in, ga2_in, bi2_in, bx_in, br_in, ga3_in, bi3_in, units,
+    f_hbm, q_hbm, we_hbm, wp_hbm, wr_hbm, wx_hbm, wd_hbm, ga1_hbm, bi1_hbm, ga2_hbm, bi2_hbm, bx_hbm, br_hbm, ga3_hbm, bi3_hbm,
+    combine_hbm, units,
     f_in, q_in, o_panel,
+    we_in, wp_in, wr_in, wx_in, wd_in, ga1_in, bi1_in, ga2_in, bi2_in, bx_in, br_in, ga3_in, bi3_in,
     copy_sems, stage, wide_stage,
     f_rows, q_rows, p_rows, f3, ft, pg3, qpt, qa,
     e_ref, a1, dv, q2, act_hi, act_lo,
-    gathered, we, wp, wr, wx, we_b, ws_b, wp_b, wd, wt, par, tq, td, acc45, acc24, cells, cov_we, nine_a, nine_b,
+    gathered, we, wp, wr, wx, we_b, ws_b, wp_b, wd, wt, par, parts, combine, acc45, acc24, cov_we, kept,
     pool, gates, spread, vec, sums, gp_panel, misc, g_panel,
     near, far, near2, far2,
     g_first, g_second, g_third,
@@ -366,8 +396,22 @@
     e_first, e_parts, e_second, e_third,
     w_sems, v_sems, g_sems, s_sems,
 ):
-    fetch_f = pltpu.make_async_copy(f_hbm, f_in, copy_sems.at[1])
-    fetch_f.start()
+    third = ROWS // 3
+    fetch_f = []
+    for i in range(3):
+        at = pl.ds(i * third, third)
+        fetch_f.append(pltpu.make_async_copy(f_hbm.at[:, at], f_in.at[:, at], copy_sems.at[16 + i]))
+        fetch_f[i].start()
+    small_copies = [
+        pltpu.make_async_copy(source, target, copy_sems.at[2 + i])
+        for i, (source, target) in enumerate((
+            (we_hbm, we_in), (wp_hbm, wp_in), (wr_hbm, wr_in), (wx_hbm, wx_in), (wd_hbm, wd_in),
+            (ga1_hbm, ga1_in), (bi1_hbm, bi1_in), (ga2_hbm, ga2_in), (bi2_hbm, bi2_in), (bx_hbm, bx_in),
+            (br_hbm, br_in), (ga3_hbm, ga3_in), (bi3_hbm, bi3_in), (combine_hbm, combine),
+        ))
+    ]
+    for copy in small_copies:
+        copy.start()
     fetch_q = pltpu.make_async_copy(q_hbm, q_in, copy_sems.at[0])
     fetch_q.start()
     x, y, c, z = place()
@@ -389,13 +433,15 @@
     early_late = [(0, 2 * GROUP), (2 * GROUP, WIDE)]
     reduce_e = Panel(column, plane, early_late, gp_panel, e_first, e_parts, e_second, e_third, s_sems.at[2])
 
-    fetch_f.wait()
-
-    ones = jnp.where(lax.broadcasted_iota(jnp.int32, (16, ROWS), 0) == 0, 1.0, 0.0)
-    hi, lo = split(jnp.concatenate([f_in[...], ones], axis=0))
-    ft[0:128, :] = hi
-    ft[128:256, :] = lo
-    gram = mm_nt(ft[...], ft[...])
+    ones = jnp.where(lax.broadcasted_iota(jnp.int32, (16, third), 0) == 0, 1.0, 0.0)
+    gram = None
+    for i in range(3):
+        fetch_f[i].wait()
+        at = slice(i * third, (i + 1) * third)
+        hi, lo = split(jnp.concatenate([f_in[:, at], ones], axis=0))
+        both = jnp.concatenate([hi, lo], axis=0)
+        part = mm_nt(both, both)
+        gram = part if gram is None else gram + part
     gram = gram[0:128, 0:128] + (gram[0:128, 128:256] + gram[128:256, 0:128]) + gram[128:256, 128:256]
     g_panel[...] = gram.reshape(8, 16, LANE)
     pl.semaphore_wait(barrier, 22)
@@ -454,6 +500,8 @@
             parts.append(gathered[k, lo : lo + rows, LANE:GROUP] + gathered[k + 1, lo : lo + rows, LANE:GROUP])
         return jnp.concatenate(parts, axis=1)
 
+    for copy in small_copies:
+        copy.wait()
     gathered[z] = jnp.zeros((PANEL, GROUP), F32)
     wide_stage[...] = jnp.zeros_like(wide_stage)
     wide_stage[0:OWN, 0:D] = we_in[...]
@@ -464,6 +512,11 @@
     for i, row in enumerate((ga1_in, bi1_in, ga2_in, bi2_in, bx_in)):
         gathered[z, AT_VECS + i : AT_VECS + i + 1, 0:OWN] = row[...]
     send_section(1)
+    wide_stage[0:OWN, 0:D] = wp_in[...]
+    gathered[z, AT_PROJECT : AT_PROJECT + D, :] = wide_stage[...].T[0:D]
+    gathered[z, AT_REDUCE : AT_REDUCE + SQZ, 0:OWN] = wr_in[...]
+    gathered[z, AT_EXCITE : AT_EXCITE + SQZ, 0:OWN] = wx_in[...]
+    send_section(2)
 
     tail = jnp.where(lax.broadcasted_iota(jnp.int32, (16, LANE), 0) == 0, 1.0, 0.0)
 
@@ -504,10 +557,12 @@
     rows_of(q_in, jnp.zeros((16, LANE), F32), q_rows)
     parts_of(q_rows, 0)
     sums[...] = jnp.zeros_like(sums)
+    parts[...] = jnp.zeros_like(parts)
     qa[...] = jnp.zeros_like(qa)
 
     forward_section(0)
     forward_section(1)
+    reduce_g.last()
     section(0)
     we[0:D, :] = assembled(0, D)
     we[D:128, :] = jnp.zeros((128 - D, WIDE), F32)
@@ -519,7 +574,7 @@
     def _(b):
         @pl.when(b == 3)
         def _():
-            reduce_g.last()
+            forward_section(2)
 
         rows = pl.ds(pl.multiple_of(b * CHUNK, CHUNK), CHUNK)
         for n in range(3):
@@ -536,13 +591,15 @@
         for m, v in enumerate(nine_weights(row[::-1])):
             wt[(4 - a) * 9 + m : (4 - a) * 9 + m + 1, :] = v
     gain1, bias1, gain2, bias2, bx = [taps[TAPS + i : TAPS + i + 1] for i in range(5)]
-    wide_stage[0:OWN, 0:D] = wp_in[...]
-    gathered[z, AT_PROJECT : AT_PROJECT + D, :] = wide_stage[...].T[0:D]
-    gathered[z, AT_REDUCE : AT_REDUCE + SQZ, 0:OWN] = wr_in[...]
-    gathered[z, AT_EXCITE : AT_EXCITE + SQZ, 0:OWN] = wx_in[...]
-
+
+    section(2)
+    wp[0:D, :] = assembled(AT_PROJECT, D)
+    wp[D:128, :] = jnp.zeros((128 - D, WIDE), F32)
+    hi, lo = split(assembled(AT_REDUCE, 32))
+    wr[...] = jnp.concatenate([hi, lo, hi, lo], axis=0)
+    hi, lo = split(assembled(AT_EXCITE, 32))
+    wx[...] = jnp.concatenate([hi, lo, hi, lo], axis=0)
     gram = reduce_g.finish() * (1.0 / TOTAL)
-    send_section(2)
     f_mean_row = gram[D : D + 1, :]
     f_mean = gram[:, D : D + 1]
     cov = gram - f_mean * f_mean_row
@@ -571,38 +628,31 @@
             total, square = carry
             base = b * 48
             scale, shift = par[0, :, cols], par[1, :, cols]
-
-            def activate(cell):
+            for cell in range(CELLS):
                 at = pl.ds(base + 2 * cell, 2)
                 h, th = half_gate(e_ref[at, :, cols], scale, shift)
-                act = h + h * th
-                a1[at, :, cols] = act
-                return act
-
-            expand_rows(nine_a, nine_inputs, activate)
-            convolve(nine_a, nine_b, wd, cols)
-            for i in range(H):
-                for j, v in enumerate(four_cells(nine_b, i)):
-                    dv[pl.ds(base + 2 * (i * W + j), 2), :, cols] = v
-                    total = total + fold(v)
-                    square = square + fold(v * v)
+                a1[at, :, cols] = h + h * th
+            tally = [total, square]
+
+            def put(i, j, v):
+                dv[pl.ds(base + 2 * (i * W + j), 2), :, cols] = v
+                tally[0] = tally[0] + fold(v)
+                tally[1] = tally[1] + fold(v * v)
+
+            convolve(column_of(a1, base, cols), wd, cols, kept, put)
+            total, square = tally
             return total, square
 
         zero = jnp.zeros((8, LANE), F32)
         total, square = lax.fori_loop(0, BLOCKS, block, (zero, zero))
-        put_sums(total, square, g, jnp.where(g < 3, 0, 3), 3)
-
-        @pl.when(g == 2)
+        put_sums(total, square, g, jnp.where(g < 4, 0, 4), jnp.where(g < 4, 4, 2))
+
+        @pl.when(g == 3)
         def _():
             sum2a.start(sums[0:8, :])
 
-        @pl.when(g == 4)
-        def _():
-            forward_section(2)
-
         @pl.when(g == 5)
         def _():
-            sum2a.middle()
             sum2b.start(sums[0:8, :])
 
     def wide(rows, first, count):
@@ -631,18 +681,12 @@
 
         @pl.loop(0, BLOCKS)
         def _(b):
-            def act(cell):
-                v = a1[pl.ds(b * 48 + 2 * cell, 2), :, cols]
-                acc24[cell] += fold(v)
-                return v
-
-            expand_rows(nine_a, nine_inputs, act)
-            expand_rows(nine_b, nine_outputs, lambda cell: dv[pl.ds(b * 48 + 2 * cell, 2), :, cols])
-            correlate(acc45, nine_b, nine_a)
-
-        row_sums(td, acc45, cols)
-        for cell in range(CELLS):
-            cells[cell : cell + 1, cols] = row_sum(acc24[cell])
+            for cell in range(CELLS):
+                acc24[cell] += fold(a1[pl.ds(b * 48 + 2 * cell, 2), :, cols])
+            correlate(acc45, column_of(dv, b * 48, cols), column_of(a1, b * 48, cols))
+
+        row_sums(parts, IN_D, acc45, cols)
+        row_sums(parts, IN_CELLS, acc24, cols)
 
     def one_activation(g):
         cols = lanes_of(g)
@@ -663,37 +707,32 @@
                 act_lo[rows, cols] = lo
             pool[b, :, cols] = pooled
 
-    @pl.loop(0, 12)
+    @pl.loop(0, 11)
     def _(step):
+        @pl.when(step == 1)
+        def _():
+            sum2a.middle()
+
         @pl.when(step == 3)
         def _():
             sum2b.middle()
 
         @pl.when(step == 5)
         def _():
-            second_norm(sum2a.finish(), 0, 3 * LANE)
+            second_norm(sum2a.finish(), 0, 4 * LANE)
 
         @pl.when(step == 9)
         def _():
-            second_norm(sum2b.finish(), 3 * LANE, WIDE)
-
-        early = (step < 5) | (step == 8)
-
-        @pl.when(early)
-        def _():
-            one_products(jnp.where(step == 8, 5, step))
-
-        @pl.when(jnp.logical_not(early))
-        def _():
-            one_activation(jnp.where(step < 8, step - 5, step - 6))
-
-    section(2)
-    wp[0:D, :] = assembled(AT_PROJECT, D)
-    wp[D:128, :] = jnp.zeros((128 - D, WIDE), F32)
-    hi, lo = split(assembled(AT_REDUCE, 32))
-    wr[...] = jnp.concatenate([hi, lo, hi, lo], axis=0)
-    hi, lo = split(assembled(AT_EXCITE, 32))
-    wx[...] = jnp.concatenate([hi, lo, hi, lo], axis=0)
+            second_norm(sum2b.finish(), 4 * LANE, WIDE)
+
+        @pl.when(step < 5)
+        def _():
+            one_products(step)
+
+        @pl.when(step >= 5)
+        def _():
+            one_activation(step - 5)
+
     seg = lax.broadcasted_iota(jnp.int32, (8, LANE), 0)
     blk = lax.broadcasted_iota(jnp.int32, (8, LANE), 1)
     u0, u1, u2 = units[z, 0], units[z, 1], units[z, 2]
@@ -772,8 +811,19 @@
             scale, shift = par[2, :, cols], par[3, :, cols]
             for cell in range(CELLS):
                 at = pl.ds(b * 48 + 2 * cell, 2)
-                q2[at, :, cols] = slope_of(dv[at, :, cols] * scale + shift, q2[at, :, cols])
-
+                q2[at, :, cols] = twice_slope_of(dv[at, :, cols] * scale + shift, q2[at, :, cols])
+
+    def one_slope(g):
+        cols = lanes_of(g)
+
+        @pl.loop(0, BLOCKS)
+        def _(b):
+            scale, shift = par[0, :, cols], par[1, :, cols]
+            for cell in range(CELLS):
+                at = pl.ds(b * 48 + 2 * cell, 2)
+                e_ref[at, :, cols] = twice_slope_of(*half_gate(e_ref[at, :, cols], scale, shift))
+
+    pl.loop(0, 2)(one_slope)
     got = sum3.finish() * (1.0 / TOTAL)
     vec[...] = jnp.zeros((8, LANE), F32)
     vec[0:1, 0:D] = ga3_in[...]
@@ -803,12 +853,12 @@
     reduced_grad = pair_nt(pair(excite_in), wx[0:64, :], 8, 32) * (sig_r * (1.0 + reduced * (1.0 - sig_r))) * live
     pooled_grad = mm(quad(reduced_grad), wr[...]) * per_count
     for b in range(BLOCKS):
-        spread[b : b + 1, :] = of_blocks(pooled_grad, b)
+        spread[b : b + 1, :] = 0.5 * of_blocks(pooled_grad, b)
 
     @rloop("pgs", BLOCKS)
     def _(b):
         at = pl.ds(b * 48, 48)
-        hi, lo = split((q_rows[at] * s3 + (p_rows[at] * pg_p + pg_0)).reshape(CHUNK, LANE))
+        hi, lo = split((q_rows[at] * (0.5 * s3) + (p_rows[at] * (0.5 * pg_p) + 0.5 * pg_0)).reshape(CHUNK, LANE))
         rows = pl.ds(pl.multiple_of(b * CHUNK, CHUNK), CHUNK)
         pg3[rows, 0:128] = hi
         pg3[rows, 128:256] = hi
@@ -847,12 +897,8 @@
         gp_panel[14, 1 + i - IN_THIRD : 2 + i - IN_THIRD, :] = g_excite[i : i + 1]
     reduce_p.start(0)
 
-    def put_misc(row, values):
-        for i in range(values.shape[0]):
-            misc[(row + i) // 8, (row + i) % 8 : (row + i) % 8 + 1, :] = values[i : i + 1]
-
-    put_misc(AT_R, exact(reduced_grad, pooled, (0, 0))[0:SQZ])
-    put_misc(AT_X, g_excite[0:IN_THIRD])
+    parts[IN_R : IN_R + 32, :] = exact(reduced_grad, pooled, (0, 0))
+    parts[IN_X : IN_X + 32, :] = g_excite
 
     @rloop("tq", GROUPS)
     def _(g):
@@ -861,15 +907,13 @@
 
         @pl.loop(0, BLOCKS)
         def _(b):
-            expand_rows(nine_a, nine_inputs, lambda cell: a1[pl.ds(b * 48 + 2 * cell, 2), :, cols])
-            expand_rows(nine_b, nine_outputs, lambda cell: q2[pl.ds(b * 48 + 2 * cell, 2), :, cols])
-            correlate(acc45, nine_b, nine_a)
-            scale, shift = par[0, :, cols], par[1, :, cols]
-            for cell in range(CELLS):
-                at = pl.ds(b * 48 + 2 * cell, 2)
-                e_ref[at, :, cols] = slope_of(*half_gate(e_ref[at, :, cols], scale, shift))
-
-        row_sums(tq, acc45, cols)
+            correlate(acc45, column_of(q2, b * 48, cols), column_of(a1, b * 48, cols))
+
+        @pl.when(g >= 2)
+        def _():
+            one_slope(g)
+
+        row_sums(parts, 0, acc45, cols)
 
         @pl.when(g == 2)
         def _():
@@ -897,20 +941,11 @@
     def emit_vector(i, row):
         emit(OUT_VECS + i, own_wide(row))
 
-    for t in range(TAPS):
-        a, k = t // 5, t % 5
-        plain = None
-        for i in range(H):
-            for j in range(W):
-                ii, jj = i + a - 2, j + k - 2
-                if 0 <= ii < H and 0 <= jj < W:
-                    v = cells[ii * W + jj : ii * W + jj + 1, :]
-                    plain = v if plain is None else plain + v
-        put_misc(AT_PLAIN + t, plain)
-    for first, source in ((0, tq), (AT_DD, td)):
-        for a in range(5):
-            for k, v in enumerate(five_taps([source[a * 9 + m : a * 9 + m + 1, :] for m in range(9)])):
-                put_misc(first + 5 * a + k, v)
+    one_products(5)
+
+    hi, lo = split(parts[...])
+    picks = combine[...].astype(BF16)
+    misc[...] = (mm(picks, hi) + mm(picks, lo)).reshape(16, 8, WIDE)
     reduce_m.start(0)
 
     got = sum4.finish()
@@ -919,9 +954,10 @@
     g2 = (wide(got, 8, GROUPS) - mean2 * b2) * inv2
     c3 = -s2 * inv2 * g2 * (1.0 / TOTAL)
     c2 = -s2 * b2 * (1.0 / TOTAL) - c3 * mean2
-    put(4, s2)
-    put(5, c2)
-    put(6, c3)
+    shift3 = -inv2 * g2 * (1.0 / TOTAL)
+    put(4, -b2 * (1.0 / TOTAL) - shift3 * mean2)
+    put(5, shift3)
+    wt[...] = wt[...] * (0.5 * s2)
     emit_vector(2, g2)
     emit_vector(3, b2)
 
@@ -932,30 +968,25 @@
             reduce_p.middle()
             reduce_p.sent()
 
-        @pl.when(g == 4)
-        def _():
-            reduce_p.last()
-
         cols = lanes_of(g)
 
         @pl.loop(0, BLOCKS)
         def _(b):
             base = b * 48
-            k1, k2, k3 = par[4, :, cols], par[5, :, cols], par[6, :, cols]
-
-            def grad(cell):
+            k2, k3 = par[4, :, cols], par[5, :, cols]
+
+            for cell in range(CELLS):
                 at = pl.ds(base + 2 * cell, 2)
-                return q2[at, :, cols] * k1 + (dv[at, :, cols] * k3 + k2)
-
-            expand_rows(nine_a, nine_inputs, grad)
-            convolve(nine_a, nine_b, wt, cols)
-            for i in range(H):
-                for j, v in enumerate(four_cells(nine_b, i)):
-                    at = pl.ds(base + 2 * (i * W + j), 2)
-                    hi, lo = split((v * e_ref[at, :, cols]).reshape(16, LANE))
-                    rows = pl.ds(b * CHUNK + 16 * (i * W + j), 16)
-                    act_hi[rows, cols] = hi
-                    act_lo[rows, cols] = lo
+                q2[at, :, cols] = q2[at, :, cols] + (dv[at, :, cols] * k3 + k2)
+
+            def put(i, j, v):
+                at = pl.ds(base + 2 * (i * W + j), 2)
+                hi, lo = split((v * e_ref[at, :, cols]).reshape(16, LANE))
+                rows = pl.ds(b * CHUNK + 16 * (i * W + j), 16)
+                act_hi[rows, cols] = hi
+                act_lo[rows, cols] = lo
+
+            convolve(column_of(q2, base, cols), wt, cols, kept, put)
 
         @pl.when(lax.rem(g, 2) == 1)
         def _():
@@ -964,6 +995,11 @@
             m = mm(ft[...], act_hi[:, cols])
             m = m[0:128] + m[128:256] + mm(ft[0:128, :], act_lo[:, cols])
             gp_panel[:, :, cols] = m.reshape(16, 8, GROUP)
+
+            @pl.when(g == 5)
+            def _():
+                reduce_e.start(1)
+
             product = row_sum(m * we[:, cols])
             for half in range(2):
                 lanes = slice(half * LANE, (half + 1) * LANE)
@@ -974,8 +1010,8 @@
             def _():
                 reduce_e.start(0)
 
-    reduce_e.start(1)
     sum5.start(sums[...])
+    reduce_p.last()
     reduce_m.middle()
 
     hi, lo = split(we[...] * s1)
@@ -998,13 +1034,13 @@
             at = pl.ds(pl.multiple_of(b * CHUNK + i * LANE, LANE), LANE)
             target[:, at] = stage[i * LANE : (i + 1) * LANE, :].T[0:D]
 
+    reduce_m.last()
+    reduce_e.middle()
+
     @rloop("out", BLOCKS)
     def _(b):
         write(f_in, b, lambda at: f_rows[at] + (p_rows[at] * s3 + t3))
 
-    reduce_e.middle()
-    reduce_m.last()
-    emit(OUT_PROJECT, reduce_p.finish())
     reduce_e.last()
     got = sum5.finish()
     b1 = wide(got, 0, GROUPS)
@@ -1025,20 +1061,21 @@
 
     emit_vector(0, g1)
     emit_vector(1, b1)
+    emit(OUT_PROJECT, reduce_p.finish())
     total_m = reduce_m.finish()
     emit(OUT_MISC, total_m)
     by = [own_wide(v) for v in (s2, c2, c3)]
     taps_grad = total_m[0:TAPS] * by[0] + total_m[AT_DD : AT_DD + TAPS] * by[2] + total_m[AT_PLAIN : AT_PLAIN + TAPS] * by[1]
     emit(OUT_MISC, taps_grad)
-    total_e = reduce_e.finish()
-    emit(0, own_wide(s1) * (total_e - f_mean * own_wide(b1) - own_wide(cov_we[...]) * own_wide(inv1 * g1)))
-
+    scale_own = own_wide(s1)
+    away = f_mean * own_wide(b1) + own_wide(cov_we[...]) * own_wide(inv1 * g1)
     for s in range(3):
         close_section(s)
     reduce_m.sent()
     reduce_e.sent()
     for item in vectors + [reduce_g, reduce_p, reduce_m, reduce_e]:
         item.close()
+    emit(0, scale_own * (reduce_e.finish() - away))
 
 
 def finish_kernel(
@@ -1093,15 +1130,17 @@
     out, igrad, panel = pl.pallas_call(
         kernel,
         out_shape=(f32(D, ROWS), f32(D, ROWS), f32(RESULTS, GROUP)),
-        in_specs=[anywhere, anywhere] + [vm] * 13 + [pl.BlockSpec(memory_space=pltpu.SMEM)],
+        in_specs=[anywhere] * 16 + [pl.BlockSpec(memory_space=pltpu.SMEM)],
         out_specs=(vm,) * 3,
         scratch_shapes=[
-            dma((2,)), f32(CHUNK, LANE), f32(GROUP, LANE),
+            f32(OWN, D), f32(OWN, D), f32(SQZ, OWN), f32(SQZ, OWN), f32(5, 5, OWN),
+            f32(1, OWN), f32(1, OWN), f32(1, OWN), f32(1, OWN), f32(1, OWN), f32(1, SQZ), f32(1, D), f32(1, D),
+            dma((19,)), f32(CHUNK, LANE), f32(GROUP, LANE),
             rows128, rows128, rows128, b16(ROWS, 384), b16(256, ROWS), b16(ROWS, 384), b16(512, ROWS), f32(3, 256, WIDE),
             big, big, big, big, half, half,
             f32(4, PANEL, GROUP), f32(128, WIDE), f32(128, WIDE), b16(128, WIDE), b16(128, WIDE),
             b16(256, WIDE), b16(256, WIDE), b16(BLOCKS, 256, WIDE), f32(48, WIDE), f32(48, WIDE), f32(12, 8, WIDE),
-            f32(48, WIDE), f32(48, WIDE), f32(45, 8, LANE), f32(CELLS, 8, LANE), f32(CELLS, WIDE), f32(128, WIDE), f32(54, 2, 8, LANE), f32(54, 2, 8, LANE),
+            f32(SUMS, WIDE), f32(128, SUMS), f32(45, 8, LANE), f32(CELLS, 8, LANE), f32(128, WIDE), f32(2 * H, 2, 8, LANE),
             f32(BLOCKS, 8, WIDE), f32(8, WIDE), f32(8, WIDE), f32(8, LANE), f32(16, LANE),
             f32(16, 8, WIDE), f32(16, 8, WIDE), f32(8, 16, LANE),
             f32(2, 8, 16, LANE), f32(2, 16, 16, LANE), f32(3, 8, 8, LANE), f32(3, 16, 8, LANE),
@@ -1115,7 +1154,7 @@
     )(
         features.T, cotangent.T, w_expand.T, w_project, w_reduce.T, w_excite, w_depth,
         row(gain_one), row(bias_one), row(gain_two), row(bias_two), row(b_excite), row(b_reduce), row(gain_three), row(bias_three),
-        seg_units,
+        jnp.asarray(combination()), seg_units,
     )
 
     small = [

time: 93.1 us -> 88.8 us (0.954)
  Pallas kernels: 92.3 us -> 88 us
    pallas_call x1, Pallas kernels: 90.2 us -> 85.9 us  [body(): pl.pallas_call(kernel, out_shape=(f32(D, ROWS), f32(D, ROWS), f32(RESULTS...]
where the time goes in v5:
time: 88.8 us; the launch traced here: 88.7 us
  Pallas kernels  88 us (99%)
    pallas_call x1, Pallas kernels, body(): pl.pallas_call(kernel, out_shape=(f32(D, ROWS), f32(D, ROWS), f32(RESULTS...  85.9 us
    pallas_call x1, Pallas kernels, body(): pl.pallas_call(finish_kernel, out_shape=(shape(D, ROWS), shape(D, ROWS))...  2.07 us

profile of v5, /device:TPU:1, one launch (start us, length us, event | category | flops | bytes accessed | tf_op | source)
XLA Modules:
  0.0 88.7 jit_solution(9652369268622312971)
XLA Ops:
  0.7 85.9 %shard_map.280 = (f32[112,2304]{1,0:T(8,128)S(1)}, f32[112,2304]{1,0:T(8,128)S(1)}, f32[400,256]{1,0:T(8,128)S(1)}) custom-call(f32[112,2304]{1,0:T(8,128)} %bitcast.24, f32[112,2304]{1,0:T(8,128)} %bitcast.25, f32[168,112]{1,0:T(8,128)} %bitcast.26, f32[168,112]{1,0:T(8,128)} %wp_hbm.1, f32[28,168]{1,0:T(8,128)} %bitcast.27, f32[28,168]{1,0:T(8,128)} %wx_hbm.1, ...), custom_call_target="tpu_custom_call" | custom-call | tf_op jit(solution)/shard_map/pallas_call | solution.py:1130
  86.6 2.1 %shard_map.281 = (f32[112,2304]{1,0:T(8,128)}, f32[112,2304]{1,0:T(8,128)}, f32[168,112]{1,0:T(8,128)}, f32[1,168]{1,0:T(1,128)}, f32[1,168]{1,0:T(1,128)}, /*in...) custom-call(f32[112,2304]{1,0:T(8,128)S(1)} %get-tuple-element.33.ou, ...), custom_call_target="tpu_custom_call" | custom-call | tf_op jit(solution)/shard_map/pallas_call | solution.py:1164

commit v6 on v5

--- a/solution.py
+++ b/solution.py
@@ -644,7 +644,7 @@
             return total, square
 
         zero = jnp.zeros((8, LANE), F32)
-        total, square = lax.fori_loop(0, BLOCKS, block, (zero, zero))
+        total, square = lax.fori_loop(0, BLOCKS // 2, lambda i, v: block(2 * i + 1, block(2 * i, v)), (zero, zero))
         put_sums(total, square, g, jnp.where(g < 4, 0, 4), jnp.where(g < 4, 4, 2))
 
         @pl.when(g == 3)
@@ -788,18 +788,14 @@
 
     parts_of(p_rows, 128)
 
-    @rloop("qa", 3)
-    def _(i):
-        for b in (2 * i, 2 * i + 1):
-            rows = pl.ds(pl.multiple_of(b * CHUNK, CHUNK), CHUNK)
-            inside = [jnp.where((b >= low) & (b < high), 1.0, 0.0) for low, high in ((0, u0), (u0, u0 + u1), (u0 + u1, 6))]
-            m = mm(qpt[:, rows], act_hi[rows, :])
-            m = m[0:256] + m[256:512] + mm(qpt[0:256, rows], act_lo[rows, :])
-            for k in range(3):
-                qa[k] += m * inside[k]
-
-        @pl.when(i == 1)
-        def _():
+    for b in range(BLOCKS):
+        rows = slice(b * CHUNK, (b + 1) * CHUNK)
+        inside = [jnp.where((b >= low) & (b < high), 1.0, 0.0) for low, high in ((0, u0), (u0, u0 + u1), (u0 + u1, 6))]
+        m = mm(qpt[:, rows], act_hi[rows, :])
+        m = m[0:256] + m[256:512] + mm(qpt[0:256, rows], act_lo[rows, :])
+        for k in range(3):
+            qa[k] += m * inside[k]
+        if b == 3:
             sum3.middle()
 
     @rloop("slope2", GROUPS)
@@ -823,7 +819,7 @@
                 at = pl.ds(b * 48 + 2 * cell, 2)
                 e_ref[at, :, cols] = twice_slope_of(*half_gate(e_ref[at, :, cols], scale, shift))
 
-    pl.loop(0, 2)(one_slope)
+    pl.loop(0, 3)(one_slope)
     got = sum3.finish() * (1.0 / TOTAL)
     vec[...] = jnp.zeros((8, LANE), F32)
     vec[0:1, 0:D] = ga3_in[...]
@@ -855,28 +851,22 @@
     for b in range(BLOCKS):
         spread[b : b + 1, :] = 0.5 * of_blocks(pooled_grad, b)
 
-    @rloop("pgs", BLOCKS)
-    def _(b):
+    for b in range(BLOCKS):
         at = pl.ds(b * 48, 48)
         hi, lo = split((q_rows[at] * (0.5 * s3) + (p_rows[at] * (0.5 * pg_p) + 0.5 * pg_0)).reshape(CHUNK, LANE))
-        rows = pl.ds(pl.multiple_of(b * CHUNK, CHUNK), CHUNK)
+        rows = pl.ds(b * CHUNK, CHUNK)
         pg3[rows, 0:128] = hi
         pg3[rows, 128:256] = hi
         pg3[rows, 256:384] = lo
 
-    def backward(i, carry):
-        total, product = carry
-        for b in (2 * i, 2 * i + 1):
-            rows = pl.ds(pl.multiple_of(b * CHUNK, CHUNK), CHUNK)
-            at = pl.ds(b * 48, 48)
-            r = mm(pg3[rows, 0:256], wp_b[b]) + mm(pg3[rows, 256:384], wp_b[b, 0:128, :])
-            r = (r.reshape(48, 8, WIDE) + spread[pl.ds(b, 1), :]) * q2[at]
-            q2[at] = r
-            total, product = total + jnp.sum(r, axis=0), product + jnp.sum(r * dv[at], axis=0)
-        return total, product
-
-    zero = jnp.zeros((8, WIDE), F32)
-    total, product = lax.fori_loop(0, 3, backward, (zero, zero))
+    total = product = jnp.zeros((8, WIDE), F32)
+    for b in range(BLOCKS):
+        rows = slice(b * CHUNK, (b + 1) * CHUNK)
+        at = slice(b * 48, (b + 1) * 48)
+        r = mm(pg3[rows, 0:256], wp_b[b]) + mm(pg3[rows, 256:384], wp_b[b, 0:128, :])
+        r = (r.reshape(48, 8, WIDE) + spread[b : b + 1, :]) * q2[at]
+        q2[at] = r
+        total, product = total + jnp.sum(r, axis=0), product + jnp.sum(r * dv[at], axis=0)
     total, product = row_sum(total), row_sum(product)
     for g in range(GROUPS):
         lanes = slice(g * LANE, (g + 1) * LANE)
@@ -909,7 +899,7 @@
         def _(b):
             correlate(acc45, column_of(q2, b * 48, cols), column_of(a1, b * 48, cols))
 
-        @pl.when(g >= 2)
+        @pl.when(g >= 3)
         def _():
             one_slope(g)
 
@@ -965,13 +955,11 @@
     def _(g):
         @pl.when(g == 1)
         def _():
-            reduce_p.middle()
             reduce_p.sent()
 
         cols = lanes_of(g)
 
-        @pl.loop(0, BLOCKS)
-        def _(b):
+        def block(b):
             base = b * 48
             k2, k3 = par[4, :, cols], par[5, :, cols]
 
@@ -987,6 +975,11 @@
                 act_lo[rows, cols] = lo
 
             convolve(column_of(q2, base, cols), wt, cols, kept, put)
+
+        @pl.loop(0, BLOCKS // 2)
+        def _(i):
+            block(2 * i)
+            block(2 * i + 1)
 
         @pl.when(lax.rem(g, 2) == 1)
         def _():
@@ -1011,7 +1004,7 @@
                 reduce_e.start(0)
 
     sum5.start(sums[...])
-    reduce_p.last()
+    reduce_p.middle()
     reduce_m.middle()
 
     hi, lo = split(we[...] * s1)
@@ -1034,8 +1027,9 @@
             at = pl.ds(pl.multiple_of(b * CHUNK + i * LANE, LANE), LANE)
             target[:, at] = stage[i * LANE : (i + 1) * LANE, :].T[0:D]
 
+    reduce_e.middle()
+    reduce_p.last()
     reduce_m.last()
-    reduce_e.middle()
 
     @rloop("out", BLOCKS)
     def _(b):

time: 88.8 us -> 87.6 us (0.986)
  Pallas kernels: 88 us -> 86.7 us
    pallas_call x1, Pallas kernels: 85.9 us -> 84.6 us  [body(): pl.pallas_call(kernel, out_shape=(f32(D, ROWS), f32(D, ROWS), f32(RESULTS...]
where the time goes in v6:
time: 87.6 us; the launch traced here: 87.5 us
  Pallas kernels  86.7 us (99%)
    pallas_call x1, Pallas kernels, body(): pl.pallas_call(kernel, out_shape=(f32(D, ROWS), f32(D, ROWS), f32(RESULTS...  84.6 us
    pallas_call x1, Pallas kernels, body(): pl.pallas_call(finish_kernel, out_shape=(shape(D, ROWS), shape(D, ROWS))...  2.07 us

profile of v6, /device:TPU:1, one launch (start us, length us, event | category | flops | bytes accessed | tf_op | source)
XLA Modules:
  0.0 87.5 jit_solution(9793184633349083597)
XLA Ops:
  0.7 84.6 %shard_map.280 = (f32[112,2304]{1,0:T(8,128)S(1)}, f32[112,2304]{1,0:T(8,128)S(1)}, f32[400,256]{1,0:T(8,128)S(1)}) custom-call(f32[112,2304]{1,0:T(8,128)} %bitcast.24, f32[112,2304]{1,0:T(8,128)} %bitcast.25, f32[168,112]{1,0:T(8,128)} %bitcast.26, f32[168,112]{1,0:T(8,128)} %wp_hbm.1, f32[28,168]{1,0:T(8,128)} %bitcast.27, f32[28,168]{1,0:T(8,128)} %wx_hbm.1, ...), custom_call_target="tpu_custom_call" | custom-call | tf_op jit(solution)/shard_map/pallas_call | solution.py:1124
  85.2 2.1 %shard_map.281 = (f32[112,2304]{1,0:T(8,128)}, f32[112,2304]{1,0:T(8,128)}, f32[168,112]{1,0:T(8,128)}, f32[1,168]{1,0:T(1,128)}, f32[1,168]{1,0:T(1,128)}, /*in...) custom-call(f32[112,2304]{1,0:T(8,128)S(1)} %get-tuple-element.33.ou, ...), custom_call_target="tpu_custom_call" | custom-call | tf_op jit(solution)/shard_map/pallas_call | solution.py:1158

commit v7 on v6

--- a/solution.py
+++ b/solution.py
@@ -691,8 +691,7 @@
     def one_activation(g):
         cols = lanes_of(g)
 
-        @pl.loop(0, BLOCKS)
-        def _(b):
+        def block(b):
             scale, shift = par[2, :, cols], par[3, :, cols]
             pooled = jnp.zeros((8, LANE), F32)
             for cell in range(CELLS):
@@ -706,6 +705,11 @@
                 act_hi[rows, cols] = hi
                 act_lo[rows, cols] = lo
             pool[b, :, cols] = pooled
+
+        @pl.loop(0, BLOCKS // 2)
+        def _(i):
+            block(2 * i)
+            block(2 * i + 1)
 
     @pl.loop(0, 11)
     def _(step):
@@ -1018,8 +1022,6 @@
         r = r[:, 0:128] + r[:, 128:256] + mm_nt(act_lo[rows, :], ws_b[0:128, :])
         q_rows[pl.ds(i * 96, 96)] += r.reshape(96, 8, LANE)
 
-    sum5.middle()
-
     def write(target, b, rows_of_cell):
         for cell in range(CELLS):
             stage[pl.ds(cell, BLOCK, stride=CELLS), :] = rows_of_cell(pl.ds(b * 48 + 2 * cell, 2)).reshape(16, LANE)
@@ -1028,6 +1030,7 @@
             target[:, at] = stage[i * LANE : (i + 1) * LANE, :].T[0:D]
 
     reduce_e.middle()
+    sum5.middle()
     reduce_p.last()
     reduce_m.last()
 

time: 87.6 us -> 87.5 us (level)
  no operation moved by 1% of the time
where the time goes in v7:
time: 87.5 us; the launch traced here: 87.4 us
  Pallas kernels  86.6 us (99%)
    pallas_call x1, Pallas kernels, body(): pl.pallas_call(kernel, out_shape=(f32(D, ROWS), f32(D, ROWS), f32(RESULTS...  84.5 us
    pallas_call x1, Pallas kernels, body(): pl.pallas_call(finish_kernel, out_shape=(shape(D, ROWS), shape(D, ROWS))...  2.07 us

profile of v7, /device:TPU:1, one launch (start us, length us, event | category | flops | bytes accessed | tf_op | source)
XLA Modules:
  0.0 87.4 jit_solution(107165617185164724)
XLA Ops:
  0.7 84.5 %shard_map.280 = (f32[112,2304]{1,0:T(8,128)S(1)}, f32[112,2304]{1,0:T(8,128)S(1)}, f32[400,256]{1,0:T(8,128)S(1)}) custom-call(f32[112,2304]{1,0:T(8,128)} %bitcast.24, f32[112,2304]{1,0:T(8,128)} %bitcast.25, f32[168,112]{1,0:T(8,128)} %bitcast.26, f32[168,112]{1,0:T(8,128)} %wp_hbm.1, f32[28,168]{1,0:T(8,128)} %bitcast.27, f32[28,168]{1,0:T(8,128)} %wx_hbm.1, ...), custom_call_target="tpu_custom_call" | custom-call | tf_op jit(solution)/shard_map/pallas_call | solution.py:1127
  85.2 2.1 %shard_map.281 = (f32[112,2304]{1,0:T(8,128)}, f32[112,2304]{1,0:T(8,128)}, f32[168,112]{1,0:T(8,128)}, f32[1,168]{1,0:T(1,128)}, f32[1,168]{1,0:T(1,128)}, /*in...) custom-call(f32[112,2304]{1,0:T(8,128)S(1)} %get-tuple-element.33.ou, ...), custom_call_target="tpu_custom_call" | custom-call | tf_op jit(solution)/shard_map/pallas_call | solution.py:1161
